TPU v7x, 128 devices: a whole 4x4x4 slice. The times are simulated.
128 devices in a mesh: kpt: 16 (over z, y_hi, core), row: 8 (over x, y_lo).
Axes of the slice: x: 4, y: 4 (y_hi: 2, y_lo: 2; y = y_hi * 2 + y_lo), z: 4, core: 2. Of those that a mesh axis runs over, the one named last changes fastest.
Arguments:
- occ_orbitals: bfloat16 [64, 2048, 128], P('kpt', 'row'), may hold values from -0.5 to 0.5
- virt_orbitals: bfloat16 [64, 2048, 256], P('kpt', 'row'), may hold values from -0.375 to 0.375
- occ_gap: bfloat16 [64, 128], P('kpt'), may hold values from 0.049804688 to 3
- virt_gap: bfloat16 [64, 256], P('kpt'), may hold values from 0.049804688 to 3
- partner: int32 [3, 64], replicated, may hold values from 0 to 63, as said below
Outputs:
- chi: float32 [3, 4, 2048, 2048], P(None, None, 'row', 'kpt')
Inputs may be any that keep to these rules, and one draw needn't show every extreme that they name: For each transfer q there is a shift s_q of 0 to 4 with partner[q, k] = (k - s_q) mod 64 for every k; the shifts of different transfers differ, and some transfer has s_q = 4.
All inputs are finite; a program needn't handle non-finite values.
Results may differ from a plain program's by a relative error of at most 0.0003.
Values may be sent and summed in bfloat16 or wider, within the bound.
No kernel may reach another device: no remote copies, remote signals or barrier semaphores. Data moves between devices by JAX's collectives and lax.ppermute only.
A program may use at most 320 MiB of HBM per device.

v0:
```python
import jax
import jax.numpy as jnp
from jax import lax
from jax.sharding import PartitionSpec as P

NTAU = 4


def shifted(block, axis, distance):
    devices = range(lax.axis_size(axis))
    route = [((i - distance) % len(devices), i) for i in devices]
    return lax.ppermute(block, axis, route)


def weighted(orbitals, energy_gap, moment):
    factor = jnp.exp(-energy_gap.astype(jnp.float32) * moment)
    return (orbitals.astype(jnp.float32) * factor[:, None, :]).astype(jnp.bfloat16)


def greens(row_panel, column_panel):
    return jnp.einsum("kri,kci->krc", row_panel, column_panel, preferred_element_type=jnp.float32)


def on_device(occ_orbitals, virt_orbitals, occ_gap, virt_gap, partner):
    local_count = occ_orbitals.shape[0]
    transfers = partner.shape[0]
    device_k = lax.axis_index("kpt")
    kpt_count = lax.axis_size("kpt")
    total_count = local_count * kpt_count
    tau_values = 0.25 * 2.0 ** jnp.arange(NTAU, dtype=jnp.float32)
    earlier, earlier_gap = shifted((virt_orbitals, virt_gap), "kpt", 1)
    window = jnp.concatenate([earlier, virt_orbitals], axis=0)
    window_gap = jnp.concatenate([earlier_gap, virt_gap], axis=0)
    occ_points, window_points = (
        lax.all_gather(occ_orbitals, "row", axis=1, tiled=True),
        lax.all_gather(window, "row", axis=1, tiled=True),
    )
    window_start = (device_k - 1) % kpt_count * local_count
    own_partners = lax.dynamic_slice_in_dim(partner, device_k * local_count, local_count, 1)
    window_slots = (own_partners - window_start) % total_count
    blocks = []
    for step_index in range(NTAU):
        moment = tau_values[step_index]
        occ_green = greens(weighted(occ_orbitals, occ_gap, moment), occ_points)
        window_green = greens(weighted(window, window_gap, moment), window_points)
        sums_here = []
        for transfer in range(transfers):
            virt_green = jnp.take(window_green, window_slots[transfer], axis=0)
            sums_here.append(jnp.sum(occ_green * virt_green, axis=0))
        blocks.append(jnp.stack(sums_here))
    partial_chi = jnp.stack(blocks, axis=1)
    return lax.psum_scatter(partial_chi, "kpt", scatter_dimension=3, tiled=True)


def solution(mesh):
    in_specs = (P("kpt", "row", None), P("kpt", "row", None), P("kpt", None), P("kpt", None), P())
    out_specs = P(None, None, "row", "kpt")
    return jax.shard_map(
        on_device, mesh=mesh, in_specs=in_specs, out_specs=out_specs, check_vma=False
    )
```

profile of v0, /device:TPU:1, one launch (start us, length us, event | category | flops | bytes accessed | tf_op | source)
XLA Modules:
  0.0 672.6 jit_solution(10902497259233163905)
XLA Ops:
  6.5 0.7 all-gather.3.cloned.1.call-update
  7.3 0.0 all-gather.5.cloned.1.call-start
  7.3 4.4 collective-permute-start
  11.7 6.4 collective-permute-done
  18.2 1.1 constant_dynamic-update-slice_fusion
  19.3 1.0 copy-done
  20.2 0.0 all-gather.5.cloned.1.call-update
  20.2 0.0 reduce-scatter.2.cloned.1.call-start
  20.3 3.9 collective-permute-start.1
  24.2 0.8 add_select_fusion
  25.0 0.6 fusion.45
  25.7 3.1 multiply_exponential_fusion.5
  28.7 3.1 multiply_exponential_fusion.1
  31.8 30.4 %all-gather.3.cloned.1.call-done = bf16[4,2048,128]{2,1,0:T(8,128)(2,1)} async-done(((bf16[4,256,128]{2,1,0:T(8,128)(2,1)}), bf16[4,2048,128]{2,1,0:T(8,128)(2,1)}) %all-gather.3.cloned.1.call-update) | async-done | bytes 2097168 | tf_op jit(solution)/shard_map/all_gather | solution.py:35
  62.2 6.3 fusion.34
  68.5 4.5 fusion.36
  72.9 4.5 fusion.32
  77.4 4.5 fusion.38
  81.8 152.2 %all-gather.5.cloned.1.call-done = bf16[8,2048,256]{2,1,0:T(8,128)(2,1)} async-done(((bf16[8,256,256]{2,1,0:T(8,128)(2,1)}), bf16[8,2048,256]{2,1,0:T(8,128)(2,1)}) %all-gather.5.cloned.1.call-update) | async-done | bytes 8388624 | tf_op jit(solution)/shard_map/all_gather | solution.py:36
  234.1 11.5 %fusion.16 = f32[8,256,2048]{2,1,0:T(8,128)} fusion(bf16[8,2048,256]{2,1,0:T(8,128)(2,1)} %all-gather.5.cloned.1.call-done, bf16[8,256,256]{2,1,0:T(8,128)(2,1)S(1)} %copy-done.1, f32[8,256]{1,0:T(8,128)S(1)} %get-tuple-element.34), kind=kOutput, calls=%fused_computation.49 | convolution fusion | flops 2149056512 | bytes 26222592 | tf_op jit(solution)/shard_map/kri,kci->krc/dot_general | solution.py:21
  245.6 10.0 %gather_fusion.11 = f32[4,256,2048]{2,1,0:T(8,128)} fusion(f32[8,256,2048]{2,1,0:T(8,128)} %fusion.16, s32[1024]{0:T(1024)S(1)} %get-tuple-element.49), kind=kCustom, calls=%fused_computation.11.clone | custom fusion | bytes 16777232 | tf_op jit(solution)/shard_map/jit(_take)/gather | solution.py:48
  255.6 10.1 %gather_fusion.10 = f32[4,256,2048]{2,1,0:T(8,128)} fusion(f32[8,256,2048]{2,1,0:T(8,128)} %fusion.16, s32[1024]{0:T(1024)S(1)} %get-tuple-element.50), kind=kCustom, calls=%fused_computation.10.clone | custom fusion | bytes 16777232 | tf_op jit(solution)/shard_map/jit(_take)/gather | solution.py:48
  265.7 11.5 %fusion.18 = f32[8,256,2048]{2,1,0:T(8,128)} fusion(bf16[8,2048,256]{2,1,0:T(8,128)(2,1)} %all-gather.5.cloned.1.call-done, bf16[8,256,256]{2,1,0:T(8,128)(2,1)S(1)} %copy-done.1, f32[8,256]{1,0:T(8,128)S(1)} %get-tuple-element.33), kind=kOutput, calls=%fused_computation.50 | convolution fusion | flops 2149056512 | bytes 26222592 | tf_op jit(solution)/shard_map/kri,kci->krc/dot_general | solution.py:21
  277.2 10.1 %gather_fusion.8 = f32[4,256,2048]{2,1,0:T(8,128)} fusion(f32[8,256,2048]{2,1,0:T(8,128)} %fusion.18, s32[1024]{0:T(1024)S(1)} %get-tuple-element.49), kind=kCustom, calls=%fused_computation.8.clone | custom fusion | bytes 16777232 | tf_op jit(solution)/shard_map/jit(_take)/gather | solution.py:48
  287.4 10.3 %gather_fusion.7 = f32[4,256,2048]{2,1,0:T(8,128)} fusion(f32[8,256,2048]{2,1,0:T(8,128)} %fusion.18, s32[1024]{0:T(1024)S(1)} %get-tuple-element.50), kind=kCustom, calls=%fused_computation.7.clone | custom fusion | bytes 16777232 | tf_op jit(solution)/shard_map/jit(_take)/gather | solution.py:48
  297.7 10.0 %gather_fusion.9 = f32[4,256,2048]{2,1,0:T(8,128)} fusion(f32[8,256,2048]{2,1,0:T(8,128)} %fusion.16, s32[1024]{0:T(1024)S(1)} %pad_clamp_fusion.2), kind=kCustom, calls=%fused_computation.9.clone | custom fusion | bytes 16777232 | tf_op jit(solution)/shard_map/jit(_take)/gather | solution.py:48
  307.7 10.0 %gather_fusion.6 = f32[4,256,2048]{2,1,0:T(8,128)} fusion(f32[8,256,2048]{2,1,0:T(8,128)} %fusion.18, s32[1024]{0:T(1024)S(1)} %pad_clamp_fusion.2), kind=kCustom, calls=%fused_computation.6.clone | custom fusion | bytes 16777232 | tf_op jit(solution)/shard_map/jit(_take)/gather | solution.py:48
  317.8 11.5 %fusion.22 = f32[8,256,2048]{2,1,0:T(8,128)} fusion(bf16[8,2048,256]{2,1,0:T(8,128)(2,1)} %all-gather.5.cloned.1.call-done, bf16[8,256,256]{2,1,0:T(8,128)(2,1)S(1)} %copy-done.1, f32[8,256]{1,0:T(8,128)S(1)} %get-tuple-element.36), kind=kOutput, calls=%fused_computation.52 | convolution fusion | flops 2149056512 | bytes 26222592 | tf_op jit(solution)/shard_map/kri,kci->krc/dot_general | solution.py:21
  329.3 10.1 %gather_fusion.2 = f32[4,256,2048]{2,1,0:T(8,128)} fusion(f32[8,256,2048]{2,1,0:T(8,128)} %fusion.22, s32[1024]{0:T(1024)S(1)} %get-tuple-element.49), kind=kCustom, calls=%fused_computation.2.clone | custom fusion | bytes 16777232 | tf_op jit(solution)/shard_map/jit(_take)/gather | solution.py:48
  339.3 10.1 %gather_fusion.1 = f32[4,256,2048]{2,1,0:T(8,128)} fusion(f32[8,256,2048]{2,1,0:T(8,128)} %fusion.22, s32[1024]{0:T(1024)S(1)} %get-tuple-element.50), kind=kCustom, calls=%fused_computation.1.clone | custom fusion | bytes 16777232 | tf_op jit(solution)/shard_map/jit(_take)/gather | solution.py:48
  349.4 10.1 %gather_fusion = f32[4,256,2048]{2,1,0:T(8,128)} fusion(f32[8,256,2048]{2,1,0:T(8,128)} %fusion.22, s32[1024]{0:T(1024)S(1)} %pad_clamp_fusion.2), kind=kCustom, calls=%fused_computation.clone | custom fusion | bytes 16777232 | tf_op jit(solution)/shard_map/jit(_take)/gather | solution.py:48
  359.5 11.5 %fusion.20 = f32[8,256,2048]{2,1,0:T(8,128)} fusion(bf16[8,2048,256]{2,1,0:T(8,128)(2,1)} %all-gather.5.cloned.1.call-done, bf16[8,256,256]{2,1,0:T(8,128)(2,1)S(1)} %copy-done.1, f32[8,256]{1,0:T(8,128)S(1)} %get-tuple-element.35), kind=kOutput, calls=%fused_computation.51 | convolution fusion | flops 2149056512 | bytes 26222592 | tf_op jit(solution)/shard_map/kri,kci->krc/dot_general | solution.py:21
  371.0 10.1 %gather_fusion.5 = f32[4,256,2048]{2,1,0:T(8,128)} fusion(f32[8,256,2048]{2,1,0:T(8,128)} %fusion.20, s32[1024]{0:T(1024)S(1)} %get-tuple-element.49), kind=kCustom, calls=%fused_computation.5.clone | custom fusion | bytes 16777232 | tf_op jit(solution)/shard_map/jit(_take)/gather | solution.py:48
  381.1 10.1 %gather_fusion.3 = f32[4,256,2048]{2,1,0:T(8,128)} fusion(f32[8,256,2048]{2,1,0:T(8,128)} %fusion.20, s32[1024]{0:T(1024)S(1)} %pad_clamp_fusion.2), kind=kCustom, calls=%fused_computation.3.clone | custom fusion | bytes 16777232 | tf_op jit(solution)/shard_map/jit(_take)/gather | solution.py:48
  391.1 10.0 %gather_fusion.4 = f32[4,256,2048]{2,1,0:T(8,128)} fusion(f32[8,256,2048]{2,1,0:T(8,128)} %fusion.20, s32[1024]{0:T(1024)S(1)} %get-tuple-element.50), kind=kCustom, calls=%fused_computation.4.clone | custom fusion | bytes 16777232 | tf_op jit(solution)/shard_map/jit(_take)/gather | solution.py:48
  401.2 51.4 %fusion.2 = (f32[256,2048]{1,0:T(8,128)}, f32[256,2048]{1,0:T(8,128)}, f32[256,2048]{1,0:T(8,128)}, f32[256,2048]{1,0:T(8,128)}, f32[256,2048]{1,0:T(8,128)}, /*...) fusion(f32[4,256,2048]{2,1,0:T(8,128)} %fusion.32, ...), kind=kLoop, calls=%fused_computation.18 | loop fusion | flops 69206016 | bytes 159383568 | tf_op jit(solution)/shard_map/reduce_sum | solution.py:49
  452.6 3.4 maximum_bitcast_fusion.3
  456.1 0.6 copy-done.8
  456.7 0.6 copy-done.9
  457.3 0.8 maximum_bitcast_fusion
  458.1 0.0 copy-done.4
  458.1 0.6 copy-done.5
  458.7 0.6 copy-done.6
  459.3 0.8 maximum_bitcast_fusion.1
  460.1 2.1 maximum_bitcast_fusion.2
  462.3 8.5 %pad_maximum_fusion = f32[3,4,256,2048]{3,2,1,0:T(8,128)} fusion(f32[3,1,256,2048]{3,2,1,0:T(8,128)S(1)} %maximum_bitcast_fusion.3, f32[3,1,256,2048]{3,2,1,0:T(8,128)S(1)} %maximum_bitcast_fusion.2, f32[3,1,256,2048]{3,2,1,0:T(8,128)S(1)} %maximum_bitcast_fusion.1, f32[3,1,256,2048]{3,2,1,0:T(8,128)S(1)} %maximum_bitcast_fusion), kind=kLoop, calls=%fused_computation.12 | loop fusion | flops 18874368 | bytes 50331648 | tf_op jit(solution)/shard_map/stack | solution.py:51
  470.8 0.0 reduce-scatter.2.cloned.1.call-update
  470.8 195.3 %reduce-scatter.2.cloned.1.call-done = f32[3,4,256,128]{3,2,1,0:T(8,128)} async-done(((f32[3,4,256,2048]{3,2,1,0:T(8,128)}), f32[3,4,256,128]{3,2,1,0:T(8,128)}) %reduce-scatter.2.cloned.1.call-update) | async-done | bytes 1572880 | tf_op jit(solution)/shard_map/reduce_scatter | solution.py:52
  (23 shorter events, 0.1 us)
Async XLA Ops:
  6.5 61.9 %copy-start.10 = (bf16[4,256,128]{2,1,0:T(8,128)(2,1)S(1)}, bf16[4,256,128]{2,1,0:T(8,128)(2,1)}, u32[]{:S(2)}) copy-start(bf16[4,256,128]{2,1,0:T(8,128)(2,1)} %param.7) | copy-start | bytes 786436
  6.5 55.7 %all-gather.3.cloned.1.call-start = ((), (), s32[]{:S(2)}) async-start(), calls=%async_computation.1 | async-start | bytes 2359296 | tf_op jit(solution)/shard_map/all_gather | solution.py:35
  7.3 226.8 %all-gather.5.cloned.1.call-start = ((), (), s32[]{:S(2)}) async-start(), calls=%async_computation.2 | async-start | bytes 9437184 | tf_op jit(solution)/shard_map/all_gather | solution.py:36
  7.3 10.8 %collective-permute-start = (bf16[4,256,256]{2,1,0:T(8,128)(2,1)}, bf16[4,256,256]{2,1,0:T(8,128)(2,1)S(1)}, u32[]{:S(2)}, u32[]{:S(2)}) collective-permute-start(bf16[4,256,256]{2,1,0:T(8,128)(2,1)} %param.8), channel_id=1, source_target_pairs={{120,0},{0,8},{8,16},{16,24},{24,32},{32,40},{40,48},{48,56},{56,6... | collective-permute-start | bytes 1572872 | tf_op jit(solution)/shard_map/ppermute | solution.py:12
  19.2 1.0 copy-start
  20.2 645.8 %reduce-scatter.2.cloned.1.call-start = ((), (), s32[]{:S(2)}) async-start(), calls=%async_computation.3 | async-start | bytes 26738688 | tf_op jit(solution)/shard_map/reduce_scatter | solution.py:52
  20.3 8.4 %collective-permute-start.1 = (bf16[4,256]{1,0:T(4,128)(2,1)}, bf16[4,256]{1,0:T(4,128)(2,1)S(1)}, u32[]{:S(2)}, u32[]{:S(2)}) collective-permute-start(bf16[4,256]{1,0:T(4,128)(2,1)} %param.10), channel_id=1, source_target_pairs={{120,0},{0,8},{8,16},{16,24},{24,32},{32,40},{40,48},{48,56},{56,6... | collective-permute-start | bytes 6152 | tf_op jit(solution)/shard_map/ppermute | solution.py:12
  62.2 6.3 copy-start.2
  72.9 161.2 %copy-start.1 = (bf16[8,256,256]{2,1,0:T(8,128)(2,1)S(1)}, bf16[8,256,256]{2,1,0:T(8,128)(2,1)}, u32[]{:S(2)}) copy-start(bf16[8,256,256]{2,1,0:T(8,128)(2,1)} %copy-done) | copy-start | bytes 3145732
  452.6 3.5 copy-start.7
  452.6 4.1 copy-start.8
  452.6 4.7 copy-start.9
  456.0 2.1 copy-start.4
  456.0 2.7 copy-start.5
  456.0 3.3 copy-start.6
  458.1 2.0 copy-start.3
Sparse Core Ops, SparseCore 0:
  9.0 53.1 all-gather.2
  63.8 170.2 all-gather.4
  470.9 195.0 reduce-scatter.1
where the time goes:
time: 674 us; the launch traced here: 673 us
  waiting for transfers between devices  385 us (57%)
  local copies, waits for them, and re-layouts  126 us (19%)
  other arithmetic  74 us (11%)
  matrix products  65.6 us (10%)
  between operations  13.2 us (2%)
  starting transfers between devices  8.4 us (1%)
    reduce_scatter x1, waiting for transfers between devices, on_device(): return lax.psum_scatter(partial_chi, 'kpt', scatter_dimension=3, tiled=True)  195 us
    all_gather x1, waiting for transfers between devices, on_device(): lax.all_gather(window, 'row', axis=1, tiled=True)  152 us
    gather x12, local copies, waits for them, and re-layouts, on_device(): virt_green = jnp.take(window_green, window_slots[transfer], axis=0)  121 us
    dot_general x8, matrix products, greens(): jnp.einsum('kri,kci->krc', row_panel, column_panel, preferred_element_typ...  65.6 us
    reduce_sum x1, other arithmetic, on_device(): sums_here.append(jnp.sum(occ_green * virt_green, axis=0))  51.4 us
    all_gather x1, waiting for transfers between devices, on_device(): lax.all_gather(occ_orbitals, 'row', axis=1, tiled=True)  30.4 us
    another operation x5, other arithmetic, on_device(): partial_chi = jnp.stack(blocks, axis=1)  15.6 us
  transfers between devices with their start and end apart: 5, of which 4 were waited for; matrix products, arithmetic and copies ran while one was open for 4% of the time, Pallas kernels for 0%

commit v1 on v0

v1 whole, which is shorter than its diff:
```python
import jax
import jax.numpy as jnp
from jax import lax
from jax.experimental import pallas as pl
from jax.experimental.pallas import tpu as pltpu
from jax.sharding import Mesh, PartitionSpec as P

AXES = ("z", "yh", "c", "x", "yl")
NTAU = 4
NT_DIMS = (((1,), (1,)), ((), ()))


def routes(target):
    def linear(z, yh, c, x, yl):
        return (((z % 4) * 2 + yh) * 2 + c) * 8 + (x % 4) * 2 + yl

    return [
        (linear(z, yh, c, x, yl), linear(*target(z, yh, c, x, yl)))
        for z in range(4)
        for yh in range(2)
        for c in range(2)
        for x in range(4)
        for yl in range(2)
    ]


def send(block, target):
    return lax.ppermute(block, AXES, routes(target))


def kernel(shift, fac, row_blk, col_blk, out, vbuf, obuf, acc):
    step = pl.program_id(0)
    par = (step + 1) % 2

    @pl.when(step == 0)
    def _():
        acc[...] = jnp.zeros_like(acc)

    for i in range(4):
        col = col_blk[0, i].astype(jnp.float32)
        virt = jnp.concatenate(
            [(col[:, 128:] * fac[0, i, t : t + 1, 128:]).astype(jnp.bfloat16) for t in range(NTAU)], 0
        )
        vbuf[par * 4 + i] = lax.dot_general(
            virt, row_blk[0, i, :, 128:], NT_DIMS, preferred_element_type=jnp.float32
        )
        occ = jnp.concatenate(
            [(col[:, :128] * fac[0, i, t : t + 1, :128]).astype(jnp.bfloat16) for t in range(NTAU)], 0
        )
        obuf[i] = lax.dot_general(
            occ, row_blk[0, i, :, :128], NT_DIMS, preferred_element_type=jnp.float32
        )

    @pl.when(step > 0)
    def _():
        height = 16

        @pl.loop(0, 512 // height)
        def _(g):
            rows = pl.ds(pl.multiple_of(g * height, height), height)
            occs = [obuf[i, rows, :] for i in range(4)]
            for q in range(3):
                total = acc[q, rows, :]
                for i in range(4):
                    total = total + occs[i] * vbuf[(par * 4 + i - shift[q] + 8) % 8, rows, :]
                acc[q, rows, :] = total

    @pl.when(step == 16)
    def _():
        for q in range(3):
            for t in range(NTAU):
                out[q, t] = acc[q, t * 128 : (t + 1) * 128, :].T


def slab_of(step):
    return (step + 15) % 16


def held_at(step):
    j = slab_of(step)
    return (j // 4) * 4 + (j % 2) * 2 + (j // 2) % 2


def polarizability(shift, fac, row_pts, col_pts):
    spec = pltpu.PrefetchScalarGridSpec(
        num_scalar_prefetch=1,
        grid=(17,),
        in_specs=[
            pl.BlockSpec((1, 4, NTAU, 384), lambda s, _: (slab_of(s), 0, 0, 0)),
            pl.BlockSpec((1, 4, 256, 384), lambda s, _: (held_at(s), 0, 0, 0)),
            pl.BlockSpec((1, 4, 128, 384), lambda s, _: (held_at(s), 0, 0, 0)),
        ],
        out_specs=pl.BlockSpec((3, NTAU, 256, 128), lambda s, _: (0, 0, 0, 0)),
        scratch_shapes=[
            pltpu.VMEM((8, 512, 256), jnp.float32),
            pltpu.VMEM((4, 512, 256), jnp.float32),
            pltpu.VMEM((3, 512, 256), jnp.float32),
        ],
    )
    return pl.pallas_call(
        kernel,
        grid_spec=spec,
        out_shape=jax.ShapeDtypeStruct((3, NTAU, 256, 128), jnp.float32),
        compiler_params=pltpu.CompilerParams(vmem_limit_bytes=40 * 2**20),
    )(shift, fac, row_pts, col_pts)


def on_device(occ_orbitals, virt_orbitals, occ_gap, virt_gap, partner):
    z, yh, c, x, yl = (lax.axis_index(a) for a in AXES)
    shift = (-partner[:, 0]) % 64
    own = jnp.concatenate([occ_orbitals, virt_orbitals], axis=2)
    gaps = jnp.concatenate([occ_gap, virt_gap], axis=1)
    gaps = lax.all_gather(gaps, ("z", "yh", "c"), axis=0).astype(jnp.float32)
    tau = 0.25 * 2.0 ** jnp.arange(NTAU, dtype=jnp.float32)
    fac = jnp.exp(-gaps[:, :, None, :] * tau[:, None])

    other = send(own, lambda z, yh, c, x, yl: (z, 1 - yh, c, x, yl))
    same_t = send(own, lambda z, yh, c, x, yl: (x, yl, c, z, yh))
    cross_t = send(own, lambda z, yh, c, x, yl: (x, yl, c, z, 1 - yh))

    rows_piece = jnp.where(yh == 0, jnp.stack([own, other]), jnp.stack([other, own]))
    cols_piece = jnp.where(yl == 0, jnp.stack([same_t, cross_t]), jnp.stack([cross_t, same_t]))
    row_pts = jnp.zeros((4, 2, 2, 4, 256, 384), jnp.bfloat16)
    col_pts = jnp.zeros((4, 2, 2, 4, 128, 384), jnp.bfloat16)
    way = 2 * c - 1

    def swap(block):
        return send(block, lambda z, yh, c, x, yl: (z, yh, 1 - c, x, yl))

    for step in range(4):
        mine, theirs = way * step, -way * step
        got = swap(rows_piece)
        row_pts = lax.dynamic_update_slice(row_pts, rows_piece[None, None], ((z + mine) % 4, c, 0, 0, 0, 0))
        row_pts = lax.dynamic_update_slice(row_pts, got[None, None], ((z + theirs) % 4, 1 - c, 0, 0, 0, 0))
        keep = lax.dynamic_slice_in_dim(cols_piece, c * 128, 128, 2)
        give = lax.dynamic_slice_in_dim(cols_piece, (1 - c) * 128, 128, 2)
        got = swap(give)
        col_pts = lax.dynamic_update_slice(col_pts, keep[None, None], ((x + mine) % 4, c, 0, 0, 0, 0))
        col_pts = lax.dynamic_update_slice(col_pts, got[None, None], ((x + theirs) % 4, 1 - c, 0, 0, 0, 0))
        if step < 3:
            rows_piece = send(rows_piece, lambda z, yh, c, x, yl: (z + 1 - 2 * c, yh, c, x, yl))
            cols_piece = send(cols_piece, lambda z, yh, c, x, yl: (z, yh, c, x + 1 - 2 * c, yl))
    return polarizability(
        shift, fac, row_pts.reshape(16, 4, 256, 384), col_pts.reshape(16, 4, 128, 384)
    )


def solution(mesh):
    fine = Mesh(mesh.devices.reshape(4, 2, 2, 4, 2), AXES)
    kpt, row = ("z", "yh", "c"), ("x", "yl")
    in_specs = (P(kpt, row, None), P(kpt, row, None), P(kpt, None), P(kpt, None), P())
    return jax.shard_map(
        on_device, mesh=fine, in_specs=in_specs, out_specs=P(None, None, row, kpt), check_vma=False
    )
```

time: 674 us -> 261 us (0.39)
  waiting for transfers between devices: 385 us -> 112 us
  local copies, waits for them, and re-layouts: 126 us -> 30.4 us
  other arithmetic: 74 us -> 5.29 us
  matrix products: 65.6 us -> 0 us
  Pallas kernels: 0 us -> 47.4 us
  blocking collectives: 0 us -> 35.7 us
  starting transfers between devices: 8.4 us -> 29 us
  between operations: 13.2 us -> 0.49 us
    reduce_scatter x1 -> x0, waiting for transfers between devices: 195 us -> none  [on_device(): return lax.psum_scatter(partial_chi, 'kpt', scatter_dimension=3, tiled=True)]
    all_gather x2 -> x0, waiting for transfers between devices: 183 us -> none  [the longest x1 152 us: on_device(): lax.all_gather(window, 'row', axis=1, tiled=True)]
    gather x12 -> x0, local copies, waits for them, and re-layouts: 121 us -> none  [on_device(): virt_green = jnp.take(window_green, window_slots[transfer], axis=0)]
    ppermute x2 -> x17, waiting for transfers between devices: 6.44 us -> 112 us  [send(): return lax.ppermute(block, AXES, routes(target))]
    dot_general x8 -> x0, matrix products: 65.6 us -> none  [greens(): jnp.einsum('kri,kci->krc', row_panel, column_panel, preferred_element_typ...]
    reduce_sum x1 -> x0, other arithmetic: 51.4 us -> none  [on_device(): sums_here.append(jnp.sum(occ_green * virt_green, axis=0))]
    pallas_call x0 -> x1, Pallas kernels: none -> 47.4 us  [polarizability(): pl.pallas_call(kernel, grid_spec=spec, out_shape=jax.ShapeDtypeStruct((3,...]
    all_gather x0 -> x1, blocking collectives: none -> 35.7 us  [on_device(): gaps = lax.all_gather(gaps, ('z', 'yh', 'c'), axis=0).astype(jnp.float32)]
  transfers between devices with their start and end apart: 5 -> 17, of which waited for: 4 -> 5; matrix products, arithmetic and copies ran while one was open for 4% -> 12% of each run, Pallas kernels for 0% -> 0%
where the time goes in v1:
time: 261 us; the launch traced here: 260 us
  waiting for transfers between devices  112 us (43%)
  Pallas kernels  47.4 us (18%)
  blocking collectives  35.7 us (14%)
  local copies, waits for them, and re-layouts  30.4 us (12%)
  starting transfers between devices  29 us (11%)
  other arithmetic  5.29 us (2%)
    ppermute x17, waiting for transfers between devices, send(): return lax.ppermute(block, AXES, routes(target))  112 us
    pallas_call x1, Pallas kernels, polarizability(): pl.pallas_call(kernel, grid_spec=spec, out_shape=jax.ShapeDtypeStruct((3,...  47.4 us
    all_gather x1, blocking collectives, on_device(): gaps = lax.all_gather(gaps, ('z', 'yh', 'c'), axis=0).astype(jnp.float32)  35.7 us
    ppermute x17, starting transfers between devices, send(): return lax.ppermute(block, AXES, routes(target))  29 us
    dynamic_update_slice x4, local copies, waits for them, and re-layouts, on_device(): lax.dynamic_update_slice(row_pts, got[None, None], ((z + theirs) % 4, 1 -...  6.7 us
    broadcast_in_dim x1, local copies, waits for them, and re-layouts, on_device(): row_pts = jnp.zeros((4, 2, 2, 4, 256, 384), jnp.bfloat16)  6.55 us
    dynamic_update_slice x3, local copies, waits for them, and re-layouts, on_device(): lax.dynamic_update_slice(row_pts, rows_piece[None, None], ((z + mine) % 4...  5.51 us
  transfers between devices with their start and end apart: 17, of which 5 were waited for; matrix products, arithmetic and copies ran while one was open for 12% of the time, Pallas kernels for 0%

profile of v1, /device:TPU:1, one launch (start us, length us, event | category | flops | bytes accessed | tf_op | source)
XLA Modules:
  0.0 260.3 jit_solution(8524996495018222622)
XLA Ops:
  0.0 1.0 constant_dynamic-update-slice_fusion.1
  1.0 1.1 constant_dynamic-update-slice_fusion
  2.1 3.8 %collective-permute-start = (bf16[4,256,384]{2,1,0:T(8,128)(2,1)S(1)}, bf16[4,256,384]{2,1,0:T(8,128)(2,1)S(1)}, u32[]{:S(2)}, u32[]{:S(2)}) collective-permute-start(bf16[4,256,384]{2,1,0:T(8,128)(2,1)S(1)} %constant_dynamic-update-slice_fusion), channel_id=1, source_target_pairs={{0,16},{1,17},{2,18},{3,19},{4,20},{5,21},{6,22},{7,23},{8,24},{9,... | collective-permute-start | bytes 2359304 | tf_op jit(solution)/shard_map/ppermute | solution.py:28
  5.9 0.4 collective-permute-start.9
  6.3 0.7 collective-permute-start.8
  7.0 87.0 %collective-permute-done = bf16[4,256,384]{2,1,0:T(8,128)(2,1)S(1)} collective-permute-done((bf16[4,256,384]{2,1,0:T(8,128)(2,1)S(1)}, bf16[4,256,384]{2,1,0:T(8,128)(2,1)S(1)}, u32[]{:S(2)}, u32[]{:S(2)}) %collective-permute-start) | collective-permute-done | bytes 786464 | tf_op jit(solution)/shard_map/ppermute | solution.py:28
  94.0 1.4 maximum_select_fusion.1
  95.5 17.4 %collective-permute-done.9 = bf16[4,256,384]{2,1,0:T(8,128)(2,1)S(1)} collective-permute-done((bf16[4,256,384]{2,1,0:T(8,128)(2,1)S(1)}, bf16[4,256,384]{2,1,0:T(8,128)(2,1)S(1)}, u32[]{:S(2)}, u32[]{:S(2)}) %collective-permute-start.9) | collective-permute-done | bytes 786464 | tf_op jit(solution)/shard_map/ppermute | solution.py:28
  112.9 0.9 copy-done
  113.8 0.3 copy-done.1
  114.1 2.2 maximum_select_fusion.2
  116.7 11.3 %collective-permute-start.4 = (bf16[2,4,256,384]{3,2,1,0:T(8,128)(2,1)}, bf16[2,4,256,384]{3,2,1,0:T(8,128)(2,1)S(1)}, u32[]{:S(2)}, u32[]{:S(2)}) collective-permute-start(bf16[2,4,256,384]{3,2,1,0:T(8,128)(2,1)} %collective-permute-done.2), channel_id=1, source_target_pairs={{0,32},{1,33},{2,34},{3,35},{4,36},{5,37},{6,38},{7,39},{8,104},{9... | collective-permute-start | bytes 4718600 | tf_op jit(solution)/shard_map/ppermute | solution.py:28
  128.1 35.7 %all-gather.1 = bf16[16,4,384]{2,1,0:T(4,128)(2,1)S(1)} all-gather(bf16[1,4,384]{2,1,0:T(4,128)(2,1)S(1)} %maximum_bitcast_fusion), channel_id=2, replica_groups=mesh['z'=4,'yh'=2,'c'=2,'x'=4,'yl'=2] {'z','yh','c'}, dimensions={0}, use_global_device_ids=true | all-gather | bytes 52224 | tf_op jit(solution)/shard_map/all_gather | solution.py:113
  163.8 0.1 slice_reduce_fusion
  163.9 0.2 collective-permute-start.1
  164.2 0.1 constant_dynamic-slice_fusion.3
  164.3 3.3 %collective-permute-start.10 = (bf16[2,4,128,384]{3,2,1,0:T(8,128)(2,1)S(1)}, bf16[2,4,128,384]{3,2,1,0:T(8,128)(2,1)}, u32[]{:S(2)}, u32[]{:S(2)}) collective-permute-start(bf16[2,4,128,384]{3,2,1,0:T(8,128)(2,1)S(1)} %constant_dynamic-slice_fusion.3), channel_id=1, source_target_pairs={{0,8},{1,9},{2,10},{3,11},{4,12},{5,13},{6,14},{7,15},{8,0},{9,1},... | collective-permute-start | bytes 2359304 | tf_op jit(solution)/shard_map/ppermute | solution.py:28
  167.6 0.2 multiply_exponential_fusion.fac
  167.8 6.6 %broadcast_in_dim.53 = bf16[4,2,2,4,256,384]{5,4,3,2,1,0:T(8,128)(2,1)} broadcast(bf16[]{:T(256)} %constant.110.clone.1), dimensions={} | broadcast | bytes 12582914 | tf_op jit(solution)/shard_map/broadcast_in_dim | solution.py:123
  174.4 1.4 fusion
  175.9 1.0 broadcast_in_dim.61
  176.9 0.2 bitcast_dynamic-update-slice_fusion.14
  177.0 1.2 constant_dynamic-slice_fusion.2
  178.3 0.5 collective-permute-start.12
  178.8 1.3 bitcast_dynamic-update-slice_fusion.13
  180.1 5.1 %collective-permute-done.13 = bf16[2,4,256,384]{3,2,1,0:T(8,128)(2,1)} collective-permute-done((bf16[2,4,256,384]{3,2,1,0:T(8,128)(2,1)}, bf16[2,4,256,384]{3,2,1,0:T(8,128)(2,1)}, u32[]{:S(2)}, u32[]{:S(2)}) %collective-permute-start.13) | collective-permute-done | bytes 1572896 | tf_op jit(solution)/shard_map/ppermute | solution.py:28
  185.2 2.7 %bitcast_dynamic-update-slice_fusion.6 = bf16[4,2,2,4,256,384]{5,4,3,2,1,0:T(8,128)(2,1)} fusion(bf16[4,2,2,4,256,384]{5,4,3,2,1,0:T(8,128)(2,1)} %fusion, s32[]{:T(128)S(6)} %select_n.174, s32[]{:T(128)S(6)} %select_n.178, bf16[2,4,256,384]{3,2,1,0:T(8,128)(2,1)} %collective-permute-done.1), kind=kLoop, calls=%fused_computation.10 | loop fusion | bytes 3145736 | tf_op jit(solution)/shard_map/dynamic_update_slice | solution.py:134
  188.0 1.3 bitcast_dynamic-update-slice_fusion.12
  189.3 2.8 %bitcast_dynamic-update-slice_fusion.5 = bf16[4,2,2,4,256,384]{5,4,3,2,1,0:T(8,128)(2,1)} fusion(bf16[4,2,2,4,256,384]{5,4,3,2,1,0:T(8,128)(2,1)} %bitcast_dynamic-update-slice_fusion.6, s32[]{:T(128)S(6)} %select_n.180, s32[]{:T(128)S(6)} %select_n.175, bf16[2,4,256,384]{3,2,1,0:T(8,128)(2,1)} %collective-permute-done.2), kind=kLoop, calls=%fused_computation.9 | loop fusion | bytes 3145736 | tf_op jit(solution)/shard_map/dynamic_update_slice | solution.py:133
  192.0 2.8 %collective-permute-start.5 = (bf16[2,4,256,384]{3,2,1,0:T(8,128)(2,1)S(1)}, bf16[2,4,256,384]{3,2,1,0:T(8,128)(2,1)S(1)}, u32[]{:S(2)}, u32[]{:S(2)}) collective-permute-start(bf16[2,4,256,384]{3,2,1,0:T(8,128)(2,1)S(1)} %collective-permute-done.4), channel_id=1, source_target_pairs={{0,8},{1,9},{2,10},{3,11},{4,12},{5,13},{6,14},{7,15},{8,0},{9,1},... | collective-permute-start | bytes 4718600 | tf_op jit(solution)/shard_map/ppermute | solution.py:28
  194.9 0.1 bitcast_dynamic-update-slice_fusion.11
  195.0 1.2 constant_dynamic-slice_fusion.1
  196.2 0.1 collective-permute-start.14
  196.4 1.3 bitcast_dynamic-update-slice_fusion.4
  197.7 0.7 collective-permute-done.6
  198.4 2.2 collective-permute-start.7
  200.5 1.4 bitcast_dynamic-update-slice_fusion.3
  201.9 1.3 bitcast_dynamic-update-slice_fusion.10
  203.2 1.8 collective-permute-done.15
  205.0 0.1 constant_dynamic-slice_fusion
  205.1 3.4 %collective-permute-start.16 = (bf16[2,4,128,384]{3,2,1,0:T(8,128)(2,1)S(1)}, bf16[2,4,128,384]{3,2,1,0:T(8,128)(2,1)S(1)}, u32[]{:S(2)}, u32[]{:S(2)}) collective-permute-start(bf16[2,4,128,384]{3,2,1,0:T(8,128)(2,1)S(1)} %constant_dynamic-slice_fusion), channel_id=1, source_target_pairs={{0,8},{1,9},{2,10},{3,11},{4,12},{5,13},{6,14},{7,15},{8,0},{9,1},... | collective-permute-start | bytes 2359304 | tf_op jit(solution)/shard_map/ppermute | solution.py:28
  208.4 0.1 bitcast_dynamic-update-slice_fusion.9
  208.6 0.2 bitcast_dynamic-update-slice_fusion.8
  208.8 1.3 bitcast_dynamic-update-slice_fusion.2
  210.1 1.3 bitcast_dynamic-update-slice_fusion.1
  211.4 0.1 bitcast_dynamic-update-slice_fusion.7
  211.6 1.3 bitcast_dynamic-update-slice_fusion
  212.9 47.4 %shard_map.55 = f32[3,4,256,128]{3,2,1,0:T(8,128)} custom-call(s32[3]{0:T(128)S(1)} %and_select_fusion.shift, f32[16,4,4,384]{3,2,1,0:T(4,128)S(1)} %multiply_exponential_fusion.fac, bf16[16,4,256,384]{3,2,1,0:T(8,128)(2,1)} %bitcast.43, bf16[16,4,128,384]{3,2,1,0:T(8,128)(2,1)S(1)} %bitcast.42), custom_call_target="tpu_custom_call" | custom-call | tf_op jit(solution)/shard_map/pallas_call | solution.py:100
  (30 shorter events, 0.2 us)
Async XLA Ops:
  2.1 92.0 %collective-permute-start = (bf16[4,256,384]{2,1,0:T(8,128)(2,1)S(1)}, bf16[4,256,384]{2,1,0:T(8,128)(2,1)S(1)}, u32[]{:S(2)}, u32[]{:S(2)}) collective-permute-start(bf16[4,256,384]{2,1,0:T(8,128)(2,1)S(1)} %constant_dynamic-update-slice_fusion), channel_id=1, source_target_pairs={{0,16},{1,17},{2,18},{3,19},{4,20},{5,21},{6,22},{7,23},{8,24},{9,... | collective-permute-start | bytes 2359304 | tf_op jit(solution)/shard_map/ppermute | solution.py:28
  5.9 107.0 %collective-permute-start.9 = (bf16[4,256,384]{2,1,0:T(8,128)(2,1)S(1)}, bf16[4,256,384]{2,1,0:T(8,128)(2,1)S(1)}, u32[]{:S(2)}, u32[]{:S(2)}) collective-permute-start(bf16[4,256,384]{2,1,0:T(8,128)(2,1)S(1)} %constant_dynamic-update-slice_fusion), channel_id=1, source_target_pairs={{0,1},{1,17},{2,33},{3,49},{4,65},{5,81},{6,97},{7,113},{8,9},{9,2... | collective-permute-start | bytes 2359304 | tf_op jit(solution)/shard_map/ppermute | solution.py:28
  6.3 106.6 %collective-permute-start.8 = (bf16[4,256,384]{2,1,0:T(8,128)(2,1)S(1)}, bf16[4,256,384]{2,1,0:T(8,128)(2,1)S(1)}, u32[]{:S(2)}, u32[]{:S(2)}) collective-permute-start(bf16[4,256,384]{2,1,0:T(8,128)(2,1)S(1)} %constant_dynamic-update-slice_fusion), channel_id=1, source_target_pairs={{0,0},{1,16},{2,32},{3,48},{4,64},{5,80},{6,96},{7,112},{8,8},{9,2... | collective-permute-start | bytes 2359304 | tf_op jit(solution)/shard_map/ppermute | solution.py:28
  94.0 34.0 %copy-start.2 = (bf16[4,256]{1,0:T(4,128)(2,1)S(1)}, bf16[4,256]{1,0:T(4,128)(2,1)}, u32[]{:S(2)}) copy-start(bf16[4,256]{1,0:T(4,128)(2,1)} %param.8) | copy-start | bytes 6148
  94.0 34.0 %copy-start.4 = (bf16[4,128]{1,0:T(4,128)(2,1)S(1)}, bf16[4,128]{1,0:T(4,128)(2,1)}, u32[]{:S(2)}) copy-start(bf16[4,128]{1,0:T(4,128)(2,1)} %param.7) | copy-start | bytes 3076
  94.0 69.8 %copy-start.3 = (s32[3,64]{1,0:T(4,128)S(1)}, s32[3,64]{1,0:T(4,128)}, u32[]{:S(2)}) copy-start(s32[3,64]{1,0:T(4,128)} %param.9) | copy-start | bytes 2308
  95.5 21.2 %collective-permute-start.2 = (bf16[2,4,256,384]{3,2,1,0:T(8,128)(2,1)}, bf16[2,4,256,384]{3,2,1,0:T(8,128)(2,1)}, u32[]{:S(2)}, u32[]{:S(2)}) collective-permute-start(bf16[2,4,256,384]{3,2,1,0:T(8,128)(2,1)} %maximum_select_fusion.1), channel_id=1, source_target_pairs={{0,32},{1,33},{2,34},{3,35},{4,36},{5,37},{6,38},{7,39},{8,104},{9... | collective-permute-start | bytes 4718600 | tf_op jit(solution)/shard_map/ppermute | solution.py:28
  112.9 0.9 copy-start
  112.9 1.2 copy-start.1
  116.3 47.8 %collective-permute-start.11 = (bf16[2,4,256,384]{3,2,1,0:T(8,128)(2,1)S(1)}, bf16[2,4,256,384]{3,2,1,0:T(8,128)(2,1)}, u32[]{:S(2)}, u32[]{:S(2)}) collective-permute-start(bf16[2,4,256,384]{3,2,1,0:T(8,128)(2,1)S(1)} %maximum_select_fusion.2), channel_id=1, source_target_pairs={{0,2},{1,3},{2,4},{3,5},{4,6},{5,7},{6,0},{7,1},{8,14},{9,15},{10,... | collective-permute-start | bytes 4718600 | tf_op jit(solution)/shard_map/ppermute | solution.py:28
  116.7 62.1 %collective-permute-start.4 = (bf16[2,4,256,384]{3,2,1,0:T(8,128)(2,1)}, bf16[2,4,256,384]{3,2,1,0:T(8,128)(2,1)S(1)}, u32[]{:S(2)}, u32[]{:S(2)}) collective-permute-start(bf16[2,4,256,384]{3,2,1,0:T(8,128)(2,1)} %collective-permute-done.2), channel_id=1, source_target_pairs={{0,32},{1,33},{2,34},{3,35},{4,36},{5,37},{6,38},{7,39},{8,104},{9... | collective-permute-start | bytes 4718600 | tf_op jit(solution)/shard_map/ppermute | solution.py:28
  163.9 21.3 %collective-permute-start.1 = (bf16[2,4,256,384]{3,2,1,0:T(8,128)(2,1)}, bf16[2,4,256,384]{3,2,1,0:T(8,128)(2,1)}, u32[]{:S(2)}, u32[]{:S(2)}) collective-permute-start(bf16[2,4,256,384]{3,2,1,0:T(8,128)(2,1)} %maximum_select_fusion.1), channel_id=1, source_target_pairs={{0,8},{1,9},{2,10},{3,11},{4,12},{5,13},{6,14},{7,15},{8,0},{9,1},... | collective-permute-start | bytes 4718600 | tf_op jit(solution)/shard_map/ppermute | solution.py:28
  164.2 21.1 %collective-permute-start.13 = (bf16[2,4,256,384]{3,2,1,0:T(8,128)(2,1)}, bf16[2,4,256,384]{3,2,1,0:T(8,128)(2,1)}, u32[]{:S(2)}, u32[]{:S(2)}) collective-permute-start(bf16[2,4,256,384]{3,2,1,0:T(8,128)(2,1)} %collective-permute-done.11), channel_id=1, source_target_pairs={{0,2},{1,3},{2,4},{3,5},{4,6},{5,7},{6,0},{7,1},{8,14},{9,15},{10,... | collective-permute-start | bytes 4718600 | tf_op jit(solution)/shard_map/ppermute | solution.py:28
  164.3 14.0 %collective-permute-start.10 = (bf16[2,4,128,384]{3,2,1,0:T(8,128)(2,1)S(1)}, bf16[2,4,128,384]{3,2,1,0:T(8,128)(2,1)}, u32[]{:S(2)}, u32[]{:S(2)}) collective-permute-start(bf16[2,4,128,384]{3,2,1,0:T(8,128)(2,1)S(1)} %constant_dynamic-slice_fusion.3), channel_id=1, source_target_pairs={{0,8},{1,9},{2,10},{3,11},{4,12},{5,13},{6,14},{7,15},{8,0},{9,1},... | collective-permute-start | bytes 2359304 | tf_op jit(solution)/shard_map/ppermute | solution.py:28
  175.8 20.5 %collective-permute-start.3 = (bf16[2,4,256,384]{3,2,1,0:T(8,128)(2,1)}, bf16[2,4,256,384]{3,2,1,0:T(8,128)(2,1)S(1)}, u32[]{:S(2)}, u32[]{:S(2)}) collective-permute-start(bf16[2,4,256,384]{3,2,1,0:T(8,128)(2,1)} %collective-permute-done.2), channel_id=1, source_target_pairs={{0,8},{1,9},{2,10},{3,11},{4,12},{5,13},{6,14},{7,15},{8,0},{9,1},... | collective-permute-start | bytes 4718600 | tf_op jit(solution)/shard_map/ppermute | solution.py:28
  178.3 16.6 %collective-permute-start.12 = (bf16[2,4,128,384]{3,2,1,0:T(8,128)(2,1)S(1)}, bf16[2,4,128,384]{3,2,1,0:T(8,128)(2,1)S(1)}, u32[]{:S(2)}, u32[]{:S(2)}) collective-permute-start(bf16[2,4,128,384]{3,2,1,0:T(8,128)(2,1)S(1)} %constant_dynamic-slice_fusion.2), channel_id=1, source_target_pairs={{0,8},{1,9},{2,10},{3,11},{4,12},{5,13},{6,14},{7,15},{8,0},{9,1},... | collective-permute-start | bytes 2359304 | tf_op jit(solution)/shard_map/ppermute | solution.py:28
  178.8 19.6 %collective-permute-start.6 = (bf16[2,4,256,384]{3,2,1,0:T(8,128)(2,1)S(1)}, bf16[2,4,256,384]{3,2,1,0:T(8,128)(2,1)S(1)}, u32[]{:S(2)}, u32[]{:S(2)}) collective-permute-start(bf16[2,4,256,384]{3,2,1,0:T(8,128)(2,1)S(1)} %collective-permute-done.4), channel_id=1, source_target_pairs={{0,32},{1,33},{2,34},{3,35},{4,36},{5,37},{6,38},{7,39},{8,104},{9... | collective-permute-start | bytes 4718600 | tf_op jit(solution)/shard_map/ppermute | solution.py:28
  185.2 19.8 %collective-permute-start.15 = (bf16[2,4,256,384]{3,2,1,0:T(8,128)(2,1)}, bf16[2,4,256,384]{3,2,1,0:T(8,128)(2,1)S(1)}, u32[]{:S(2)}, u32[]{:S(2)}) collective-permute-start(bf16[2,4,256,384]{3,2,1,0:T(8,128)(2,1)} %collective-permute-done.13), channel_id=1, source_target_pairs={{0,2},{1,3},{2,4},{3,5},{4,6},{5,7},{6,0},{7,1},{8,14},{9,15},{10,... | collective-permute-start | bytes 4718600 | tf_op jit(solution)/shard_map/ppermute | solution.py:28
  192.0 16.7 %collective-permute-start.5 = (bf16[2,4,256,384]{3,2,1,0:T(8,128)(2,1)S(1)}, bf16[2,4,256,384]{3,2,1,0:T(8,128)(2,1)S(1)}, u32[]{:S(2)}, u32[]{:S(2)}) collective-permute-start(bf16[2,4,256,384]{3,2,1,0:T(8,128)(2,1)S(1)} %collective-permute-done.4), channel_id=1, source_target_pairs={{0,8},{1,9},{2,10},{3,11},{4,12},{5,13},{6,14},{7,15},{8,0},{9,1},... | collective-permute-start | bytes 4718600 | tf_op jit(solution)/shard_map/ppermute | solution.py:28
  196.2 12.2 %collective-permute-start.14 = (bf16[2,4,128,384]{3,2,1,0:T(8,128)(2,1)S(1)}, bf16[2,4,128,384]{3,2,1,0:T(8,128)(2,1)S(1)}, u32[]{:S(2)}, u32[]{:S(2)}) collective-permute-start(bf16[2,4,128,384]{3,2,1,0:T(8,128)(2,1)S(1)} %constant_dynamic-slice_fusion.1), channel_id=1, source_target_pairs={{0,8},{1,9},{2,10},{3,11},{4,12},{5,13},{6,14},{7,15},{8,0},{9,1},... | collective-permute-start | bytes 2359304 | tf_op jit(solution)/shard_map/ppermute | solution.py:28
  198.4 13.2 %collective-permute-start.7 = (bf16[2,4,256,384]{3,2,1,0:T(8,128)(2,1)S(1)}, bf16[2,4,256,384]{3,2,1,0:T(8,128)(2,1)S(1)}, u32[]{:S(2)}, u32[]{:S(2)}) collective-permute-start(bf16[2,4,256,384]{3,2,1,0:T(8,128)(2,1)S(1)} %collective-permute-done.6), channel_id=1, source_target_pairs={{0,8},{1,9},{2,10},{3,11},{4,12},{5,13},{6,14},{7,15},{8,0},{9,1},... | collective-permute-start | bytes 4718600 | tf_op jit(solution)/shard_map/ppermute | solution.py:28
  205.1 6.3 %collective-permute-start.16 = (bf16[2,4,128,384]{3,2,1,0:T(8,128)(2,1)S(1)}, bf16[2,4,128,384]{3,2,1,0:T(8,128)(2,1)S(1)}, u32[]{:S(2)}, u32[]{:S(2)}) collective-permute-start(bf16[2,4,128,384]{3,2,1,0:T(8,128)(2,1)S(1)} %constant_dynamic-slice_fusion), channel_id=1, source_target_pairs={{0,8},{1,9},{2,10},{3,11},{4,12},{5,13},{6,14},{7,15},{8,0},{9,1},... | collective-permute-start | bytes 2359304 | tf_op jit(solution)/shard_map/ppermute | solution.py:28

commit v2 on v0

v2 whole, which is shorter than its diff:
```python
import jax
import jax.numpy as jnp
from jax import lax
from jax.experimental import pallas as pl
from jax.experimental.pallas import tpu as pltpu
from jax.sharding import Mesh, PartitionSpec as P

AXES = ("z", "yh", "c", "x", "yl")
NTAU = 4
TAUS = [0.25 * 2.0**t for t in range(NTAU)]
NT_DIMS = (((1,), (1,)), ((), ()))


def routes(target):
    def linear(z, yh, c, x, yl):
        return (((z % 4) * 2 + yh) * 2 + c) * 8 + (x % 4) * 2 + yl

    return [
        (linear(z, yh, c, x, yl), linear(*target(z, yh, c, x, yl)))
        for z in range(4)
        for yh in range(2)
        for c in range(2)
        for x in range(4)
        for yl in range(2)
    ]


def send(block, target):
    return lax.ppermute(block, AXES, routes(target))


def kernel(shift, slots, row_src, *refs):
    sources, (out, row_pts, col_pts, vbuf, obuf, acc, row_sems, col_sems) = refs[:16], refs[16:]
    core = slots[16]
    first = pl.multiple_of(core * 128, 128)
    points = pl.ds(pl.multiple_of(core * 16, 16), 128)
    levels = pl.ds((1 - core) * 128, 1)

    def row_copy(slab):
        return pltpu.make_async_copy(row_src.at[slab], row_pts.at[slab], row_sems.at[slab])

    def col_copy(n, slab):
        return pltpu.make_async_copy(
            sources[n].at[:, pl.ds(first, 144), :], col_pts.at[slab], col_sems.at[slab]
        )

    row_copy(15).start()
    for n in range(16):
        col_copy(n, slots[n]).start()
    for n in range(15):
        row_copy(n).start()
    acc[...] = jnp.zeros_like(acc)

    @pl.loop(0, 17)
    def _(step):
        par = (step + 1) % 2
        slab = (step + 15) % 16

        @pl.when(step < 16)
        def _():
            row_copy(slab).wait()
            col_copy(0, slab).wait()

        for i in range(4):
            col = col_pts[slab, i, points, :].astype(jnp.float32)
            gap = col_pts[slab, i, levels, :].astype(jnp.float32)
            panel = jnp.concatenate(
                [(col * jnp.exp(-gap * TAUS[t])).astype(jnp.bfloat16) for t in range(NTAU)], 0
            )
            vbuf[par * 4 + i] = lax.dot_general(
                panel[:, 128:], row_pts[slab, i, :, 128:], NT_DIMS, preferred_element_type=jnp.float32
            )
            obuf[i] = lax.dot_general(
                panel[:, :128], row_pts[slab, i, :, :128], NT_DIMS, preferred_element_type=jnp.float32
            )

        @pl.when(step > 0)
        def _():
            height = 64

            @pl.loop(0, 512 // height)
            def _(g):
                rows = pl.ds(pl.multiple_of(g * height, height), height)
                occs = [obuf[i, rows, :] for i in range(4)]
                for q in range(3):
                    total = acc[q, rows, :]
                    for i in range(4):
                        total = total + occs[i] * vbuf[(par * 4 + i - shift[q] + 8) % 8, rows, :]
                    acc[q, rows, :] = total

    for q in range(3):
        for t in range(NTAU):
            out[q, t] = acc[q, t * 128 : (t + 1) * 128, :].T


def polarizability(shift, slots, row_pts, sources):
    anywhere = pl.BlockSpec(memory_space=pl.ANY)
    scalars = pl.BlockSpec(memory_space=pltpu.SMEM)
    return pl.pallas_call(
        kernel,
        in_specs=[scalars, scalars] + [anywhere] * 17,
        out_specs=pl.BlockSpec(memory_space=pltpu.VMEM),
        scratch_shapes=[
            pltpu.VMEM((16, 4, 256, 384), jnp.bfloat16),
            pltpu.VMEM((16, 4, 144, 384), jnp.bfloat16),
            pltpu.VMEM((8, 512, 256), jnp.float32),
            pltpu.VMEM((4, 512, 256), jnp.float32),
            pltpu.VMEM((3, 512, 256), jnp.float32),
            pltpu.SemaphoreType.DMA((16,)),
            pltpu.SemaphoreType.DMA((16,)),
        ],
        out_shape=jax.ShapeDtypeStruct((3, NTAU, 256, 128), jnp.float32),
        compiler_params=pltpu.CompilerParams(vmem_limit_bytes=44 * 2**20),
    )(shift, slots, row_pts, *sources)


def on_device(occ_orbitals, virt_orbitals, occ_gap, virt_gap, partner):
    z, yh, c, x, yl = (lax.axis_index(a) for a in AXES)
    shift = (-partner[:, 0]) % 64
    own = jnp.concatenate([occ_orbitals, virt_orbitals], axis=2)
    gaps = jnp.concatenate([occ_gap, virt_gap], axis=1)
    gaps = jnp.broadcast_to(gaps[:, None, :], (4, 16, 384))
    carried = jnp.concatenate([own[:, :128], gaps, own[:, 128:]], axis=1)
    row_pts = lax.all_gather(own, ("z", "yh", "c"), axis=0)

    same = [send(carried, lambda z, yh, c, x, yl: (x, yl, c, x + z, yh))]
    cross = [send(same[0], lambda z, yh, c, x, yl: (z, yh, c, x, 1 - yl))]
    for ring in (same, cross):
        for _ in range(3):
            ring.append(send(ring[-1], lambda z, yh, c, x, yl: (z, yh, c, x + 1 - 2 * c, yl)))
    sources, slots = [], []
    for s in range(4):
        for ring, yl_held in ((same, yl), (cross, 1 - yl)):
            got = send(ring[s], lambda z, yh, c, x, yl: (z, yh, 1 - c, x, yl))
            for block, core in ((ring[s], c), (got, 1 - c)):
                sources.append(block)
                slots.append((x - z + (2 * core - 1) * s) % 4 * 4 + yl_held * 2 + core)
    slots = jnp.stack(slots + [c]).astype(jnp.int32)
    return polarizability(shift, slots, row_pts, sources)


def solution(mesh):
    fine = Mesh(mesh.devices.reshape(4, 2, 2, 4, 2), AXES)
    kpt, row = ("z", "yh", "c"), ("x", "yl")
    in_specs = (P(kpt, row, None), P(kpt, row, None), P(kpt, None), P(kpt, None), P())
    return jax.shard_map(
        on_device, mesh=fine, in_specs=in_specs, out_specs=P(None, None, row, kpt), check_vma=False
    )
```

time: 674 us -> 164 us (0.24)
  the two profiles are of different devices: /device:TPU:1 before, /device:TPU:113 now
where the time goes in v2:
time: 164 us; the launch traced here: 163 us
  waiting for transfers between devices  67.9 us (41%)
  starting transfers between devices  41.4 us (25%)
  Pallas kernels  29.7 us (18%)
  between operations  13.5 us (8%)
  local copies, waits for them, and re-layouts  10.6 us (6%)
    ppermute x16, waiting for transfers between devices, send(): return lax.ppermute(block, AXES, routes(target))  67.9 us
    ppermute x16, starting transfers between devices, send(): return lax.ppermute(block, AXES, routes(target))  41.4 us
    pallas_call x1, Pallas kernels, polarizability(): pl.pallas_call(kernel, in_specs=[scalars, scalars] + [anywhere] * 17, out...  29.7 us
    unnamed x21, local copies, waits for them, and re-layouts  8.09 us
  transfers between devices with their start and end apart: 17, of which 5 were waited for; matrix products, arithmetic and copies ran while one was open for 1% of the time, Pallas kernels for 0%

profile of v2, /device:TPU:113, one launch (start us, length us, event | category | flops | bytes accessed | tf_op | source)
XLA Modules:
  0.0 163.2 jit_solution(8523878520388286680)
XLA Ops:
  6.5 1.0 constant_dynamic-update-slice_fusion.1
  7.6 1.1 constant_dynamic-update-slice_fusion
  8.7 0.9 copy-done.6
  9.6 0.0 all-gather.3.cloned.1.call-update
  9.6 0.0 copy-start.8
  9.7 1.2 fusion.1
  10.9 0.1 pad_maximum_fusion
  11.0 2.9 %collective-permute-start = (bf16[4,272,384]{2,1,0:T(8,128)(2,1)S(1)}, bf16[4,272,384]{2,1,0:T(8,128)(2,1)S(1)}, u32[]{:S(2)}, u32[]{:S(2)}) collective-permute-start(bf16[4,272,384]{2,1,0:T(8,128)(2,1)S(1)} %pad_maximum_fusion), channel_id=1, source_target_pairs={{0,0},{1,16},{2,34},{3,50},{4,68},{5,84},{6,102},{7,118},{8,8},{9,... | collective-permute-start | bytes 2506760 | tf_op jit(solution)/shard_map/ppermute | solution.py:29
  13.9 31.1 %collective-permute-done.refs_0_ = bf16[4,272,384]{2,1,0:T(8,128)(2,1)S(1)} collective-permute-done((bf16[4,272,384]{2,1,0:T(8,128)(2,1)S(1)}, bf16[4,272,384]{2,1,0:T(8,128)(2,1)S(1)}, u32[]{:S(2)}, u32[]{:S(2)}) %collective-permute-start) | collective-permute-done | bytes 835616 | tf_op jit(solution)/shard_map/ppermute | solution.py:29
  45.0 0.0 collective-permute-start.2
  45.0 0.4 collective-permute-start.4
  45.4 18.2 %collective-permute-done.2.refs_2_ = bf16[4,272,384]{2,1,0:T(8,128)(2,1)S(1)} collective-permute-done((bf16[4,272,384]{2,1,0:T(8,128)(2,1)S(1)}, bf16[4,272,384]{2,1,0:T(8,128)(2,1)S(1)}, u32[]{:S(2)}, u32[]{:S(2)}) %collective-permute-start.2) | collective-permute-done | bytes 835616 | tf_op jit(solution)/shard_map/ppermute | solution.py:29
  63.6 0.2 collective-permute-start.6
  63.9 0.0 collective-permute-done.4.refs_4_
  63.9 0.0 collective-permute-start.8
  63.9 11.5 %collective-permute-done.6.refs_6_ = bf16[4,272,384]{2,1,0:T(8,128)(2,1)S(1)} collective-permute-done((bf16[4,272,384]{2,1,0:T(8,128)(2,1)S(1)}, bf16[4,272,384]{2,1,0:T(8,128)(2,1)S(1)}, u32[]{:S(2)}, u32[]{:S(2)}) %collective-permute-start.6) | collective-permute-done | bytes 835616 | tf_op jit(solution)/shard_map/ppermute | solution.py:29
  75.4 1.4 collective-permute-start.10
  76.8 8.1 %collective-permute-start.1 = (bf16[4,272,384]{2,1,0:T(8,128)(2,1)S(1)}, bf16[4,272,384]{2,1,0:T(8,128)(2,1)S(1)}, u32[]{:S(2)}, u32[]{:S(2)}) collective-permute-start(bf16[4,272,384]{2,1,0:T(8,128)(2,1)S(1)} %collective-permute-done.refs_0_), channel_id=1, source_target_pairs={{0,8},{1,9},{2,10},{3,11},{4,12},{5,13},{6,14},{7,15},{8,0},{9,1},... | collective-permute-start | bytes 2506760 | tf_op jit(solution)/shard_map/ppermute | solution.py:29
  84.9 0.0 collective-permute-start.5
  84.9 0.5 collective-permute-start.3
  85.5 0.0 collective-permute-done.8.refs_8_
  85.5 3.0 %collective-permute-start.12 = (bf16[4,272,384]{2,1,0:T(8,128)(2,1)}, bf16[4,272,384]{2,1,0:T(8,128)(2,1)}, u32[]{:S(2)}, u32[]{:S(2)}) collective-permute-start(bf16[4,272,384]{2,1,0:T(8,128)(2,1)} %collective-permute-done.8.refs_8_), channel_id=1, source_target_pairs={{0,2},{1,3},{2,4},{3,5},{4,6},{5,7},{6,0},{7,1},{8,14},{9,15},{10,... | collective-permute-start | bytes 2506760 | tf_op jit(solution)/shard_map/ppermute | solution.py:29
  88.4 4.9 %collective-permute-done.10.refs_10_ = bf16[4,272,384]{2,1,0:T(8,128)(2,1)} collective-permute-done((bf16[4,272,384]{2,1,0:T(8,128)(2,1)S(1)}, bf16[4,272,384]{2,1,0:T(8,128)(2,1)}, u32[]{:S(2)}, u32[]{:S(2)}) %collective-permute-start.10) | collective-permute-done | bytes 835616 | tf_op jit(solution)/shard_map/ppermute | solution.py:29
  93.3 1.4 collective-permute-start.14
  94.7 0.0 collective-permute-done.1.refs_1_
  94.7 0.9 copy-done
  95.6 8.3 %collective-permute-start.9 = (bf16[4,272,384]{2,1,0:T(8,128)(2,1)}, bf16[4,272,384]{2,1,0:T(8,128)(2,1)}, u32[]{:S(2)}, u32[]{:S(2)}) collective-permute-start(bf16[4,272,384]{2,1,0:T(8,128)(2,1)} %collective-permute-done.8.refs_8_), channel_id=1, source_target_pairs={{0,8},{1,9},{2,10},{3,11},{4,12},{5,13},{6,14},{7,15},{8,0},{9,1},... | collective-permute-start | bytes 2506760 | tf_op jit(solution)/shard_map/ppermute | solution.py:29
  103.9 0.0 collective-permute-done.5.refs_5_
  103.9 0.9 copy-done.2
  104.7 0.0 collective-permute-start.7
  104.8 0.0 collective-permute-done.3.refs_3_
  104.8 0.9 copy-done.4
  105.7 0.5 collective-permute-start.11
  106.2 0.0 collective-permute-done.12.refs_12_
  106.2 5.7 %collective-permute-start.13 = (bf16[4,272,384]{2,1,0:T(8,128)(2,1)}, bf16[4,272,384]{2,1,0:T(8,128)(2,1)}, u32[]{:S(2)}, u32[]{:S(2)}) collective-permute-start(bf16[4,272,384]{2,1,0:T(8,128)(2,1)} %collective-permute-done.12.refs_12_), channel_id=1, source_target_pairs={{0,8},{1,9},{2,10},{3,11},{4,12},{5,13},{6,14},{7,15},{8,0},{9,1},... | collective-permute-start | bytes 2506760 | tf_op jit(solution)/shard_map/ppermute | solution.py:29
  111.9 0.0 collective-permute-done.14.refs_14_
  111.9 8.9 %collective-permute-start.15 = (bf16[4,272,384]{2,1,0:T(8,128)(2,1)}, bf16[4,272,384]{2,1,0:T(8,128)(2,1)}, u32[]{:S(2)}, u32[]{:S(2)}) collective-permute-start(bf16[4,272,384]{2,1,0:T(8,128)(2,1)} %collective-permute-done.14.refs_14_), channel_id=1, source_target_pairs={{0,8},{1,9},{2,10},{3,11},{4,12},{5,13},{6,14},{7,15},{8,0},{9,1},... | collective-permute-start | bytes 2506760 | tf_op jit(solution)/shard_map/ppermute | solution.py:29
  120.9 0.1 stack.71.slots
  121.0 0.1 slice_reduce_fusion
  121.1 0.0 collective-permute-done.9.refs_9_
  121.1 0.0 collective-permute-done.7.refs_7_
  121.1 0.0 collective-permute-done.13.refs_13_
  121.1 0.0 collective-permute-done.11.refs_11_
  121.1 2.1 %collective-permute-done.15.refs_15_ = bf16[4,272,384]{2,1,0:T(8,128)(2,1)} collective-permute-done((bf16[4,272,384]{2,1,0:T(8,128)(2,1)}, bf16[4,272,384]{2,1,0:T(8,128)(2,1)}, u32[]{:S(2)}, u32[]{:S(2)}) %collective-permute-start.15) | collective-permute-done | bytes 835616 | tf_op jit(solution)/shard_map/ppermute | solution.py:29
  123.2 1.1 copy-done.1
  124.3 1.1 copy-done.3
  125.5 1.1 copy-done.5
  126.6 29.7 %shard_map.55 = f32[3,4,256,128]{3,2,1,0:T(8,128)} custom-call(s32[3]{0:T(128)S(1)} %and_select_fusion.shift, s32[17]{0:T(128)S(1)} %stack.71.slots, bf16[16,4,256,384]{3,2,1,0:T(8,128)(2,1)} %bitcast.18, bf16[4,272,384]{2,1,0:T(8,128)(2,1)S(1)} %collective-permute-done.refs_0_, bf16[4,272,384]{2,1,0:T(8,128)(2,1)S(1)} %copy-done.1, ...), custom_call_target="tpu_custom_call" | custom-call | tf_op jit(solution)/shard_map/pallas_call | solution.py:99
  (17 shorter events, 0.1 us)
Async XLA Ops:
  6.5 3.1 %copy-start.7 = (bf16[4,256]{1,0:T(4,128)(2,1)S(1)}, bf16[4,256]{1,0:T(4,128)(2,1)}, u32[]{:S(2)}) copy-start(bf16[4,256]{1,0:T(4,128)(2,1)} %param.8) | copy-start | bytes 6148
  6.5 3.1 %copy-start.9 = (bf16[4,128]{1,0:T(4,128)(2,1)S(1)}, bf16[4,128]{1,0:T(4,128)(2,1)}, u32[]{:S(2)}) copy-start(bf16[4,128]{1,0:T(4,128)(2,1)} %param.7) | copy-start | bytes 3076
  6.5 116.6 %all-gather.3.cloned.1.call-start = ((), (), s32[]{:S(2)}) async-start(), calls=%async_computation | async-start | bytes 13369344 | tf_op jit(solution)/shard_map/all_gather | solution.py:124
  8.6 0.9 copy-start.6
  9.6 111.3 %copy-start.8 = (s32[3,64]{1,0:T(4,128)S(1)}, s32[3,64]{1,0:T(4,128)}, u32[]{:S(2)}) copy-start(s32[3,64]{1,0:T(4,128)} %param.9) | copy-start | bytes 2308
  11.0 34.1 %collective-permute-start = (bf16[4,272,384]{2,1,0:T(8,128)(2,1)S(1)}, bf16[4,272,384]{2,1,0:T(8,128)(2,1)S(1)}, u32[]{:S(2)}, u32[]{:S(2)}) collective-permute-start(bf16[4,272,384]{2,1,0:T(8,128)(2,1)S(1)} %pad_maximum_fusion), channel_id=1, source_target_pairs={{0,0},{1,16},{2,34},{3,50},{4,68},{5,84},{6,102},{7,118},{8,8},{9,... | collective-permute-start | bytes 2506760 | tf_op jit(solution)/shard_map/ppermute | solution.py:29
  45.0 18.6 %collective-permute-start.2 = (bf16[4,272,384]{2,1,0:T(8,128)(2,1)S(1)}, bf16[4,272,384]{2,1,0:T(8,128)(2,1)S(1)}, u32[]{:S(2)}, u32[]{:S(2)}) collective-permute-start(bf16[4,272,384]{2,1,0:T(8,128)(2,1)S(1)} %collective-permute-done.refs_0_), channel_id=1, source_target_pairs={{0,1},{1,0},{2,3},{3,2},{4,5},{5,4},{6,7},{7,6},{8,9},{9,8},{10,11... | collective-permute-start | bytes 2506760 | tf_op jit(solution)/shard_map/ppermute | solution.py:29
  45.0 18.8 %collective-permute-start.4 = (bf16[4,272,384]{2,1,0:T(8,128)(2,1)S(1)}, bf16[4,272,384]{2,1,0:T(8,128)(2,1)S(1)}, u32[]{:S(2)}, u32[]{:S(2)}) collective-permute-start(bf16[4,272,384]{2,1,0:T(8,128)(2,1)S(1)} %collective-permute-done.refs_0_), channel_id=1, source_target_pairs={{0,2},{1,3},{2,4},{3,5},{4,6},{5,7},{6,0},{7,1},{8,14},{9,15},{10,... | collective-permute-start | bytes 2506760 | tf_op jit(solution)/shard_map/ppermute | solution.py:29
  63.6 11.8 %collective-permute-start.6 = (bf16[4,272,384]{2,1,0:T(8,128)(2,1)S(1)}, bf16[4,272,384]{2,1,0:T(8,128)(2,1)S(1)}, u32[]{:S(2)}, u32[]{:S(2)}) collective-permute-start(bf16[4,272,384]{2,1,0:T(8,128)(2,1)S(1)} %collective-permute-done.2.refs_2_), channel_id=1, source_target_pairs={{0,2},{1,3},{2,4},{3,5},{4,6},{5,7},{6,0},{7,1},{8,14},{9,15},{10,... | collective-permute-start | bytes 2506760 | tf_op jit(solution)/shard_map/ppermute | solution.py:29
  63.9 21.6 %collective-permute-start.8 = (bf16[4,272,384]{2,1,0:T(8,128)(2,1)S(1)}, bf16[4,272,384]{2,1,0:T(8,128)(2,1)}, u32[]{:S(2)}, u32[]{:S(2)}) collective-permute-start(bf16[4,272,384]{2,1,0:T(8,128)(2,1)S(1)} %collective-permute-done.4.refs_4_), channel_id=1, source_target_pairs={{0,2},{1,3},{2,4},{3,5},{4,6},{5,7},{6,0},{7,1},{8,14},{9,15},{10,... | collective-permute-start | bytes 2506760 | tf_op jit(solution)/shard_map/ppermute | solution.py:29
  75.4 17.9 %collective-permute-start.10 = (bf16[4,272,384]{2,1,0:T(8,128)(2,1)S(1)}, bf16[4,272,384]{2,1,0:T(8,128)(2,1)}, u32[]{:S(2)}, u32[]{:S(2)}) collective-permute-start(bf16[4,272,384]{2,1,0:T(8,128)(2,1)S(1)} %collective-permute-done.6.refs_6_), channel_id=1, source_target_pairs={{0,2},{1,3},{2,4},{3,5},{4,6},{5,7},{6,0},{7,1},{8,14},{9,15},{10,... | collective-permute-start | bytes 2506760 | tf_op jit(solution)/shard_map/ppermute | solution.py:29
  76.8 17.8 %collective-permute-start.1 = (bf16[4,272,384]{2,1,0:T(8,128)(2,1)S(1)}, bf16[4,272,384]{2,1,0:T(8,128)(2,1)S(1)}, u32[]{:S(2)}, u32[]{:S(2)}) collective-permute-start(bf16[4,272,384]{2,1,0:T(8,128)(2,1)S(1)} %collective-permute-done.refs_0_), channel_id=1, source_target_pairs={{0,8},{1,9},{2,10},{3,11},{4,12},{5,13},{6,14},{7,15},{8,0},{9,1},... | collective-permute-start | bytes 2506760 | tf_op jit(solution)/shard_map/ppermute | solution.py:29
  84.9 18.9 %collective-permute-start.5 = (bf16[4,272,384]{2,1,0:T(8,128)(2,1)S(1)}, bf16[4,272,384]{2,1,0:T(8,128)(2,1)S(1)}, u32[]{:S(2)}, u32[]{:S(2)}) collective-permute-start(bf16[4,272,384]{2,1,0:T(8,128)(2,1)S(1)} %collective-permute-done.4.refs_4_), channel_id=1, source_target_pairs={{0,8},{1,9},{2,10},{3,11},{4,12},{5,13},{6,14},{7,15},{8,0},{9,1},... | collective-permute-start | bytes 2506760 | tf_op jit(solution)/shard_map/ppermute | solution.py:29
  84.9 19.8 %collective-permute-start.3 = (bf16[4,272,384]{2,1,0:T(8,128)(2,1)S(1)}, bf16[4,272,384]{2,1,0:T(8,128)(2,1)S(1)}, u32[]{:S(2)}, u32[]{:S(2)}) collective-permute-start(bf16[4,272,384]{2,1,0:T(8,128)(2,1)S(1)} %collective-permute-done.2.refs_2_), channel_id=1, source_target_pairs={{0,8},{1,9},{2,10},{3,11},{4,12},{5,13},{6,14},{7,15},{8,0},{9,1},... | collective-permute-start | bytes 2506760 | tf_op jit(solution)/shard_map/ppermute | solution.py:29
  85.5 20.7 %collective-permute-start.12 = (bf16[4,272,384]{2,1,0:T(8,128)(2,1)}, bf16[4,272,384]{2,1,0:T(8,128)(2,1)}, u32[]{:S(2)}, u32[]{:S(2)}) collective-permute-start(bf16[4,272,384]{2,1,0:T(8,128)(2,1)} %collective-permute-done.8.refs_8_), channel_id=1, source_target_pairs={{0,2},{1,3},{2,4},{3,5},{4,6},{5,7},{6,0},{7,1},{8,14},{9,15},{10,... | collective-permute-start | bytes 2506760 | tf_op jit(solution)/shard_map/ppermute | solution.py:29
  93.3 18.6 %collective-permute-start.14 = (bf16[4,272,384]{2,1,0:T(8,128)(2,1)}, bf16[4,272,384]{2,1,0:T(8,128)(2,1)}, u32[]{:S(2)}, u32[]{:S(2)}) collective-permute-start(bf16[4,272,384]{2,1,0:T(8,128)(2,1)} %collective-permute-done.10.refs_10_), channel_id=1, source_target_pairs={{0,2},{1,3},{2,4},{3,5},{4,6},{5,7},{6,0},{7,1},{8,14},{9,15},{10,... | collective-permute-start | bytes 2506760 | tf_op jit(solution)/shard_map/ppermute | solution.py:29
  94.7 0.9 copy-start
  95.6 25.5 %collective-permute-start.9 = (bf16[4,272,384]{2,1,0:T(8,128)(2,1)}, bf16[4,272,384]{2,1,0:T(8,128)(2,1)}, u32[]{:S(2)}, u32[]{:S(2)}) collective-permute-start(bf16[4,272,384]{2,1,0:T(8,128)(2,1)} %collective-permute-done.8.refs_8_), channel_id=1, source_target_pairs={{0,8},{1,9},{2,10},{3,11},{4,12},{5,13},{6,14},{7,15},{8,0},{9,1},... | collective-permute-start | bytes 2506760 | tf_op jit(solution)/shard_map/ppermute | solution.py:29
  103.9 0.9 copy-start.2
  104.7 16.4 %collective-permute-start.7 = (bf16[4,272,384]{2,1,0:T(8,128)(2,1)S(1)}, bf16[4,272,384]{2,1,0:T(8,128)(2,1)}, u32[]{:S(2)}, u32[]{:S(2)}) collective-permute-start(bf16[4,272,384]{2,1,0:T(8,128)(2,1)S(1)} %collective-permute-done.6.refs_6_), channel_id=1, source_target_pairs={{0,8},{1,9},{2,10},{3,11},{4,12},{5,13},{6,14},{7,15},{8,0},{9,1},... | collective-permute-start | bytes 2506760 | tf_op jit(solution)/shard_map/ppermute | solution.py:29
  104.8 0.9 copy-start.4
  105.7 15.5 %collective-permute-start.11 = (bf16[4,272,384]{2,1,0:T(8,128)(2,1)}, bf16[4,272,384]{2,1,0:T(8,128)(2,1)}, u32[]{:S(2)}, u32[]{:S(2)}) collective-permute-start(bf16[4,272,384]{2,1,0:T(8,128)(2,1)} %collective-permute-done.10.refs_10_), channel_id=1, source_target_pairs={{0,8},{1,9},{2,10},{3,11},{4,12},{5,13},{6,14},{7,15},{8,0},{9,1},... | collective-permute-start | bytes 2506760 | tf_op jit(solution)/shard_map/ppermute | solution.py:29
  106.2 14.9 %collective-permute-start.13 = (bf16[4,272,384]{2,1,0:T(8,128)(2,1)}, bf16[4,272,384]{2,1,0:T(8,128)(2,1)}, u32[]{:S(2)}, u32[]{:S(2)}) collective-permute-start(bf16[4,272,384]{2,1,0:T(8,128)(2,1)} %collective-permute-done.12.refs_12_), channel_id=1, source_target_pairs={{0,8},{1,9},{2,10},{3,11},{4,12},{5,13},{6,14},{7,15},{8,0},{9,1},... | collective-permute-start | bytes 2506760 | tf_op jit(solution)/shard_map/ppermute | solution.py:29
  111.9 11.3 %collective-permute-start.15 = (bf16[4,272,384]{2,1,0:T(8,128)(2,1)}, bf16[4,272,384]{2,1,0:T(8,128)(2,1)}, u32[]{:S(2)}, u32[]{:S(2)}) collective-permute-start(bf16[4,272,384]{2,1,0:T(8,128)(2,1)} %collective-permute-done.14.refs_14_), channel_id=1, source_target_pairs={{0,8},{1,9},{2,10},{3,11},{4,12},{5,13},{6,14},{7,15},{8,0},{9,1},... | collective-permute-start | bytes 2506760 | tf_op jit(solution)/shard_map/ppermute | solution.py:29
  123.2 1.2 copy-start.1
  124.3 1.1 copy-start.3
  125.5 1.1 copy-start.5
Sparse Core Ops, SparseCore 0:
  9.8 100.4 all-gather.2

commit v3 on v2

v3 whole, which is shorter than its diff:
```python
import jax
import jax.numpy as jnp
from jax import lax
from jax.experimental import pallas as pl
from jax.experimental.pallas import tpu as pltpu
from jax.sharding import Mesh, PartitionSpec as P

AXES = ("z", "yh", "c", "x", "yl")
NTAU = 4
TAUS = [0.25 * 2.0**t for t in range(NTAU)]
NT_DIMS = (((1,), (1,)), ((), ()))


def routes(target):
    def linear(z, yh, c, x, yl):
        return (((z % 4) * 2 + yh) * 2 + c) * 8 + (x % 4) * 2 + yl

    return [
        (linear(z, yh, c, x, yl), linear(*target(z, yh, c, x, yl)))
        for z in range(4)
        for yh in range(2)
        for c in range(2)
        for x in range(4)
        for yl in range(2)
    ]


def send(block, target):
    return lax.ppermute(block, AXES, routes(target))


def kernel(shift, source, *refs):
    row_src, col_src, refs = refs[:16], refs[16:32], refs[32:]
    out, row_pts, col_pts, vbuf, obuf, acc, row_sems, col_sems = refs
    core = source[32]
    first = pl.multiple_of(core * 128, 128)
    points = pl.ds(pl.multiple_of(core * 16, 16), 128)
    levels = pl.ds((1 - core) * 128, 1)

    def row_copy(n, slot):
        return pltpu.make_async_copy(row_src[n], row_pts.at[slot], row_sems.at[slot])

    def col_copy(n, slot):
        return pltpu.make_async_copy(
            col_src[n].at[:, pl.ds(first, 144), :], col_pts.at[slot], col_sems.at[slot]
        )

    def fetch(step):
        slab, slot = lax.rem(step + 15, 16), lax.rem(step, 3)
        row_from, col_from = source[slab], source[16 + slab]
        for n in range(16):

            @pl.when(row_from == n)
            def _():
                row_copy(n, slot).start()

            @pl.when(col_from == n)
            def _():
                col_copy(n, slot).start()

    fetch(0)
    fetch(1)
    acc[...] = jnp.zeros_like(acc)

    @pl.loop(0, 17)
    def _(step):
        par = lax.rem(step + 1, 2) * 4
        slot = lax.rem(step, 3)

        @pl.when(step < 15)
        def _():
            fetch(step + 2)

        row_copy(0, slot).wait()
        col_copy(0, slot).wait()
        for i in range(4):
            col = col_pts[slot, i, points, :].astype(jnp.float32)
            gap = col_pts[slot, i, levels, :].astype(jnp.float32)
            panel = jnp.concatenate(
                [(col * jnp.exp(-gap * TAUS[t])).astype(jnp.bfloat16) for t in range(NTAU)], 0
            )
            vbuf[par + i] = lax.dot_general(
                panel[:, 128:], row_pts[slot, i, :, 128:], NT_DIMS, preferred_element_type=jnp.float32
            )
            obuf[i] = lax.dot_general(
                panel[:, :128], row_pts[slot, i, :, :128], NT_DIMS, preferred_element_type=jnp.float32
            )

        @pl.when(step > 0)
        def _():
            height = 32
            for g in range(512 // height):
                rows = pl.ds(g * height, height)
                occs = [obuf[i, rows, :] for i in range(4)]
                for q in range(3):
                    total = acc[q, rows, :]
                    for i in range(4):
                        total = total + occs[i] * vbuf[lax.rem(par + i - shift[q] + 8, 8), rows, :]
                    acc[q, rows, :] = total

    for q in range(3):
        for t in range(NTAU):
            out[q, t] = acc[q, t * 128 : (t + 1) * 128, :].T


def polarizability(shift, source, pieces):
    anywhere = pl.BlockSpec(memory_space=pl.ANY)
    scalars = pl.BlockSpec(memory_space=pltpu.SMEM)
    return pl.pallas_call(
        kernel,
        in_specs=[scalars, scalars] + [anywhere] * 32,
        out_specs=pl.BlockSpec(memory_space=pltpu.VMEM),
        scratch_shapes=[
            pltpu.VMEM((3, 4, 256, 384), jnp.bfloat16),
            pltpu.VMEM((3, 4, 144, 384), jnp.bfloat16),
            pltpu.VMEM((8, 512, 256), jnp.float32),
            pltpu.VMEM((4, 512, 256), jnp.float32),
            pltpu.VMEM((3, 512, 256), jnp.float32),
            pltpu.SemaphoreType.DMA((3,)),
            pltpu.SemaphoreType.DMA((3,)),
        ],
        out_shape=jax.ShapeDtypeStruct((3, NTAU, 256, 128), jnp.float32),
        compiler_params=pltpu.CompilerParams(vmem_limit_bytes=20 * 2**20),
    )(shift, source, *[pltpu.with_memory_space_constraint(p, pltpu.HBM) for p in pieces])


def after(block, *others):
    return lax.optimization_barrier((block,) + others)[0]


def swap(block):
    return send(block, lambda z, yh, c, x, yl: (z, yh, 1 - c, x, yl))


def z_step(block, sign):
    return send(block, lambda z, yh, c, x, yl: (z + sign * (1 - 2 * c), yh, c, x, yl))


def x_step(block, sign):
    return send(block, lambda z, yh, c, x, yl: (z, yh, c, x + sign * (1 - 2 * c), yl))


def across_yh(block):
    return send(block, lambda z, yh, c, x, yl: (z, 1 - yh, c, x, yl))


def on_device(occ_orbitals, virt_orbitals, occ_gap, virt_gap, partner):
    z, yh, c, x, yl = (lax.axis_index(a) for a in AXES)
    shift = (-partner[:, 0]) % 64
    own = jnp.concatenate([occ_orbitals, virt_orbitals], axis=2)
    gaps = jnp.concatenate([occ_gap, virt_gap], axis=1)
    gaps = jnp.broadcast_to(gaps[:, None, :], (4, 16, 384))
    carried = jnp.concatenate([own[:, :128], gaps, own[:, 128:]], axis=1)

    cols = send(carried, lambda z, yh, c, x, yl: (x, yl, c, x + z, yh))
    cols_same, rows_same = [cols], [own]
    cols_cross = [send(cols, lambda z, yh, c, x, yl: (z, yh, c, x, 1 - yl))]
    for _ in range(3):
        rows_same.append(z_step(rows_same[-1], 1))
        cols_same.append(x_step(cols_same[-1], 1))
    rows_cross = [across_yh(own)]
    cols_cross.append(x_step(cols_cross[0], 1))
    rows_cross.append(z_step(rows_cross[0], 1))
    cols_cross += [x_step(cols_cross[1], 1)]
    cols_cross += [x_step(cols_cross[2], 1)]
    rows_cross += [z_step(rows_cross[1], 1)]
    rows_cross += [z_step(rows_cross[2], 1)]

    def placed(pieces, at, low):
        found = []
        for piece, offset in zip(pieces, range(4)):
            for block, core in ((piece, c), (swap(piece), 1 - c)):
                found.append((block, (at + (2 * core - 1) * offset) % 4 * 4 + low * 2 + core))
        return found

    pieces = placed(rows_same, z, yh) + placed(rows_cross, z, 1 - yh)
    pieces += placed(cols_same, x - z, yl) + placed(cols_cross, x - z, 1 - yl)
    slots = jnp.stack([slot for _, slot in pieces])
    held = jnp.arange(16)
    source = [jnp.sum((part[:, None] == held) * held[:, None], axis=0) for part in (slots[:16], slots[16:])]
    source = jnp.concatenate(source + [c[None]]).astype(jnp.int32)
    return polarizability(shift, source, [block for block, _ in pieces])


def solution(mesh):
    fine = Mesh(mesh.devices.reshape(4, 2, 2, 4, 2), AXES)
    kpt, row = ("z", "yh", "c"), ("x", "yl")
    in_specs = (P(kpt, row, None), P(kpt, row, None), P(kpt, None), P(kpt, None), P())
    return jax.shard_map(
        on_device, mesh=fine, in_specs=in_specs, out_specs=P(None, None, row, kpt), check_vma=False
    )
```

time: 164 us -> 146 us (0.89)
  the two profiles are of different devices: /device:TPU:113 before, /device:TPU:1 now
where the time goes in v3:
time: 146 us
  starting transfers between devices  64.6 us (44%)
  waiting for transfers between devices  53.8 us (37%)
  Pallas kernels  23.8 us (16%)
  local copies, waits for them, and re-layouts  3.35 us (2%)
    ppermute x31, starting transfers between devices, send(): return lax.ppermute(block, AXES, routes(target))  64.6 us
    ppermute x31, waiting for transfers between devices, send(): return lax.ppermute(block, AXES, routes(target))  53.8 us
    pallas_call x1, Pallas kernels, polarizability(): pl.pallas_call(kernel, in_specs=[scalars, scalars] + [anywhere] * 32, out...  23.8 us
  transfers between devices with their start and end apart: 31, of which 11 were waited for; matrix products, arithmetic and copies ran while one was open for 0% of the time, Pallas kernels for 0%

profile of v3, /device:TPU:1, one launch (start us, length us, event | category | flops | bytes accessed | tf_op | source)
XLA Modules:
  0.0 146.1 jit_solution(1257124629390293158)
XLA Ops:
  0.0 1.0 constant_dynamic-update-slice_fusion.1
  1.0 1.1 constant_dynamic-update-slice_fusion.refs_0_
  2.1 3.8 %collective-permute-start.7 = (bf16[4,256,384]{2,1,0:T(8,128)(2,1)S(1)}, bf16[4,256,384]{2,1,0:T(8,128)(2,1)S(1)}, u32[]{:S(2)}, u32[]{:S(2)}) collective-permute-start(bf16[4,256,384]{2,1,0:T(8,128)(2,1)S(1)} %constant_dynamic-update-slice_fusion.refs_0_), channel_id=1, source_target_pairs={{0,16},{1,17},{2,18},{3,19},{4,20},{5,21},{6,22},{7,23},{8,24},{9,... | collective-permute-start | bytes 2359304 | tf_op jit(solution)/shard_map/ppermute | solution.py:29
  6.0 0.1 fusion.1
  6.1 0.1 pad_maximum_fusion
  6.2 0.7 collective-permute-start.15
  6.9 6.1 %collective-permute-start.1 = (bf16[4,256,384]{2,1,0:T(8,128)(2,1)S(1)}, bf16[4,256,384]{2,1,0:T(8,128)(2,1)S(1)}, u32[]{:S(2)}, u32[]{:S(2)}) collective-permute-start(bf16[4,256,384]{2,1,0:T(8,128)(2,1)S(1)} %constant_dynamic-update-slice_fusion.refs_0_), channel_id=1, source_target_pairs={{0,32},{1,33},{2,34},{3,35},{4,36},{5,37},{6,38},{7,39},{8,104},{9... | collective-permute-start | bytes 2359304 | tf_op jit(solution)/shard_map/ppermute | solution.py:29
  13.0 9.9 %collective-permute-done.7.refs_8_ = bf16[4,256,384]{2,1,0:T(8,128)(2,1)S(1)} collective-permute-done((bf16[4,256,384]{2,1,0:T(8,128)(2,1)S(1)}, bf16[4,256,384]{2,1,0:T(8,128)(2,1)S(1)}, u32[]{:S(2)}, u32[]{:S(2)}) %collective-permute-start.7) | collective-permute-done | bytes 786464 | tf_op jit(solution)/shard_map/ppermute | solution.py:29
  22.9 15.4 %collective-permute-start.9 = (bf16[4,256,384]{2,1,0:T(8,128)(2,1)S(1)}, bf16[4,256,384]{2,1,0:T(8,128)(2,1)S(1)}, u32[]{:S(2)}, u32[]{:S(2)}) collective-permute-start(bf16[4,256,384]{2,1,0:T(8,128)(2,1)S(1)} %collective-permute-done.7.refs_8_), channel_id=1, source_target_pairs={{0,32},{1,33},{2,34},{3,35},{4,36},{5,37},{6,38},{7,39},{8,104},{9... | collective-permute-start | bytes 2359304 | tf_op jit(solution)/shard_map/ppermute | solution.py:29
  38.3 3.0 %collective-permute-start.8 = (bf16[4,256,384]{2,1,0:T(8,128)(2,1)S(1)}, bf16[4,256,384]{2,1,0:T(8,128)(2,1)}, u32[]{:S(2)}, u32[]{:S(2)}) collective-permute-start(bf16[4,256,384]{2,1,0:T(8,128)(2,1)S(1)} %collective-permute-done.7.refs_8_), channel_id=1, source_target_pairs={{0,8},{1,9},{2,10},{3,11},{4,12},{5,13},{6,14},{7,15},{8,0},{9,1},... | collective-permute-start | bytes 2359304 | tf_op jit(solution)/shard_map/ppermute | solution.py:29
  41.4 1.8 %collective-permute-start.23 = (bf16[4,272,384]{2,1,0:T(8,128)(2,1)S(1)}, bf16[4,272,384]{2,1,0:T(8,128)(2,1)S(1)}, u32[]{:S(2)}, u32[]{:S(2)}) collective-permute-start(bf16[4,272,384]{2,1,0:T(8,128)(2,1)S(1)} %collective-permute-done.15.refs_16_), channel_id=1, source_target_pairs={{0,1},{1,0},{2,3},{3,2},{4,5},{5,4},{6,7},{7,6},{8,9},{9,8},{10,11... | collective-permute-start | bytes 2506760 | tf_op jit(solution)/shard_map/ppermute | solution.py:29
  43.2 5.0 %collective-permute-start.17 = (bf16[4,272,384]{2,1,0:T(8,128)(2,1)S(1)}, bf16[4,272,384]{2,1,0:T(8,128)(2,1)S(1)}, u32[]{:S(2)}, u32[]{:S(2)}) collective-permute-start(bf16[4,272,384]{2,1,0:T(8,128)(2,1)S(1)} %collective-permute-done.15.refs_16_), channel_id=1, source_target_pairs={{0,2},{1,3},{2,4},{3,5},{4,6},{5,7},{6,0},{7,1},{8,14},{9,15},{10,... | collective-permute-start | bytes 2506760 | tf_op jit(solution)/shard_map/ppermute | solution.py:29
  48.2 1.8 %collective-permute-start.3 = (bf16[4,256,384]{2,1,0:T(8,128)(2,1)S(1)}, bf16[4,256,384]{2,1,0:T(8,128)(2,1)S(1)}, u32[]{:S(2)}, u32[]{:S(2)}) collective-permute-start(bf16[4,256,384]{2,1,0:T(8,128)(2,1)S(1)} %collective-permute-done.1.refs_2_), channel_id=1, source_target_pairs={{0,32},{1,33},{2,34},{3,35},{4,36},{5,37},{6,38},{7,39},{8,104},{9... | collective-permute-start | bytes 2359304 | tf_op jit(solution)/shard_map/ppermute | solution.py:29
  50.0 1.3 collective-permute-start.2
  51.3 0.1 collective-permute-start.16
  51.4 10.4 %collective-permute-done.23.refs_24_ = bf16[4,272,384]{2,1,0:T(8,128)(2,1)S(1)} collective-permute-done((bf16[4,272,384]{2,1,0:T(8,128)(2,1)S(1)}, bf16[4,272,384]{2,1,0:T(8,128)(2,1)S(1)}, u32[]{:S(2)}, u32[]{:S(2)}) %collective-permute-start.23) | collective-permute-done | bytes 835616 | tf_op jit(solution)/shard_map/ppermute | solution.py:29
  61.7 5.1 %collective-permute-start.25 = (bf16[4,272,384]{2,1,0:T(8,128)(2,1)S(1)}, bf16[4,272,384]{2,1,0:T(8,128)(2,1)S(1)}, u32[]{:S(2)}, u32[]{:S(2)}) collective-permute-start(bf16[4,272,384]{2,1,0:T(8,128)(2,1)S(1)} %collective-permute-done.23.refs_24_), channel_id=1, source_target_pairs={{0,2},{1,3},{2,4},{3,5},{4,6},{5,7},{6,0},{7,1},{8,14},{9,15},{10,... | collective-permute-start | bytes 2506760 | tf_op jit(solution)/shard_map/ppermute | solution.py:29
  66.8 2.0 %collective-permute-start.11 = (bf16[4,256,384]{2,1,0:T(8,128)(2,1)S(1)}, bf16[4,256,384]{2,1,0:T(8,128)(2,1)S(1)}, u32[]{:S(2)}, u32[]{:S(2)}) collective-permute-start(bf16[4,256,384]{2,1,0:T(8,128)(2,1)S(1)} %collective-permute-done.9.refs_10_), channel_id=1, source_target_pairs={{0,32},{1,33},{2,34},{3,35},{4,36},{5,37},{6,38},{7,39},{8,104},{9... | collective-permute-start | bytes 2359304 | tf_op jit(solution)/shard_map/ppermute | solution.py:29
  68.9 1.8 %collective-permute-start.5 = (bf16[4,256,384]{2,1,0:T(8,128)(2,1)S(1)}, bf16[4,256,384]{2,1,0:T(8,128)(2,1)S(1)}, u32[]{:S(2)}, u32[]{:S(2)}) collective-permute-start(bf16[4,256,384]{2,1,0:T(8,128)(2,1)S(1)} %collective-permute-done.3.refs_4_), channel_id=1, source_target_pairs={{0,32},{1,33},{2,34},{3,35},{4,36},{5,37},{6,38},{7,39},{8,104},{9... | collective-permute-start | bytes 2359304 | tf_op jit(solution)/shard_map/ppermute | solution.py:29
  70.7 7.6 %collective-permute-done.11.refs_12_ = bf16[4,256,384]{2,1,0:T(8,128)(2,1)S(1)} collective-permute-done((bf16[4,256,384]{2,1,0:T(8,128)(2,1)S(1)}, bf16[4,256,384]{2,1,0:T(8,128)(2,1)S(1)}, u32[]{:S(2)}, u32[]{:S(2)}) %collective-permute-start.11) | collective-permute-done | bytes 786464 | tf_op jit(solution)/shard_map/ppermute | solution.py:29
  78.3 0.1 collective-permute-start.19
  78.4 1.3 collective-permute-start.27
  79.7 3.1 %collective-permute-start.24 = (bf16[4,272,384]{2,1,0:T(8,128)(2,1)S(1)}, bf16[4,272,384]{2,1,0:T(8,128)(2,1)S(1)}, u32[]{:S(2)}, u32[]{:S(2)}) collective-permute-start(bf16[4,272,384]{2,1,0:T(8,128)(2,1)S(1)} %collective-permute-done.23.refs_24_), channel_id=1, source_target_pairs={{0,8},{1,9},{2,10},{3,11},{4,12},{5,13},{6,14},{7,15},{8,0},{9,1},... | collective-permute-start | bytes 2506760 | tf_op jit(solution)/shard_map/ppermute | solution.py:29
  82.8 4.1 %collective-permute-done.5.refs_6_ = bf16[4,256,384]{2,1,0:T(8,128)(2,1)S(1)} collective-permute-done((bf16[4,256,384]{2,1,0:T(8,128)(2,1)S(1)}, bf16[4,256,384]{2,1,0:T(8,128)(2,1)S(1)}, u32[]{:S(2)}, u32[]{:S(2)}) %collective-permute-start.5) | collective-permute-done | bytes 786464 | tf_op jit(solution)/shard_map/ppermute | solution.py:29
  86.9 2.9 %collective-permute-start.13 = (bf16[4,256,384]{2,1,0:T(8,128)(2,1)S(1)}, bf16[4,256,384]{2,1,0:T(8,128)(2,1)}, u32[]{:S(2)}, u32[]{:S(2)}) collective-permute-start(bf16[4,256,384]{2,1,0:T(8,128)(2,1)S(1)} %collective-permute-done.11.refs_12_), channel_id=1, source_target_pairs={{0,32},{1,33},{2,34},{3,35},{4,36},{5,37},{6,38},{7,39},{8,104},{9... | collective-permute-start | bytes 2359304 | tf_op jit(solution)/shard_map/ppermute | solution.py:29
  89.8 0.3 collective-permute-done.19.refs_20_
  90.1 1.0 collective-permute-start.21
  91.1 8.0 %collective-permute-done.27.refs_28_ = bf16[4,272,384]{2,1,0:T(8,128)(2,1)} collective-permute-done((bf16[4,272,384]{2,1,0:T(8,128)(2,1)S(1)}, bf16[4,272,384]{2,1,0:T(8,128)(2,1)}, u32[]{:S(2)}, u32[]{:S(2)}) %collective-permute-start.27) | collective-permute-done | bytes 835616 | tf_op jit(solution)/shard_map/ppermute | solution.py:29
  99.0 1.3 collective-permute-start.29
  100.3 1.9 %collective-permute-start.12 = (bf16[4,256,384]{2,1,0:T(8,128)(2,1)S(1)}, bf16[4,256,384]{2,1,0:T(8,128)(2,1)S(1)}, u32[]{:S(2)}, u32[]{:S(2)}) collective-permute-start(bf16[4,256,384]{2,1,0:T(8,128)(2,1)S(1)} %collective-permute-done.11.refs_12_), channel_id=1, source_target_pairs={{0,8},{1,9},{2,10},{3,11},{4,12},{5,13},{6,14},{7,15},{8,0},{9,1},... | collective-permute-start | bytes 2359304 | tf_op jit(solution)/shard_map/ppermute | solution.py:29
  102.2 0.1 collective-permute-start.6
  102.4 0.5 collective-permute-start.26
  102.8 1.3 collective-permute-done.12.refs_13_
  104.1 0.4 collective-permute-start.20
  104.5 0.7 collective-permute-done.6.refs_7_
  105.3 0.4 collective-permute-start.28
  105.6 2.3 %collective-permute-done.21.refs_22_ = bf16[4,272,384]{2,1,0:T(8,128)(2,1)} collective-permute-done((bf16[4,272,384]{2,1,0:T(8,128)(2,1)}, bf16[4,272,384]{2,1,0:T(8,128)(2,1)}, u32[]{:S(2)}, u32[]{:S(2)}) %collective-permute-start.21) | collective-permute-done | bytes 835616 | tf_op jit(solution)/shard_map/ppermute | solution.py:29
  108.0 1.8 %collective-permute-start.22 = (bf16[4,272,384]{2,1,0:T(8,128)(2,1)}, bf16[4,272,384]{2,1,0:T(8,128)(2,1)}, u32[]{:S(2)}, u32[]{:S(2)}) collective-permute-start(bf16[4,272,384]{2,1,0:T(8,128)(2,1)} %collective-permute-done.21.refs_22_), channel_id=1, source_target_pairs={{0,8},{1,9},{2,10},{3,11},{4,12},{5,13},{6,14},{7,15},{8,0},{9,1},... | collective-permute-start | bytes 2506760 | tf_op jit(solution)/shard_map/ppermute | solution.py:29
  109.8 7.1 %collective-permute-done.29.refs_30_ = bf16[4,272,384]{2,1,0:T(8,128)(2,1)} collective-permute-done((bf16[4,272,384]{2,1,0:T(8,128)(2,1)}, bf16[4,272,384]{2,1,0:T(8,128)(2,1)}, u32[]{:S(2)}, u32[]{:S(2)}) %collective-permute-start.29) | collective-permute-done | bytes 835616 | tf_op jit(solution)/shard_map/ppermute | solution.py:29
  116.9 1.8 %collective-permute-start.30 = (bf16[4,272,384]{2,1,0:T(8,128)(2,1)}, bf16[4,272,384]{2,1,0:T(8,128)(2,1)}, u32[]{:S(2)}, u32[]{:S(2)}) collective-permute-start(bf16[4,272,384]{2,1,0:T(8,128)(2,1)} %collective-permute-done.29.refs_30_), channel_id=1, source_target_pairs={{0,8},{1,9},{2,10},{3,11},{4,12},{5,13},{6,14},{7,15},{8,0},{9,1},... | collective-permute-start | bytes 2506760 | tf_op jit(solution)/shard_map/ppermute | solution.py:29
  118.8 0.1 collective-permute-start.14
  118.9 0.8 copy-done.8
  119.7 0.1 stack.135
  119.8 0.1 stack.118
  119.9 0.1 select_reduce_fusion
  120.1 0.1 slice_reduce_fusion
  120.2 2.0 %collective-permute-done.14.refs_15_ = bf16[4,256,384]{2,1,0:T(8,128)(2,1)} collective-permute-done((bf16[4,256,384]{2,1,0:T(8,128)(2,1)}, bf16[4,256,384]{2,1,0:T(8,128)(2,1)}, u32[]{:S(2)}, u32[]{:S(2)}) %collective-permute-start.14) | collective-permute-done | bytes 786464 | tf_op jit(solution)/shard_map/ppermute | solution.py:29
  122.3 23.8 %shard_map.55 = f32[3,4,256,128]{3,2,1,0:T(8,128)} custom-call(s32[3]{0:T(128)S(1)} %and_select_fusion.shift, s32[33]{0:T(128)S(1)} %pad_add_fusion.source, bf16[4,256,384]{2,1,0:T(8,128)(2,1)} %copy-done, bf16[4,256,384]{2,1,0:T(8,128)(2,1)} %copy-done.11, bf16[4,256,384]{2,1,0:T(8,128)(2,1)} %copy-done.10, bf16[4,256,384]{2,1,0:T(8,128)(2,1)} %copy-done.14, ...), custom_call_target="tpu_custom_call" | custom-call | tf_op jit(solution)/shard_map/pallas_call | solution.py:109
  (75 shorter events, 0.3 us)
Async XLA Ops:
  2.1 20.8 %collective-permute-start.7 = (bf16[4,256,384]{2,1,0:T(8,128)(2,1)S(1)}, bf16[4,256,384]{2,1,0:T(8,128)(2,1)S(1)}, u32[]{:S(2)}, u32[]{:S(2)}) collective-permute-start(bf16[4,256,384]{2,1,0:T(8,128)(2,1)S(1)} %constant_dynamic-update-slice_fusion.refs_0_), channel_id=1, source_target_pairs={{0,16},{1,17},{2,18},{3,19},{4,20},{5,21},{6,22},{7,23},{8,24},{9,... | collective-permute-start | bytes 2359304 | tf_op jit(solution)/shard_map/ppermute | solution.py:29
  6.0 114.1 %copy-start.22 = (s32[3,64]{1,0:T(4,128)S(1)}, s32[3,64]{1,0:T(4,128)}, u32[]{:S(2)}) copy-start(s32[3,64]{1,0:T(4,128)} %param.9) | copy-start | bytes 2308
  6.2 35.2 %collective-permute-start.15 = (bf16[4,272,384]{2,1,0:T(8,128)(2,1)S(1)}, bf16[4,272,384]{2,1,0:T(8,128)(2,1)S(1)}, u32[]{:S(2)}, u32[]{:S(2)}) collective-permute-start(bf16[4,272,384]{2,1,0:T(8,128)(2,1)S(1)} %pad_maximum_fusion), channel_id=1, source_target_pairs={{0,0},{1,16},{2,34},{3,50},{4,68},{5,84},{6,102},{7,118},{8,8},{9,... | collective-permute-start | bytes 2506760 | tf_op jit(solution)/shard_map/ppermute | solution.py:29
  6.9 36.3 %collective-permute-start.1 = (bf16[4,256,384]{2,1,0:T(8,128)(2,1)S(1)}, bf16[4,256,384]{2,1,0:T(8,128)(2,1)S(1)}, u32[]{:S(2)}, u32[]{:S(2)}) collective-permute-start(bf16[4,256,384]{2,1,0:T(8,128)(2,1)S(1)} %constant_dynamic-update-slice_fusion.refs_0_), channel_id=1, source_target_pairs={{0,32},{1,33},{2,34},{3,35},{4,36},{5,37},{6,38},{7,39},{8,104},{9... | collective-permute-start | bytes 2359304 | tf_op jit(solution)/shard_map/ppermute | solution.py:29
  13.0 35.2 %collective-permute-start = (bf16[4,256,384]{2,1,0:T(8,128)(2,1)S(1)}, bf16[4,256,384]{2,1,0:T(8,128)(2,1)S(1)}, u32[]{:S(2)}, u32[]{:S(2)}) collective-permute-start(bf16[4,256,384]{2,1,0:T(8,128)(2,1)S(1)} %constant_dynamic-update-slice_fusion.refs_0_), channel_id=1, source_target_pairs={{0,8},{1,9},{2,10},{3,11},{4,12},{5,13},{6,14},{7,15},{8,0},{9,1},... | collective-permute-start | bytes 2359304 | tf_op jit(solution)/shard_map/ppermute | solution.py:29
  22.9 95.9 %copy-start.9 = (bf16[4,256,384]{2,1,0:T(8,128)(2,1)}, bf16[4,256,384]{2,1,0:T(8,128)(2,1)S(1)}, u32[]{:S(2)}) copy-start(bf16[4,256,384]{2,1,0:T(8,128)(2,1)S(1)} %collective-permute-done.7.refs_8_) | copy-start | bytes 2359300
  22.9 27.0 %collective-permute-start.9 = (bf16[4,256,384]{2,1,0:T(8,128)(2,1)S(1)}, bf16[4,256,384]{2,1,0:T(8,128)(2,1)S(1)}, u32[]{:S(2)}, u32[]{:S(2)}) collective-permute-start(bf16[4,256,384]{2,1,0:T(8,128)(2,1)S(1)} %collective-permute-done.7.refs_8_), channel_id=1, source_target_pairs={{0,32},{1,33},{2,34},{3,35},{4,36},{5,37},{6,38},{7,39},{8,104},{9... | collective-permute-start | bytes 2359304 | tf_op jit(solution)/shard_map/ppermute | solution.py:29
  38.3 13.0 %collective-permute-start.8 = (bf16[4,256,384]{2,1,0:T(8,128)(2,1)S(1)}, bf16[4,256,384]{2,1,0:T(8,128)(2,1)}, u32[]{:S(2)}, u32[]{:S(2)}) collective-permute-start(bf16[4,256,384]{2,1,0:T(8,128)(2,1)S(1)} %collective-permute-done.7.refs_8_), channel_id=1, source_target_pairs={{0,8},{1,9},{2,10},{3,11},{4,12},{5,13},{6,14},{7,15},{8,0},{9,1},... | collective-permute-start | bytes 2359304 | tf_op jit(solution)/shard_map/ppermute | solution.py:29
  41.4 80.9 %copy-start.1 = (bf16[4,272,384]{2,1,0:T(8,128)(2,1)}, bf16[4,272,384]{2,1,0:T(8,128)(2,1)S(1)}, u32[]{:S(2)}) copy-start(bf16[4,272,384]{2,1,0:T(8,128)(2,1)S(1)} %collective-permute-done.15.refs_16_) | copy-start | bytes 2506756
  41.4 20.4 %collective-permute-start.23 = (bf16[4,272,384]{2,1,0:T(8,128)(2,1)S(1)}, bf16[4,272,384]{2,1,0:T(8,128)(2,1)S(1)}, u32[]{:S(2)}, u32[]{:S(2)}) collective-permute-start(bf16[4,272,384]{2,1,0:T(8,128)(2,1)S(1)} %collective-permute-done.15.refs_16_), channel_id=1, source_target_pairs={{0,1},{1,0},{2,3},{3,2},{4,5},{5,4},{6,7},{7,6},{8,9},{9,8},{10,11... | collective-permute-start | bytes 2506760 | tf_op jit(solution)/shard_map/ppermute | solution.py:29
  43.2 36.5 %copy-start.10 = (bf16[4,256,384]{2,1,0:T(8,128)(2,1)}, bf16[4,256,384]{2,1,0:T(8,128)(2,1)S(1)}, u32[]{:S(2)}) copy-start(bf16[4,256,384]{2,1,0:T(8,128)(2,1)S(1)} %collective-permute-done.1.refs_2_) | copy-start | bytes 2359300
  43.2 25.6 %collective-permute-start.17 = (bf16[4,272,384]{2,1,0:T(8,128)(2,1)S(1)}, bf16[4,272,384]{2,1,0:T(8,128)(2,1)S(1)}, u32[]{:S(2)}, u32[]{:S(2)}) collective-permute-start(bf16[4,272,384]{2,1,0:T(8,128)(2,1)S(1)} %collective-permute-done.15.refs_16_), channel_id=1, source_target_pairs={{0,2},{1,3},{2,4},{3,5},{4,6},{5,7},{6,0},{7,1},{8,14},{9,15},{10,... | collective-permute-start | bytes 2506760 | tf_op jit(solution)/shard_map/ppermute | solution.py:29
  48.2 18.6 %collective-permute-start.3 = (bf16[4,256,384]{2,1,0:T(8,128)(2,1)S(1)}, bf16[4,256,384]{2,1,0:T(8,128)(2,1)S(1)}, u32[]{:S(2)}, u32[]{:S(2)}) collective-permute-start(bf16[4,256,384]{2,1,0:T(8,128)(2,1)S(1)} %collective-permute-done.1.refs_2_), channel_id=1, source_target_pairs={{0,32},{1,33},{2,34},{3,35},{4,36},{5,37},{6,38},{7,39},{8,104},{9... | collective-permute-start | bytes 2359304 | tf_op jit(solution)/shard_map/ppermute | solution.py:29
  50.0 29.7 %copy-start.12 = (bf16[4,256,384]{2,1,0:T(8,128)(2,1)}, bf16[4,256,384]{2,1,0:T(8,128)(2,1)S(1)}, u32[]{:S(2)}) copy-start(bf16[4,256,384]{2,1,0:T(8,128)(2,1)S(1)} %collective-permute-done.9.refs_10_) | copy-start | bytes 2359300
  50.0 18.8 %collective-permute-start.2 = (bf16[4,256,384]{2,1,0:T(8,128)(2,1)S(1)}, bf16[4,256,384]{2,1,0:T(8,128)(2,1)S(1)}, u32[]{:S(2)}, u32[]{:S(2)}) collective-permute-start(bf16[4,256,384]{2,1,0:T(8,128)(2,1)S(1)} %collective-permute-done.1.refs_2_), channel_id=1, source_target_pairs={{0,8},{1,9},{2,10},{3,11},{4,12},{5,13},{6,14},{7,15},{8,0},{9,1},... | collective-permute-start | bytes 2359304 | tf_op jit(solution)/shard_map/ppermute | solution.py:29
  51.3 19.4 %collective-permute-start.16 = (bf16[4,272,384]{2,1,0:T(8,128)(2,1)S(1)}, bf16[4,272,384]{2,1,0:T(8,128)(2,1)S(1)}, u32[]{:S(2)}, u32[]{:S(2)}) collective-permute-start(bf16[4,272,384]{2,1,0:T(8,128)(2,1)S(1)} %collective-permute-done.15.refs_16_), channel_id=1, source_target_pairs={{0,8},{1,9},{2,10},{3,11},{4,12},{5,13},{6,14},{7,15},{8,0},{9,1},... | collective-permute-start | bytes 2506760 | tf_op jit(solution)/shard_map/ppermute | solution.py:29
  61.7 60.5 %copy-start.2 = (bf16[4,272,384]{2,1,0:T(8,128)(2,1)}, bf16[4,272,384]{2,1,0:T(8,128)(2,1)S(1)}, u32[]{:S(2)}) copy-start(bf16[4,272,384]{2,1,0:T(8,128)(2,1)S(1)} %collective-permute-done.23.refs_24_) | copy-start | bytes 2506756
  61.7 16.7 %collective-permute-start.25 = (bf16[4,272,384]{2,1,0:T(8,128)(2,1)S(1)}, bf16[4,272,384]{2,1,0:T(8,128)(2,1)S(1)}, u32[]{:S(2)}, u32[]{:S(2)}) collective-permute-start(bf16[4,272,384]{2,1,0:T(8,128)(2,1)S(1)} %collective-permute-done.23.refs_24_), channel_id=1, source_target_pairs={{0,2},{1,3},{2,4},{3,5},{4,6},{5,7},{6,0},{7,1},{8,14},{9,15},{10,... | collective-permute-start | bytes 2506760 | tf_op jit(solution)/shard_map/ppermute | solution.py:29
  66.8 55.4 %copy-start.13 = (bf16[4,256,384]{2,1,0:T(8,128)(2,1)}, bf16[4,256,384]{2,1,0:T(8,128)(2,1)S(1)}, u32[]{:S(2)}) copy-start(bf16[4,256,384]{2,1,0:T(8,128)(2,1)S(1)} %collective-permute-done.3.refs_4_) | copy-start | bytes 2359300
  66.8 11.5 %collective-permute-start.11 = (bf16[4,256,384]{2,1,0:T(8,128)(2,1)S(1)}, bf16[4,256,384]{2,1,0:T(8,128)(2,1)S(1)}, u32[]{:S(2)}, u32[]{:S(2)}) collective-permute-start(bf16[4,256,384]{2,1,0:T(8,128)(2,1)S(1)} %collective-permute-done.9.refs_10_), channel_id=1, source_target_pairs={{0,32},{1,33},{2,34},{3,35},{4,36},{5,37},{6,38},{7,39},{8,104},{9... | collective-permute-start | bytes 2359304 | tf_op jit(solution)/shard_map/ppermute | solution.py:29
  68.8 10.9 %collective-permute-start.10 = (bf16[4,256,384]{2,1,0:T(8,128)(2,1)S(1)}, bf16[4,256,384]{2,1,0:T(8,128)(2,1)S(1)}, u32[]{:S(2)}, u32[]{:S(2)}) collective-permute-start(bf16[4,256,384]{2,1,0:T(8,128)(2,1)S(1)} %collective-permute-done.9.refs_10_), channel_id=1, source_target_pairs={{0,8},{1,9},{2,10},{3,11},{4,12},{5,13},{6,14},{7,15},{8,0},{9,1},... | collective-permute-start | bytes 2359304 | tf_op jit(solution)/shard_map/ppermute | solution.py:29
  68.8 53.4 %copy-start.3 = (bf16[4,272,384]{2,1,0:T(8,128)(2,1)}, bf16[4,272,384]{2,1,0:T(8,128)(2,1)S(1)}, u32[]{:S(2)}) copy-start(bf16[4,272,384]{2,1,0:T(8,128)(2,1)S(1)} %collective-permute-done.17.refs_18_) | copy-start | bytes 2506756
  68.9 18.0 %collective-permute-start.5 = (bf16[4,256,384]{2,1,0:T(8,128)(2,1)S(1)}, bf16[4,256,384]{2,1,0:T(8,128)(2,1)S(1)}, u32[]{:S(2)}, u32[]{:S(2)}) collective-permute-start(bf16[4,256,384]{2,1,0:T(8,128)(2,1)S(1)} %collective-permute-done.3.refs_4_), channel_id=1, source_target_pairs={{0,32},{1,33},{2,34},{3,35},{4,36},{5,37},{6,38},{7,39},{8,104},{9... | collective-permute-start | bytes 2359304 | tf_op jit(solution)/shard_map/ppermute | solution.py:29
  70.7 31.6 %copy-start.4 = (bf16[4,272,384]{2,1,0:T(8,128)(2,1)}, bf16[4,272,384]{2,1,0:T(8,128)(2,1)S(1)}, u32[]{:S(2)}) copy-start(bf16[4,272,384]{2,1,0:T(8,128)(2,1)S(1)} %collective-permute-done.16.refs_17_) | copy-start | bytes 2506756
  70.7 16.2 %collective-permute-start.4 = (bf16[4,256,384]{2,1,0:T(8,128)(2,1)S(1)}, bf16[4,256,384]{2,1,0:T(8,128)(2,1)S(1)}, u32[]{:S(2)}, u32[]{:S(2)}) collective-permute-start(bf16[4,256,384]{2,1,0:T(8,128)(2,1)S(1)} %collective-permute-done.3.refs_4_), channel_id=1, source_target_pairs={{0,8},{1,9},{2,10},{3,11},{4,12},{5,13},{6,14},{7,15},{8,0},{9,1},... | collective-permute-start | bytes 2359304 | tf_op jit(solution)/shard_map/ppermute | solution.py:29
  78.3 40.6 %copy-start.15 = (bf16[4,256,384]{2,1,0:T(8,128)(2,1)}, bf16[4,256,384]{2,1,0:T(8,128)(2,1)S(1)}, u32[]{:S(2)}) copy-start(bf16[4,256,384]{2,1,0:T(8,128)(2,1)S(1)} %collective-permute-done.11.refs_12_) | copy-start | bytes 2359300
  78.3 11.8 %collective-permute-start.19 = (bf16[4,272,384]{2,1,0:T(8,128)(2,1)S(1)}, bf16[4,272,384]{2,1,0:T(8,128)(2,1)}, u32[]{:S(2)}, u32[]{:S(2)}) collective-permute-start(bf16[4,272,384]{2,1,0:T(8,128)(2,1)S(1)} %collective-permute-done.17.refs_18_), channel_id=1, source_target_pairs={{0,2},{1,3},{2,4},{3,5},{4,6},{5,7},{6,0},{7,1},{8,14},{9,15},{10,... | collective-permute-start | bytes 2506760 | tf_op jit(solution)/shard_map/ppermute | solution.py:29
  78.4 24.0 %copy-start.5 = (bf16[4,272,384]{2,1,0:T(8,128)(2,1)}, bf16[4,272,384]{2,1,0:T(8,128)(2,1)S(1)}, u32[]{:S(2)}) copy-start(bf16[4,272,384]{2,1,0:T(8,128)(2,1)S(1)} %collective-permute-done.25.refs_26_) | copy-start | bytes 2506756
  78.4 20.6 %collective-permute-start.27 = (bf16[4,272,384]{2,1,0:T(8,128)(2,1)S(1)}, bf16[4,272,384]{2,1,0:T(8,128)(2,1)}, u32[]{:S(2)}, u32[]{:S(2)}) collective-permute-start(bf16[4,272,384]{2,1,0:T(8,128)(2,1)S(1)} %collective-permute-done.25.refs_26_), channel_id=1, source_target_pairs={{0,2},{1,3},{2,4},{3,5},{4,6},{5,7},{6,0},{7,1},{8,14},{9,15},{10,... | collective-permute-start | bytes 2506760 | tf_op jit(solution)/shard_map/ppermute | solution.py:29
  79.7 39.2 %copy-start.16 = (bf16[4,256,384]{2,1,0:T(8,128)(2,1)}, bf16[4,256,384]{2,1,0:T(8,128)(2,1)S(1)}, u32[]{:S(2)}) copy-start(bf16[4,256,384]{2,1,0:T(8,128)(2,1)S(1)} %collective-permute-done.10.refs_11_) | copy-start | bytes 2359300
  79.7 20.6 %collective-permute-start.24 = (bf16[4,272,384]{2,1,0:T(8,128)(2,1)S(1)}, bf16[4,272,384]{2,1,0:T(8,128)(2,1)S(1)}, u32[]{:S(2)}, u32[]{:S(2)}) collective-permute-start(bf16[4,272,384]{2,1,0:T(8,128)(2,1)S(1)} %collective-permute-done.23.refs_24_), channel_id=1, source_target_pairs={{0,8},{1,9},{2,10},{3,11},{4,12},{5,13},{6,14},{7,15},{8,0},{9,1},... | collective-permute-start | bytes 2506760 | tf_op jit(solution)/shard_map/ppermute | solution.py:29
  86.8 32.1 %copy-start.17 = (bf16[4,256,384]{2,1,0:T(8,128)(2,1)}, bf16[4,256,384]{2,1,0:T(8,128)(2,1)S(1)}, u32[]{:S(2)}) copy-start(bf16[4,256,384]{2,1,0:T(8,128)(2,1)S(1)} %collective-permute-done.5.refs_6_) | copy-start | bytes 2359300
  86.8 15.4 %collective-permute-start.18 = (bf16[4,272,384]{2,1,0:T(8,128)(2,1)S(1)}, bf16[4,272,384]{2,1,0:T(8,128)(2,1)S(1)}, u32[]{:S(2)}, u32[]{:S(2)}) collective-permute-start(bf16[4,272,384]{2,1,0:T(8,128)(2,1)S(1)} %collective-permute-done.17.refs_18_), channel_id=1, source_target_pairs={{0,8},{1,9},{2,10},{3,11},{4,12},{5,13},{6,14},{7,15},{8,0},{9,1},... | collective-permute-start | bytes 2506760 | tf_op jit(solution)/shard_map/ppermute | solution.py:29
  86.8 32.1 %copy-start.18 = (bf16[4,256,384]{2,1,0:T(8,128)(2,1)}, bf16[4,256,384]{2,1,0:T(8,128)(2,1)S(1)}, u32[]{:S(2)}) copy-start(bf16[4,256,384]{2,1,0:T(8,128)(2,1)S(1)} %collective-permute-done.4.refs_5_) | copy-start | bytes 2359300
  86.9 15.5 %collective-permute-start.13 = (bf16[4,256,384]{2,1,0:T(8,128)(2,1)S(1)}, bf16[4,256,384]{2,1,0:T(8,128)(2,1)}, u32[]{:S(2)}, u32[]{:S(2)}) collective-permute-start(bf16[4,256,384]{2,1,0:T(8,128)(2,1)S(1)} %collective-permute-done.11.refs_12_), channel_id=1, source_target_pairs={{0,32},{1,33},{2,34},{3,35},{4,36},{5,37},{6,38},{7,39},{8,104},{9... | collective-permute-start | bytes 2359304 | tf_op jit(solution)/shard_map/ppermute | solution.py:29
  90.1 17.9 %collective-permute-start.21 = (bf16[4,272,384]{2,1,0:T(8,128)(2,1)}, bf16[4,272,384]{2,1,0:T(8,128)(2,1)}, u32[]{:S(2)}, u32[]{:S(2)}) collective-permute-start(bf16[4,272,384]{2,1,0:T(8,128)(2,1)} %collective-permute-done.19.refs_20_), channel_id=1, source_target_pairs={{0,2},{1,3},{2,4},{3,5},{4,6},{5,7},{6,0},{7,1},{8,14},{9,15},{10,... | collective-permute-start | bytes 2506760 | tf_op jit(solution)/shard_map/ppermute | solution.py:29
  99.0 17.9 %collective-permute-start.29 = (bf16[4,272,384]{2,1,0:T(8,128)(2,1)}, bf16[4,272,384]{2,1,0:T(8,128)(2,1)}, u32[]{:S(2)}, u32[]{:S(2)}) collective-permute-start(bf16[4,272,384]{2,1,0:T(8,128)(2,1)} %collective-permute-done.27.refs_28_), channel_id=1, source_target_pairs={{0,2},{1,3},{2,4},{3,5},{4,6},{5,7},{6,0},{7,1},{8,14},{9,15},{10,... | collective-permute-start | bytes 2506760 | tf_op jit(solution)/shard_map/ppermute | solution.py:29
  100.3 18.4 %copy-start.6 = (bf16[4,272,384]{2,1,0:T(8,128)(2,1)}, bf16[4,272,384]{2,1,0:T(8,128)(2,1)S(1)}, u32[]{:S(2)}) copy-start(bf16[4,272,384]{2,1,0:T(8,128)(2,1)S(1)} %collective-permute-done.24.refs_25_) | copy-start | bytes 2506756
  100.3 3.8 %collective-permute-start.12 = (bf16[4,256,384]{2,1,0:T(8,128)(2,1)S(1)}, bf16[4,256,384]{2,1,0:T(8,128)(2,1)S(1)}, u32[]{:S(2)}, u32[]{:S(2)}) collective-permute-start(bf16[4,256,384]{2,1,0:T(8,128)(2,1)S(1)} %collective-permute-done.11.refs_12_), channel_id=1, source_target_pairs={{0,8},{1,9},{2,10},{3,11},{4,12},{5,13},{6,14},{7,15},{8,0},{9,1},... | collective-permute-start | bytes 2359304 | tf_op jit(solution)/shard_map/ppermute | solution.py:29
  102.2 16.7 %copy-start.7 = (bf16[4,272,384]{2,1,0:T(8,128)(2,1)}, bf16[4,272,384]{2,1,0:T(8,128)(2,1)S(1)}, u32[]{:S(2)}) copy-start(bf16[4,272,384]{2,1,0:T(8,128)(2,1)S(1)} %collective-permute-done.18.refs_19_) | copy-start | bytes 2506756
  102.2 3.0 %collective-permute-start.6 = (bf16[4,256,384]{2,1,0:T(8,128)(2,1)S(1)}, bf16[4,256,384]{2,1,0:T(8,128)(2,1)S(1)}, u32[]{:S(2)}, u32[]{:S(2)}) collective-permute-start(bf16[4,256,384]{2,1,0:T(8,128)(2,1)S(1)} %collective-permute-done.5.refs_6_), channel_id=1, source_target_pairs={{0,8},{1,9},{2,10},{3,11},{4,12},{5,13},{6,14},{7,15},{8,0},{9,1},... | collective-permute-start | bytes 2359304 | tf_op jit(solution)/shard_map/ppermute | solution.py:29
  102.4 16.4 %collective-permute-start.26 = (bf16[4,272,384]{2,1,0:T(8,128)(2,1)S(1)}, bf16[4,272,384]{2,1,0:T(8,128)(2,1)S(1)}, u32[]{:S(2)}, u32[]{:S(2)}) collective-permute-start(bf16[4,272,384]{2,1,0:T(8,128)(2,1)S(1)} %collective-permute-done.25.refs_26_), channel_id=1, source_target_pairs={{0,8},{1,9},{2,10},{3,11},{4,12},{5,13},{6,14},{7,15},{8,0},{9,1},... | collective-permute-start | bytes 2506760 | tf_op jit(solution)/shard_map/ppermute | solution.py:29
  104.1 14.8 %copy-start.19 = (bf16[4,256,384]{2,1,0:T(8,128)(2,1)}, bf16[4,256,384]{2,1,0:T(8,128)(2,1)S(1)}, u32[]{:S(2)}) copy-start(bf16[4,256,384]{2,1,0:T(8,128)(2,1)S(1)} %collective-permute-done.12.refs_13_) | copy-start | bytes 2359300
  104.1 16.1 %collective-permute-start.20 = (bf16[4,272,384]{2,1,0:T(8,128)(2,1)}, bf16[4,272,384]{2,1,0:T(8,128)(2,1)}, u32[]{:S(2)}, u32[]{:S(2)}) collective-permute-start(bf16[4,272,384]{2,1,0:T(8,128)(2,1)} %collective-permute-done.19.refs_20_), channel_id=1, source_target_pairs={{0,8},{1,9},{2,10},{3,11},{4,12},{5,13},{6,14},{7,15},{8,0},{9,1},... | collective-permute-start | bytes 2506760 | tf_op jit(solution)/shard_map/ppermute | solution.py:29
  105.3 16.9 %collective-permute-start.28 = (bf16[4,272,384]{2,1,0:T(8,128)(2,1)}, bf16[4,272,384]{2,1,0:T(8,128)(2,1)}, u32[]{:S(2)}, u32[]{:S(2)}) collective-permute-start(bf16[4,272,384]{2,1,0:T(8,128)(2,1)} %collective-permute-done.27.refs_28_), channel_id=1, source_target_pairs={{0,8},{1,9},{2,10},{3,11},{4,12},{5,13},{6,14},{7,15},{8,0},{9,1},... | collective-permute-start | bytes 2506760 | tf_op jit(solution)/shard_map/ppermute | solution.py:29
  108.0 14.2 %collective-permute-start.22 = (bf16[4,272,384]{2,1,0:T(8,128)(2,1)}, bf16[4,272,384]{2,1,0:T(8,128)(2,1)}, u32[]{:S(2)}, u32[]{:S(2)}) collective-permute-start(bf16[4,272,384]{2,1,0:T(8,128)(2,1)} %collective-permute-done.21.refs_22_), channel_id=1, source_target_pairs={{0,8},{1,9},{2,10},{3,11},{4,12},{5,13},{6,14},{7,15},{8,0},{9,1},... | collective-permute-start | bytes 2506760 | tf_op jit(solution)/shard_map/ppermute | solution.py:29
  116.9 5.3 %collective-permute-start.30 = (bf16[4,272,384]{2,1,0:T(8,128)(2,1)}, bf16[4,272,384]{2,1,0:T(8,128)(2,1)}, u32[]{:S(2)}, u32[]{:S(2)}) collective-permute-start(bf16[4,272,384]{2,1,0:T(8,128)(2,1)} %collective-permute-done.29.refs_30_), channel_id=1, source_target_pairs={{0,8},{1,9},{2,10},{3,11},{4,12},{5,13},{6,14},{7,15},{8,0},{9,1},... | collective-permute-start | bytes 2506760 | tf_op jit(solution)/shard_map/ppermute | solution.py:29
  118.8 3.4 %collective-permute-start.14 = (bf16[4,256,384]{2,1,0:T(8,128)(2,1)}, bf16[4,256,384]{2,1,0:T(8,128)(2,1)}, u32[]{:S(2)}, u32[]{:S(2)}) collective-permute-start(bf16[4,256,384]{2,1,0:T(8,128)(2,1)} %collective-permute-done.13.refs_14_), channel_id=1, source_target_pairs={{0,8},{1,9},{2,10},{3,11},{4,12},{5,13},{6,14},{7,15},{8,0},{9,1},... | collective-permute-start | bytes 2359304 | tf_op jit(solution)/shard_map/ppermute | solution.py:29
  (7 other events, 54.4 us)

commit v4 on v3

--- a/solution.py
+++ b/solution.py
@@ -30,20 +30,14 @@
 
 
 def kernel(shift, source, *refs):
-    row_src, col_src, refs = refs[:16], refs[16:32], refs[32:]
+    row_src, col_src, refs = refs[:16], refs[16:24], refs[24:]
     out, row_pts, col_pts, vbuf, obuf, acc, row_sems, col_sems = refs
-    core = source[32]
-    first = pl.multiple_of(core * 128, 128)
-    points = pl.ds(pl.multiple_of(core * 16, 16), 128)
-    levels = pl.ds((1 - core) * 128, 1)
 
     def row_copy(n, slot):
         return pltpu.make_async_copy(row_src[n], row_pts.at[slot], row_sems.at[slot])
 
     def col_copy(n, slot):
-        return pltpu.make_async_copy(
-            col_src[n].at[:, pl.ds(first, 144), :], col_pts.at[slot], col_sems.at[slot]
-        )
+        return pltpu.make_async_copy(col_src[n // 2].at[n % 2], col_pts.at[slot, pl.ds(0, 528)], col_sems.at[slot])
 
     def fetch(step):
         slab, slot = lax.rem(step + 15, 16), lax.rem(step, 3)
@@ -73,11 +67,12 @@
 
         row_copy(0, slot).wait()
         col_copy(0, slot).wait()
+        gaps = col_pts[slot, 512:528, :].astype(jnp.float32)
+        factors = [jnp.exp(-gaps * TAUS[t]) for t in range(NTAU)]
         for i in range(4):
-            col = col_pts[slot, i, points, :].astype(jnp.float32)
-            gap = col_pts[slot, i, levels, :].astype(jnp.float32)
+            col = col_pts[slot, i * 128 : (i + 1) * 128, :].astype(jnp.float32)
             panel = jnp.concatenate(
-                [(col * jnp.exp(-gap * TAUS[t])).astype(jnp.bfloat16) for t in range(NTAU)], 0
+                [(col * factors[t][i : i + 1]).astype(jnp.bfloat16) for t in range(NTAU)], 0
             )
             vbuf[par + i] = lax.dot_general(
                 panel[:, 128:], row_pts[slot, i, :, 128:], NT_DIMS, preferred_element_type=jnp.float32
@@ -108,11 +103,11 @@
     scalars = pl.BlockSpec(memory_space=pltpu.SMEM)
     return pl.pallas_call(
         kernel,
-        in_specs=[scalars, scalars] + [anywhere] * 32,
+        in_specs=[scalars, scalars] + [anywhere] * 24,
         out_specs=pl.BlockSpec(memory_space=pltpu.VMEM),
         scratch_shapes=[
             pltpu.VMEM((3, 4, 256, 384), jnp.bfloat16),
-            pltpu.VMEM((3, 4, 144, 384), jnp.bfloat16),
+            pltpu.VMEM((3, 576, 384), jnp.bfloat16),
             pltpu.VMEM((8, 512, 256), jnp.float32),
             pltpu.VMEM((4, 512, 256), jnp.float32),
             pltpu.VMEM((3, 512, 256), jnp.float32),
@@ -120,7 +115,7 @@
             pltpu.SemaphoreType.DMA((3,)),
         ],
         out_shape=jax.ShapeDtypeStruct((3, NTAU, 256, 128), jnp.float32),
-        compiler_params=pltpu.CompilerParams(vmem_limit_bytes=20 * 2**20),
+        compiler_params=pltpu.CompilerParams(vmem_limit_bytes=24 * 2**20),
     )(shift, source, *[pltpu.with_memory_space_constraint(p, pltpu.HBM) for p in pieces])
 
 
@@ -149,37 +144,45 @@
     shift = (-partner[:, 0]) % 64
     own = jnp.concatenate([occ_orbitals, virt_orbitals], axis=2)
     gaps = jnp.concatenate([occ_gap, virt_gap], axis=1)
-    gaps = jnp.broadcast_to(gaps[:, None, :], (4, 16, 384))
-    carried = jnp.concatenate([own[:, :128], gaps, own[:, 128:]], axis=1)
+    gaps = jnp.pad(gaps, ((0, 12), (0, 0)))
 
-    cols = send(carried, lambda z, yh, c, x, yl: (x, yl, c, x + z, yh))
+    def half(core):
+        cut = [lax.dynamic_slice_in_dim(a, core * 128, 128, 1) for a in (occ_orbitals, virt_orbitals)]
+        return jnp.concatenate([jnp.concatenate(cut, axis=2).reshape(512, 384), gaps])
+
+    here = send(half(c), lambda z, yh, c, x, yl: (x, yl, c, x + z, yh))
+    there = send(half(1 - c), lambda z, yh, c, x, yl: (x, yl, 1 - c, x + z, yh))
+    cols = jnp.stack([here, there])
     cols_same, rows_same = [cols], [own]
     cols_cross = [send(cols, lambda z, yh, c, x, yl: (z, yh, c, x, 1 - yl))]
     for _ in range(3):
         rows_same.append(z_step(rows_same[-1], 1))
         cols_same.append(x_step(cols_same[-1], 1))
-    rows_cross = [across_yh(own)]
-    cols_cross.append(x_step(cols_cross[0], 1))
+    rows_cross = [across_yh(after(own, cols_cross[0]))]
+    cols_cross.append(x_step(after(cols_cross[0], cols_same[1]), 1))
     rows_cross.append(z_step(rows_cross[0], 1))
     cols_cross += [x_step(cols_cross[1], 1)]
     cols_cross += [x_step(cols_cross[2], 1)]
     rows_cross += [z_step(rows_cross[1], 1)]
-    rows_cross += [z_step(rows_cross[2], 1)]
+    rows_cross += [across_yh(after(rows_same[3], rows_cross[0]))]
 
-    def placed(pieces, at, low):
-        found = []
-        for piece, offset in zip(pieces, range(4)):
-            for block, core in ((piece, c), (swap(piece), 1 - c)):
-                found.append((block, (at + (2 * core - 1) * offset) % 4 * 4 + low * 2 + core))
-        return found
+    def slab(at, low, core):
+        return at % 4 * 4 + low * 2 + core
 
-    pieces = placed(rows_same, z, yh) + placed(rows_cross, z, 1 - yh)
-    pieces += placed(cols_same, x - z, yl) + placed(cols_cross, x - z, 1 - yl)
-    slots = jnp.stack([slot for _, slot in pieces])
+    pieces, slots = [], []
+    for held, low in ((rows_same, yh), (rows_cross, 1 - yh)):
+        for step, piece in enumerate(held):
+            pieces += [piece, swap(piece)]
+            slots += [slab(z + (2 * core - 1) * step, low, core) for core in (c, 1 - c)]
+    for held, low in ((cols_same, yl), (cols_cross, 1 - yl)):
+        for step, piece in enumerate(held):
+            pieces.append(piece)
+            slots += [slab(x - z + (2 * c - 1) * step, low, core) for core in (c, 1 - c)]
+    slots = jnp.stack(slots)
     held = jnp.arange(16)
     source = [jnp.sum((part[:, None] == held) * held[:, None], axis=0) for part in (slots[:16], slots[16:])]
-    source = jnp.concatenate(source + [c[None]]).astype(jnp.int32)
-    return polarizability(shift, source, [block for block, _ in pieces])
+    source = jnp.concatenate(source).astype(jnp.int32)
+    return polarizability(shift, source, pieces)
 
 
 def solution(mesh):

time: 146 us -> 127 us (0.87)
  waiting for transfers between devices: 53.8 us -> 38.3 us
  starting transfers between devices: 64.6 us -> 60.9 us
    ppermute x31 -> x24, waiting for transfers between devices: 53.8 us -> 38.3 us  [send(): return lax.ppermute(block, AXES, routes(target))]
    ppermute x31 -> x24, starting transfers between devices: 64.6 us -> 60.9 us  [send(): return lax.ppermute(block, AXES, routes(target))]
    dynamic_slice x0 -> x2, local copies, waits for them, and re-layouts: none -> 2.09 us  [half(): lax.dynamic_slice_in_dim(a, core * 128, 128, 1)]
  transfers between devices with their start and end apart: 31 -> 24, of which waited for: 11 -> 9; matrix products, arithmetic and copies ran while one was open for 0% -> 0% of each run, Pallas kernels for 0% -> 0%
where the time goes in v4:
time: 127 us
  starting transfers between devices  60.9 us (48%)
  waiting for transfers between devices  38.3 us (30%)
  Pallas kernels  23.7 us (19%)
  local copies, waits for them, and re-layouts  3.44 us (3%)
    ppermute x24, starting transfers between devices, send(): return lax.ppermute(block, AXES, routes(target))  60.9 us
    ppermute x24, waiting for transfers between devices, send(): return lax.ppermute(block, AXES, routes(target))  38.3 us
    pallas_call x1, Pallas kernels, polarizability(): pl.pallas_call(kernel, in_specs=[scalars, scalars] + [anywhere] * 24, out...  23.7 us
  transfers between devices with their start and end apart: 24, of which 9 were waited for; matrix products, arithmetic and copies ran while one was open for 0% of the time, Pallas kernels for 0%

profile of v4, /device:TPU:1, one launch (start us, length us, event | category | flops | bytes accessed | tf_op | source)
XLA Modules:
  0.0 127.2 jit_solution(7154090885400666923)
XLA Ops:
  0.0 1.0 constant_dynamic-slice_fusion.3
  1.0 1.1 constant_dynamic-slice_fusion.2
  2.1 0.0 copy-start.3
  2.1 0.1 pad_maximum_fusion.3
  2.3 0.0 copy-start.1
  2.3 0.1 pad_maximum_fusion.2
  2.4 0.8 collective-permute-start.7
  3.2 1.5 %collective-permute-start.8 = (bf16[528,384]{1,0:T(8,128)(2,1)S(1)}, bf16[528,384]{1,0:T(8,128)(2,1)S(1)}, u32[]{:S(2)}, u32[]{:S(2)}) collective-permute-start(bf16[528,384]{1,0:T(8,128)(2,1)S(1)} %get-tuple-element.16), channel_id=1, source_target_pairs={{0,8},{1,24},{2,42},{3,58},{4,76},{5,92},{6,110},{7,126},{8,0},{9,... | collective-permute-start | bytes 1216520 | tf_op jit(solution)/shard_map/ppermute | solution.py:29
  4.7 1.3 %collective-permute-done.8 = bf16[528,384]{1,0:T(8,128)(2,1)S(1)} collective-permute-done((bf16[528,384]{1,0:T(8,128)(2,1)S(1)}, bf16[528,384]{1,0:T(8,128)(2,1)S(1)}, u32[]{:S(2)}, u32[]{:S(2)}) %collective-permute-start.8) | collective-permute-done | bytes 405536 | tf_op jit(solution)/shard_map/ppermute | solution.py:29
  6.1 0.1 pad_maximum_fusion.refs_16_
  6.2 24.8 %collective-permute-start.18 = (bf16[2,528,384]{2,1,0:T(8,128)(2,1)S(1)}, bf16[2,528,384]{2,1,0:T(8,128)(2,1)S(1)}, u32[]{:S(2)}, u32[]{:S(2)}) collective-permute-start(bf16[2,528,384]{2,1,0:T(8,128)(2,1)S(1)} %pad_maximum_fusion.refs_16_), channel_id=1, source_target_pairs={{0,2},{1,3},{2,4},{3,5},{4,6},{5,7},{6,0},{7,1},{8,14},{9,15},{10,... | collective-permute-start | bytes 2433032 | tf_op jit(solution)/shard_map/ppermute | solution.py:29
  31.0 2.2 %collective-permute-start.9 = (bf16[2,528,384]{2,1,0:T(8,128)(2,1)S(1)}, bf16[2,528,384]{2,1,0:T(8,128)(2,1)S(1)}, u32[]{:S(2)}, u32[]{:S(2)}) collective-permute-start(bf16[2,528,384]{2,1,0:T(8,128)(2,1)S(1)} %pad_maximum_fusion.refs_16_), channel_id=1, source_target_pairs={{0,1},{1,0},{2,3},{3,2},{4,5},{5,4},{6,7},{7,6},{8,9},{9,8},{10,11... | collective-permute-start | bytes 2433032 | tf_op jit(solution)/shard_map/ppermute | solution.py:29
  33.2 1.7 %collective-permute-start.1 = (bf16[4,256,384]{2,1,0:T(8,128)(2,1)S(1)}, bf16[4,256,384]{2,1,0:T(8,128)(2,1)S(1)}, u32[]{:S(2)}, u32[]{:S(2)}) collective-permute-start(bf16[4,256,384]{2,1,0:T(8,128)(2,1)S(1)} %constant_dynamic-update-slice_fusion.refs_0_), channel_id=1, source_target_pairs={{0,32},{1,33},{2,34},{3,35},{4,36},{5,37},{6,38},{7,39},{8,104},{9... | collective-permute-start | bytes 2359304 | tf_op jit(solution)/shard_map/ppermute | solution.py:29
  35.0 9.5 %collective-permute-done.1.refs_2_ = bf16[4,256,384]{2,1,0:T(8,128)(2,1)S(1)} collective-permute-done((bf16[4,256,384]{2,1,0:T(8,128)(2,1)S(1)}, bf16[4,256,384]{2,1,0:T(8,128)(2,1)S(1)}, u32[]{:S(2)}, u32[]{:S(2)}) %collective-permute-start.1) | collective-permute-done | bytes 786464 | tf_op jit(solution)/shard_map/ppermute | solution.py:29
  44.4 2.6 %collective-permute-start.3 = (bf16[4,256,384]{2,1,0:T(8,128)(2,1)S(1)}, bf16[4,256,384]{2,1,0:T(8,128)(2,1)S(1)}, u32[]{:S(2)}, u32[]{:S(2)}) collective-permute-start(bf16[4,256,384]{2,1,0:T(8,128)(2,1)S(1)} %collective-permute-done.1.refs_2_), channel_id=1, source_target_pairs={{0,32},{1,33},{2,34},{3,35},{4,36},{5,37},{6,38},{7,39},{8,104},{9... | collective-permute-start | bytes 2359304 | tf_op jit(solution)/shard_map/ppermute | solution.py:29
  47.0 0.1 collective-permute-start.19
  47.1 0.4 collective-permute-start
  47.5 0.3 collective-permute-done.9.refs_20_
  47.8 3.7 %collective-permute-start.10 = (bf16[4,256,384]{2,1,0:T(8,128)(2,1)S(1)}, bf16[4,256,384]{2,1,0:T(8,128)(2,1)S(1)}, u32[]{:S(2)}, u32[]{:S(2)}) collective-permute-start(bf16[4,256,384]{2,1,0:T(8,128)(2,1)S(1)} %constant_dynamic-update-slice_fusion.refs_0_), channel_id=1, source_target_pairs={{0,16},{1,17},{2,18},{3,19},{4,20},{5,21},{6,22},{7,23},{8,24},{9,... | collective-permute-start | bytes 2359304 | tf_op jit(solution)/shard_map/ppermute | solution.py:29
  51.5 3.5 %collective-permute-start.21 = (bf16[2,528,384]{2,1,0:T(8,128)(2,1)S(1)}, bf16[2,528,384]{2,1,0:T(8,128)(2,1)S(1)}, u32[]{:S(2)}, u32[]{:S(2)}) collective-permute-start(bf16[2,528,384]{2,1,0:T(8,128)(2,1)S(1)} %collective-permute-done.9.refs_20_), channel_id=1, source_target_pairs={{0,2},{1,3},{2,4},{3,5},{4,6},{5,7},{6,0},{7,1},{8,14},{9,15},{10,... | collective-permute-start | bytes 2433032 | tf_op jit(solution)/shard_map/ppermute | solution.py:29
  55.0 1.0 collective-permute-done.3.refs_4_
  56.0 3.4 %collective-permute-start.5 = (bf16[4,256,384]{2,1,0:T(8,128)(2,1)S(1)}, bf16[4,256,384]{2,1,0:T(8,128)(2,1)}, u32[]{:S(2)}, u32[]{:S(2)}) collective-permute-start(bf16[4,256,384]{2,1,0:T(8,128)(2,1)S(1)} %collective-permute-done.3.refs_4_), channel_id=1, source_target_pairs={{0,32},{1,33},{2,34},{3,35},{4,36},{5,37},{6,38},{7,39},{8,104},{9... | collective-permute-start | bytes 2359304 | tf_op jit(solution)/shard_map/ppermute | solution.py:29
  59.4 0.0 collective-permute-start.2
  59.4 9.5 %collective-permute-done.10.refs_8_ = bf16[4,256,384]{2,1,0:T(8,128)(2,1)S(1)} collective-permute-done((bf16[4,256,384]{2,1,0:T(8,128)(2,1)S(1)}, bf16[4,256,384]{2,1,0:T(8,128)(2,1)S(1)}, u32[]{:S(2)}, u32[]{:S(2)}) %collective-permute-start.10) | collective-permute-done | bytes 786464 | tf_op jit(solution)/shard_map/ppermute | solution.py:29
  68.9 0.3 collective-permute-start.4
  69.2 0.0 collective-permute-done.19.refs_18_
  69.2 5.7 %collective-permute-start.12 = (bf16[4,256,384]{2,1,0:T(8,128)(2,1)S(1)}, bf16[4,256,384]{2,1,0:T(8,128)(2,1)}, u32[]{:S(2)}, u32[]{:S(2)}) collective-permute-start(bf16[4,256,384]{2,1,0:T(8,128)(2,1)S(1)} %collective-permute-done.10.refs_8_), channel_id=1, source_target_pairs={{0,32},{1,33},{2,34},{3,35},{4,36},{5,37},{6,38},{7,39},{8,104},{9... | collective-permute-start | bytes 2359304 | tf_op jit(solution)/shard_map/ppermute | solution.py:29
  74.9 0.0 collective-permute-done.21.refs_21_
  74.9 0.0 collective-permute-done.5.refs_6_
  74.9 2.0 %collective-permute-start.20 = (bf16[2,528,384]{2,1,0:T(8,128)(2,1)S(1)}, bf16[2,528,384]{2,1,0:T(8,128)(2,1)S(1)}, u32[]{:S(2)}, u32[]{:S(2)}) collective-permute-start(bf16[2,528,384]{2,1,0:T(8,128)(2,1)S(1)} %collective-permute-done.19.refs_18_), channel_id=1, source_target_pairs={{0,2},{1,3},{2,4},{3,5},{4,6},{5,7},{6,0},{7,1},{8,14},{9,15},{10,... | collective-permute-start | bytes 2433032 | tf_op jit(solution)/shard_map/ppermute | solution.py:29
  76.9 0.0 collective-permute-start.11
  76.9 0.0 collective-permute-done.4.refs_5_
  76.9 3.0 %collective-permute-start.16 = (bf16[4,256,384]{2,1,0:T(8,128)(2,1)}, bf16[4,256,384]{2,1,0:T(8,128)(2,1)}, u32[]{:S(2)}, u32[]{:S(2)}) collective-permute-start(bf16[4,256,384]{2,1,0:T(8,128)(2,1)} %collective-permute-done.5.refs_6_), channel_id=1, source_target_pairs={{0,16},{1,17},{2,18},{3,19},{4,20},{5,21},{6,22},{7,23},{8,24},{9,... | collective-permute-start | bytes 2359304 | tf_op jit(solution)/shard_map/ppermute | solution.py:29
  80.0 3.9 %collective-permute-done.12.refs_10_ = bf16[4,256,384]{2,1,0:T(8,128)(2,1)} collective-permute-done((bf16[4,256,384]{2,1,0:T(8,128)(2,1)S(1)}, bf16[4,256,384]{2,1,0:T(8,128)(2,1)}, u32[]{:S(2)}, u32[]{:S(2)}) %collective-permute-start.12) | collective-permute-done | bytes 786464 | tf_op jit(solution)/shard_map/ppermute | solution.py:29
  83.8 3.5 %collective-permute-start.14 = (bf16[4,256,384]{2,1,0:T(8,128)(2,1)}, bf16[4,256,384]{2,1,0:T(8,128)(2,1)}, u32[]{:S(2)}, u32[]{:S(2)}) collective-permute-start(bf16[4,256,384]{2,1,0:T(8,128)(2,1)} %collective-permute-done.12.refs_10_), channel_id=1, source_target_pairs={{0,32},{1,33},{2,34},{3,35},{4,36},{5,37},{6,38},{7,39},{8,104},{9... | collective-permute-start | bytes 2359304 | tf_op jit(solution)/shard_map/ppermute | solution.py:29
  87.3 0.3 collective-permute-start.23
  87.6 7.5 %collective-permute-done.20.refs_19_ = bf16[2,528,384]{2,1,0:T(8,128)(2,1)S(1)} collective-permute-done((bf16[2,528,384]{2,1,0:T(8,128)(2,1)S(1)}, bf16[2,528,384]{2,1,0:T(8,128)(2,1)S(1)}, u32[]{:S(2)}, u32[]{:S(2)}) %collective-permute-start.20) | collective-permute-done | bytes 811040 | tf_op jit(solution)/shard_map/ppermute | solution.py:29
  95.1 0.9 copy-done.8
  96.0 1.6 %collective-permute-done.16.refs_14_ = bf16[4,256,384]{2,1,0:T(8,128)(2,1)} collective-permute-done((bf16[4,256,384]{2,1,0:T(8,128)(2,1)}, bf16[4,256,384]{2,1,0:T(8,128)(2,1)}, u32[]{:S(2)}, u32[]{:S(2)}) %collective-permute-start.16) | collective-permute-done | bytes 786464 | tf_op jit(solution)/shard_map/ppermute | solution.py:29
  97.5 1.2 collective-permute-start.17
  98.8 0.1 collective-permute-start.15
  99.1 0.1 stack.127
  99.2 0.1 stack.144
  99.3 0.1 select_reduce_fusion
  99.4 0.1 pad_add_fusion.source
  99.5 0.1 slice_reduce_fusion
  99.7 3.8 %collective-permute-done.23.refs_23_ = bf16[2,528,384]{2,1,0:T(8,128)(2,1)} collective-permute-done((bf16[2,528,384]{2,1,0:T(8,128)(2,1)}, bf16[2,528,384]{2,1,0:T(8,128)(2,1)}, u32[]{:S(2)}, u32[]{:S(2)}) %collective-permute-start.23) | collective-permute-done | bytes 811040 | tf_op jit(solution)/shard_map/ppermute | solution.py:29
  103.5 23.7 %shard_map.55 = f32[3,4,256,128]{3,2,1,0:T(8,128)} custom-call(s32[3]{0:T(128)S(1)} %and_select_fusion.shift, s32[32]{0:T(128)S(1)} %pad_add_fusion.source, bf16[4,256,384]{2,1,0:T(8,128)(2,1)} %copy-done.2, bf16[4,256,384]{2,1,0:T(8,128)(2,1)} %copy-done.11, bf16[4,256,384]{2,1,0:T(8,128)(2,1)} %copy-done.9, bf16[4,256,384]{2,1,0:T(8,128)(2,1)} %copy-done.13, ...), custom_call_target="tpu_custom_call" | custom-call | tf_op jit(solution)/shard_map/pallas_call | solution.py:104
  (53 shorter events, 0.2 us)
Async XLA Ops:
  0.0 2.1 %copy-start.16 = (bf16[4,256]{1,0:T(4,128)(2,1)S(1)}, bf16[4,256]{1,0:T(4,128)(2,1)}, u32[]{:S(2)}) copy-start(bf16[4,256]{1,0:T(4,128)(2,1)} %param.8) | copy-start | bytes 6148
  0.0 2.1 %copy-start.18 = (bf16[4,128]{1,0:T(4,128)(2,1)S(1)}, bf16[4,128]{1,0:T(4,128)(2,1)}, u32[]{:S(2)}) copy-start(bf16[4,128]{1,0:T(4,128)(2,1)} %param.7) | copy-start | bytes 3076
  2.1 2.5 %copy-start.3 = (bf16[4,256,128]{2,1,0:T(8,128)(2,1)S(1)}, bf16[4,256,128]{2,1,0:T(8,128)(2,1)}, u32[]{:S(2)}) copy-start(bf16[4,256,128]{2,1,0:T(8,128)(2,1)} %param.5) | copy-start | bytes 786436
  2.3 30.9 %copy-start.1 = (bf16[4,256,256]{2,1,0:T(8,128)(2,1)S(1)}, bf16[4,256,256]{2,1,0:T(8,128)(2,1)}, u32[]{:S(2)}) copy-start(bf16[4,256,256]{2,1,0:T(8,128)(2,1)} %param.6) | copy-start | bytes 1572868
  2.4 2.4 %collective-permute-start.7 = (bf16[528,384]{1,0:T(8,128)(2,1)S(1)}, bf16[528,384]{1,0:T(8,128)(2,1)S(1)}, u32[]{:S(2)}, u32[]{:S(2)}) collective-permute-start(bf16[528,384]{1,0:T(8,128)(2,1)S(1)} %get-tuple-element.15), channel_id=1, source_target_pairs={{0,0},{1,16},{2,34},{3,50},{4,68},{5,84},{6,102},{7,118},{8,8},{9,... | collective-permute-start | bytes 1216520 | tf_op jit(solution)/shard_map/ppermute | solution.py:29
  3.2 2.9 %collective-permute-start.8 = (bf16[528,384]{1,0:T(8,128)(2,1)S(1)}, bf16[528,384]{1,0:T(8,128)(2,1)S(1)}, u32[]{:S(2)}, u32[]{:S(2)}) collective-permute-start(bf16[528,384]{1,0:T(8,128)(2,1)S(1)} %get-tuple-element.16), channel_id=1, source_target_pairs={{0,8},{1,24},{2,42},{3,58},{4,76},{5,92},{6,110},{7,126},{8,0},{9,... | collective-permute-start | bytes 1216520 | tf_op jit(solution)/shard_map/ppermute | solution.py:29
  6.0 93.5 %copy-start.17 = (s32[3,64]{1,0:T(4,128)S(1)}, s32[3,64]{1,0:T(4,128)}, u32[]{:S(2)}) copy-start(s32[3,64]{1,0:T(4,128)} %param.9) | copy-start | bytes 2308
  6.1 97.3 %copy-start = (bf16[2,528,384]{2,1,0:T(8,128)(2,1)}, bf16[2,528,384]{2,1,0:T(8,128)(2,1)S(1)}, u32[]{:S(2)}) copy-start(bf16[2,528,384]{2,1,0:T(8,128)(2,1)S(1)} %pad_maximum_fusion.refs_16_) | copy-start | bytes 2433028
  6.2 40.9 %collective-permute-start.18 = (bf16[2,528,384]{2,1,0:T(8,128)(2,1)S(1)}, bf16[2,528,384]{2,1,0:T(8,128)(2,1)S(1)}, u32[]{:S(2)}, u32[]{:S(2)}) collective-permute-start(bf16[2,528,384]{2,1,0:T(8,128)(2,1)S(1)} %pad_maximum_fusion.refs_16_), channel_id=1, source_target_pairs={{0,2},{1,3},{2,4},{3,5},{4,6},{5,7},{6,0},{7,1},{8,14},{9,15},{10,... | collective-permute-start | bytes 2433032 | tf_op jit(solution)/shard_map/ppermute | solution.py:29
  31.0 16.8 %collective-permute-start.9 = (bf16[2,528,384]{2,1,0:T(8,128)(2,1)S(1)}, bf16[2,528,384]{2,1,0:T(8,128)(2,1)S(1)}, u32[]{:S(2)}, u32[]{:S(2)}) collective-permute-start(bf16[2,528,384]{2,1,0:T(8,128)(2,1)S(1)} %pad_maximum_fusion.refs_16_), channel_id=1, source_target_pairs={{0,1},{1,0},{2,3},{3,2},{4,5},{5,4},{6,7},{7,6},{8,9},{9,8},{10,11... | collective-permute-start | bytes 2433032 | tf_op jit(solution)/shard_map/ppermute | solution.py:29
  33.2 70.3 %copy-start.2 = (bf16[4,256,384]{2,1,0:T(8,128)(2,1)}, bf16[4,256,384]{2,1,0:T(8,128)(2,1)S(1)}, u32[]{:S(2)}) copy-start(bf16[4,256,384]{2,1,0:T(8,128)(2,1)S(1)} %constant_dynamic-update-slice_fusion.refs_0_) | copy-start | bytes 2359300
  33.2 11.2 %collective-permute-start.1 = (bf16[4,256,384]{2,1,0:T(8,128)(2,1)S(1)}, bf16[4,256,384]{2,1,0:T(8,128)(2,1)S(1)}, u32[]{:S(2)}, u32[]{:S(2)}) collective-permute-start(bf16[4,256,384]{2,1,0:T(8,128)(2,1)S(1)} %constant_dynamic-update-slice_fusion.refs_0_), channel_id=1, source_target_pairs={{0,32},{1,33},{2,34},{3,35},{4,36},{5,37},{6,38},{7,39},{8,104},{9... | collective-permute-start | bytes 2359304 | tf_op jit(solution)/shard_map/ppermute | solution.py:29
  44.4 53.1 %copy-start.9 = (bf16[4,256,384]{2,1,0:T(8,128)(2,1)}, bf16[4,256,384]{2,1,0:T(8,128)(2,1)S(1)}, u32[]{:S(2)}) copy-start(bf16[4,256,384]{2,1,0:T(8,128)(2,1)S(1)} %collective-permute-done.1.refs_2_) | copy-start | bytes 2359300
  44.4 11.5 %collective-permute-start.3 = (bf16[4,256,384]{2,1,0:T(8,128)(2,1)S(1)}, bf16[4,256,384]{2,1,0:T(8,128)(2,1)S(1)}, u32[]{:S(2)}, u32[]{:S(2)}) collective-permute-start(bf16[4,256,384]{2,1,0:T(8,128)(2,1)S(1)} %collective-permute-done.1.refs_2_), channel_id=1, source_target_pairs={{0,32},{1,33},{2,34},{3,35},{4,36},{5,37},{6,38},{7,39},{8,104},{9... | collective-permute-start | bytes 2359304 | tf_op jit(solution)/shard_map/ppermute | solution.py:29
  47.0 56.5 %copy-start.4 = (bf16[2,528,384]{2,1,0:T(8,128)(2,1)}, bf16[2,528,384]{2,1,0:T(8,128)(2,1)S(1)}, u32[]{:S(2)}) copy-start(bf16[2,528,384]{2,1,0:T(8,128)(2,1)S(1)} %collective-permute-done.18.refs_17_) | copy-start | bytes 2433028
  47.0 22.2 %collective-permute-start.19 = (bf16[2,528,384]{2,1,0:T(8,128)(2,1)S(1)}, bf16[2,528,384]{2,1,0:T(8,128)(2,1)S(1)}, u32[]{:S(2)}, u32[]{:S(2)}) collective-permute-start(bf16[2,528,384]{2,1,0:T(8,128)(2,1)S(1)} %collective-permute-done.18.refs_17_), channel_id=1, source_target_pairs={{0,2},{1,3},{2,4},{3,5},{4,6},{5,7},{6,0},{7,1},{8,14},{9,15},{10,... | collective-permute-start | bytes 2433032 | tf_op jit(solution)/shard_map/ppermute | solution.py:29
  47.1 12.3 %collective-permute-start = (bf16[4,256,384]{2,1,0:T(8,128)(2,1)S(1)}, bf16[4,256,384]{2,1,0:T(8,128)(2,1)S(1)}, u32[]{:S(2)}, u32[]{:S(2)}) collective-permute-start(bf16[4,256,384]{2,1,0:T(8,128)(2,1)S(1)} %constant_dynamic-update-slice_fusion.refs_0_), channel_id=1, source_target_pairs={{0,8},{1,9},{2,10},{3,11},{4,12},{5,13},{6,14},{7,15},{8,0},{9,1},... | collective-permute-start | bytes 2359304 | tf_op jit(solution)/shard_map/ppermute | solution.py:29
  47.8 55.7 %copy-start.5 = (bf16[2,528,384]{2,1,0:T(8,128)(2,1)}, bf16[2,528,384]{2,1,0:T(8,128)(2,1)S(1)}, u32[]{:S(2)}) copy-start(bf16[2,528,384]{2,1,0:T(8,128)(2,1)S(1)} %collective-permute-done.9.refs_20_) | copy-start | bytes 2433028
  47.8 21.0 %collective-permute-start.10 = (bf16[4,256,384]{2,1,0:T(8,128)(2,1)S(1)}, bf16[4,256,384]{2,1,0:T(8,128)(2,1)S(1)}, u32[]{:S(2)}, u32[]{:S(2)}) collective-permute-start(bf16[4,256,384]{2,1,0:T(8,128)(2,1)S(1)} %constant_dynamic-update-slice_fusion.refs_0_), channel_id=1, source_target_pairs={{0,16},{1,17},{2,18},{3,19},{4,20},{5,21},{6,22},{7,23},{8,24},{9,... | collective-permute-start | bytes 2359304 | tf_op jit(solution)/shard_map/ppermute | solution.py:29
  51.5 23.4 %collective-permute-start.21 = (bf16[2,528,384]{2,1,0:T(8,128)(2,1)S(1)}, bf16[2,528,384]{2,1,0:T(8,128)(2,1)S(1)}, u32[]{:S(2)}, u32[]{:S(2)}) collective-permute-start(bf16[2,528,384]{2,1,0:T(8,128)(2,1)S(1)} %collective-permute-done.9.refs_20_), channel_id=1, source_target_pairs={{0,2},{1,3},{2,4},{3,5},{4,6},{5,7},{6,0},{7,1},{8,14},{9,15},{10,... | collective-permute-start | bytes 2433032 | tf_op jit(solution)/shard_map/ppermute | solution.py:29
  56.0 42.8 %copy-start.10 = (bf16[4,256,384]{2,1,0:T(8,128)(2,1)}, bf16[4,256,384]{2,1,0:T(8,128)(2,1)S(1)}, u32[]{:S(2)}) copy-start(bf16[4,256,384]{2,1,0:T(8,128)(2,1)S(1)} %collective-permute-done.3.refs_4_) | copy-start | bytes 2359300
  56.0 18.9 %collective-permute-start.5 = (bf16[4,256,384]{2,1,0:T(8,128)(2,1)S(1)}, bf16[4,256,384]{2,1,0:T(8,128)(2,1)}, u32[]{:S(2)}, u32[]{:S(2)}) collective-permute-start(bf16[4,256,384]{2,1,0:T(8,128)(2,1)S(1)} %collective-permute-done.3.refs_4_), channel_id=1, source_target_pairs={{0,32},{1,33},{2,34},{3,35},{4,36},{5,37},{6,38},{7,39},{8,104},{9... | collective-permute-start | bytes 2359304 | tf_op jit(solution)/shard_map/ppermute | solution.py:29
  59.4 15.5 %copy-start.11 = (bf16[4,256,384]{2,1,0:T(8,128)(2,1)}, bf16[4,256,384]{2,1,0:T(8,128)(2,1)S(1)}, u32[]{:S(2)}) copy-start(bf16[4,256,384]{2,1,0:T(8,128)(2,1)S(1)} %collective-permute-done.refs_1_) | copy-start | bytes 2359300
  59.4 17.5 %collective-permute-start.2 = (bf16[4,256,384]{2,1,0:T(8,128)(2,1)S(1)}, bf16[4,256,384]{2,1,0:T(8,128)(2,1)S(1)}, u32[]{:S(2)}, u32[]{:S(2)}) collective-permute-start(bf16[4,256,384]{2,1,0:T(8,128)(2,1)S(1)} %collective-permute-done.1.refs_2_), channel_id=1, source_target_pairs={{0,8},{1,9},{2,10},{3,11},{4,12},{5,13},{6,14},{7,15},{8,0},{9,1},... | collective-permute-start | bytes 2359304 | tf_op jit(solution)/shard_map/ppermute | solution.py:29
  68.9 29.9 %copy-start.12 = (bf16[4,256,384]{2,1,0:T(8,128)(2,1)}, bf16[4,256,384]{2,1,0:T(8,128)(2,1)S(1)}, u32[]{:S(2)}) copy-start(bf16[4,256,384]{2,1,0:T(8,128)(2,1)S(1)} %collective-permute-done.10.refs_8_) | copy-start | bytes 2359300
  68.9 8.0 %collective-permute-start.4 = (bf16[4,256,384]{2,1,0:T(8,128)(2,1)S(1)}, bf16[4,256,384]{2,1,0:T(8,128)(2,1)S(1)}, u32[]{:S(2)}, u32[]{:S(2)}) collective-permute-start(bf16[4,256,384]{2,1,0:T(8,128)(2,1)S(1)} %collective-permute-done.3.refs_4_), channel_id=1, source_target_pairs={{0,8},{1,9},{2,10},{3,11},{4,12},{5,13},{6,14},{7,15},{8,0},{9,1},... | collective-permute-start | bytes 2359304 | tf_op jit(solution)/shard_map/ppermute | solution.py:29
  69.2 5.7 %copy-start.6 = (bf16[2,528,384]{2,1,0:T(8,128)(2,1)}, bf16[2,528,384]{2,1,0:T(8,128)(2,1)S(1)}, u32[]{:S(2)}) copy-start(bf16[2,528,384]{2,1,0:T(8,128)(2,1)S(1)} %collective-permute-done.19.refs_18_) | copy-start | bytes 2433028
  69.2 14.6 %collective-permute-start.12 = (bf16[4,256,384]{2,1,0:T(8,128)(2,1)S(1)}, bf16[4,256,384]{2,1,0:T(8,128)(2,1)}, u32[]{:S(2)}, u32[]{:S(2)}) collective-permute-start(bf16[4,256,384]{2,1,0:T(8,128)(2,1)S(1)} %collective-permute-done.10.refs_8_), channel_id=1, source_target_pairs={{0,32},{1,33},{2,34},{3,35},{4,36},{5,37},{6,38},{7,39},{8,104},{9... | collective-permute-start | bytes 2359304 | tf_op jit(solution)/shard_map/ppermute | solution.py:29
  74.9 20.2 %copy-start.7 = (bf16[2,528,384]{2,1,0:T(8,128)(2,1)}, bf16[2,528,384]{2,1,0:T(8,128)(2,1)S(1)}, u32[]{:S(2)}) copy-start(bf16[2,528,384]{2,1,0:T(8,128)(2,1)S(1)} %collective-permute-done.21.refs_21_) | copy-start | bytes 2433028
  74.9 12.4 %collective-permute-start.22 = (bf16[2,528,384]{2,1,0:T(8,128)(2,1)S(1)}, bf16[2,528,384]{2,1,0:T(8,128)(2,1)}, u32[]{:S(2)}, u32[]{:S(2)}) collective-permute-start(bf16[2,528,384]{2,1,0:T(8,128)(2,1)S(1)} %collective-permute-done.21.refs_21_), channel_id=1, source_target_pairs={{0,2},{1,3},{2,4},{3,5},{4,6},{5,7},{6,0},{7,1},{8,14},{9,15},{10,... | collective-permute-start | bytes 2433032 | tf_op jit(solution)/shard_map/ppermute | solution.py:29
  74.9 20.2 %collective-permute-start.20 = (bf16[2,528,384]{2,1,0:T(8,128)(2,1)S(1)}, bf16[2,528,384]{2,1,0:T(8,128)(2,1)S(1)}, u32[]{:S(2)}, u32[]{:S(2)}) collective-permute-start(bf16[2,528,384]{2,1,0:T(8,128)(2,1)S(1)} %collective-permute-done.19.refs_18_), channel_id=1, source_target_pairs={{0,2},{1,3},{2,4},{3,5},{4,6},{5,7},{6,0},{7,1},{8,14},{9,15},{10,... | collective-permute-start | bytes 2433032 | tf_op jit(solution)/shard_map/ppermute | solution.py:29
  76.9 21.9 %copy-start.13 = (bf16[4,256,384]{2,1,0:T(8,128)(2,1)}, bf16[4,256,384]{2,1,0:T(8,128)(2,1)S(1)}, u32[]{:S(2)}) copy-start(bf16[4,256,384]{2,1,0:T(8,128)(2,1)S(1)} %collective-permute-done.2.refs_3_) | copy-start | bytes 2359300
  76.9 10.7 %collective-permute-start.11 = (bf16[4,256,384]{2,1,0:T(8,128)(2,1)S(1)}, bf16[4,256,384]{2,1,0:T(8,128)(2,1)S(1)}, u32[]{:S(2)}, u32[]{:S(2)}) collective-permute-start(bf16[4,256,384]{2,1,0:T(8,128)(2,1)S(1)} %collective-permute-done.10.refs_8_), channel_id=1, source_target_pairs={{0,8},{1,9},{2,10},{3,11},{4,12},{5,13},{6,14},{7,15},{8,0},{9,1},... | collective-permute-start | bytes 2359304 | tf_op jit(solution)/shard_map/ppermute | solution.py:29
  76.9 21.9 %copy-start.14 = (bf16[4,256,384]{2,1,0:T(8,128)(2,1)}, bf16[4,256,384]{2,1,0:T(8,128)(2,1)S(1)}, u32[]{:S(2)}) copy-start(bf16[4,256,384]{2,1,0:T(8,128)(2,1)S(1)} %collective-permute-done.4.refs_5_) | copy-start | bytes 2359300
  76.9 20.6 %collective-permute-start.16 = (bf16[4,256,384]{2,1,0:T(8,128)(2,1)}, bf16[4,256,384]{2,1,0:T(8,128)(2,1)}, u32[]{:S(2)}, u32[]{:S(2)}) collective-permute-start(bf16[4,256,384]{2,1,0:T(8,128)(2,1)} %collective-permute-done.5.refs_6_), channel_id=1, source_target_pairs={{0,16},{1,17},{2,18},{3,19},{4,20},{5,21},{6,22},{7,23},{8,24},{9,... | collective-permute-start | bytes 2359304 | tf_op jit(solution)/shard_map/ppermute | solution.py:29
  83.8 15.0 %collective-permute-start.14 = (bf16[4,256,384]{2,1,0:T(8,128)(2,1)}, bf16[4,256,384]{2,1,0:T(8,128)(2,1)}, u32[]{:S(2)}, u32[]{:S(2)}) collective-permute-start(bf16[4,256,384]{2,1,0:T(8,128)(2,1)} %collective-permute-done.12.refs_10_), channel_id=1, source_target_pairs={{0,32},{1,33},{2,34},{3,35},{4,36},{5,37},{6,38},{7,39},{8,104},{9... | collective-permute-start | bytes 2359304 | tf_op jit(solution)/shard_map/ppermute | solution.py:29
  87.3 16.1 %collective-permute-start.23 = (bf16[2,528,384]{2,1,0:T(8,128)(2,1)}, bf16[2,528,384]{2,1,0:T(8,128)(2,1)}, u32[]{:S(2)}, u32[]{:S(2)}) collective-permute-start(bf16[2,528,384]{2,1,0:T(8,128)(2,1)} %collective-permute-done.22.refs_22_), channel_id=1, source_target_pairs={{0,2},{1,3},{2,4},{3,5},{4,6},{5,7},{6,0},{7,1},{8,14},{9,15},{10,... | collective-permute-start | bytes 2433032 | tf_op jit(solution)/shard_map/ppermute | solution.py:29
  87.6 11.2 %copy-start.15 = (bf16[4,256,384]{2,1,0:T(8,128)(2,1)}, bf16[4,256,384]{2,1,0:T(8,128)(2,1)S(1)}, u32[]{:S(2)}) copy-start(bf16[4,256,384]{2,1,0:T(8,128)(2,1)S(1)} %collective-permute-done.11.refs_9_) | copy-start | bytes 2359300
  87.6 12.0 %collective-permute-start.6 = (bf16[4,256,384]{2,1,0:T(8,128)(2,1)}, bf16[4,256,384]{2,1,0:T(8,128)(2,1)}, u32[]{:S(2)}, u32[]{:S(2)}) collective-permute-start(bf16[4,256,384]{2,1,0:T(8,128)(2,1)} %collective-permute-done.5.refs_6_), channel_id=1, source_target_pairs={{0,8},{1,9},{2,10},{3,11},{4,12},{5,13},{6,14},{7,15},{8,0},{9,1},... | collective-permute-start | bytes 2359304 | tf_op jit(solution)/shard_map/ppermute | solution.py:29
  95.1 0.9 copy-start.8
  95.1 4.6 %collective-permute-start.13 = (bf16[4,256,384]{2,1,0:T(8,128)(2,1)}, bf16[4,256,384]{2,1,0:T(8,128)(2,1)}, u32[]{:S(2)}, u32[]{:S(2)}) collective-permute-start(bf16[4,256,384]{2,1,0:T(8,128)(2,1)} %collective-permute-done.12.refs_10_), channel_id=1, source_target_pairs={{0,8},{1,9},{2,10},{3,11},{4,12},{5,13},{6,14},{7,15},{8,0},{9,1},... | collective-permute-start | bytes 2359304 | tf_op jit(solution)/shard_map/ppermute | solution.py:29
  97.5 5.9 %collective-permute-start.17 = (bf16[4,256,384]{2,1,0:T(8,128)(2,1)}, bf16[4,256,384]{2,1,0:T(8,128)(2,1)}, u32[]{:S(2)}, u32[]{:S(2)}) collective-permute-start(bf16[4,256,384]{2,1,0:T(8,128)(2,1)} %collective-permute-done.16.refs_14_), channel_id=1, source_target_pairs={{0,8},{1,9},{2,10},{3,11},{4,12},{5,13},{6,14},{7,15},{8,0},{9,1},... | collective-permute-start | bytes 2359304 | tf_op jit(solution)/shard_map/ppermute | solution.py:29
  98.8 4.7 %collective-permute-start.15 = (bf16[4,256,384]{2,1,0:T(8,128)(2,1)}, bf16[4,256,384]{2,1,0:T(8,128)(2,1)}, u32[]{:S(2)}, u32[]{:S(2)}) collective-permute-start(bf16[4,256,384]{2,1,0:T(8,128)(2,1)} %collective-permute-done.14.refs_12_), channel_id=1, source_target_pairs={{0,8},{1,9},{2,10},{3,11},{4,12},{5,13},{6,14},{7,15},{8,0},{9,1},... | collective-permute-start | bytes 2359304 | tf_op jit(solution)/shard_map/ppermute | solution.py:29

commit v5 on v4

--- a/solution.py
+++ b/solution.py
@@ -7,6 +7,7 @@
 
 AXES = ("z", "yh", "c", "x", "yl")
 NTAU = 4
+HEIGHT = 16
 TAUS = [0.25 * 2.0**t for t in range(NTAU)]
 NT_DIMS = (((1,), (1,)), ((), ()))
 
@@ -40,7 +41,7 @@
         return pltpu.make_async_copy(col_src[n // 2].at[n % 2], col_pts.at[slot, pl.ds(0, 528)], col_sems.at[slot])
 
     def fetch(step):
-        slab, slot = lax.rem(step + 15, 16), lax.rem(step, 3)
+        slab, slot = lax.rem(step + 15, 16), lax.rem(step, 4)
         row_from, col_from = source[slab], source[16 + slab]
         for n in range(16):
 
@@ -52,21 +53,8 @@
             def _():
                 col_copy(n, slot).start()
 
-    fetch(0)
-    fetch(1)
-    acc[...] = jnp.zeros_like(acc)
-
-    @pl.loop(0, 17)
-    def _(step):
-        par = lax.rem(step + 1, 2) * 4
-        slot = lax.rem(step, 3)
-
-        @pl.when(step < 15)
-        def _():
-            fetch(step + 2)
-
-        row_copy(0, slot).wait()
-        col_copy(0, slot).wait()
+    def products(step, base, obase):
+        slot = lax.rem(step, 4)
         gaps = col_pts[slot, 512:528, :].astype(jnp.float32)
         factors = [jnp.exp(-gaps * TAUS[t]) for t in range(NTAU)]
         for i in range(4):
@@ -74,23 +62,42 @@
             panel = jnp.concatenate(
                 [(col * factors[t][i : i + 1]).astype(jnp.bfloat16) for t in range(NTAU)], 0
             )
-            vbuf[par + i] = lax.dot_general(
+            vbuf[base + i] = lax.dot_general(
                 panel[:, 128:], row_pts[slot, i, :, 128:], NT_DIMS, preferred_element_type=jnp.float32
             )
-            obuf[i] = lax.dot_general(
-                panel[:, :128], row_pts[slot, i, :, :128], NT_DIMS, preferred_element_type=jnp.float32
-            )
-
-        @pl.when(step > 0)
+            if obase is not None:
+                obuf[obase + i] = lax.dot_general(
+                    panel[:, :128], row_pts[slot, i, :, :128], NT_DIMS, preferred_element_type=jnp.float32
+                )
+
+    def arrive(step):
+        row_copy(0, lax.rem(step, 4)).wait()
+        col_copy(0, lax.rem(step, 4)).wait()
+
+    for step in range(3):
+        fetch(step)
+    acc[...] = jnp.zeros_like(acc)
+    arrive(0)
+    products(0, 4, None)
+
+    @pl.loop(0, 8)
+    def _(pair):
+        @pl.when(pair < 7)
         def _():
-            height = 32
-            for g in range(512 // height):
-                rows = pl.ds(g * height, height)
-                occs = [obuf[i, rows, :] for i in range(4)]
+            fetch(2 * pair + 3)
+            fetch(2 * pair + 4)
+
+        arrive(2 * pair + 1)
+        arrive(2 * pair + 2)
+        for part in (0, 4):
+            products(2 * pair + 1 + part // 4, part, part)
+            for g in range(512 // HEIGHT):
+                rows = pl.ds(g * HEIGHT, HEIGHT)
+                occs = [obuf[part + i, rows, :] for i in range(4)]
                 for q in range(3):
                     total = acc[q, rows, :]
                     for i in range(4):
-                        total = total + occs[i] * vbuf[lax.rem(par + i - shift[q] + 8, 8), rows, :]
+                        total = total + occs[i] * vbuf[lax.rem(part + i - shift[q] + 8, 8), rows, :]
                     acc[q, rows, :] = total
 
     for q in range(3):
@@ -106,13 +113,13 @@
         in_specs=[scalars, scalars] + [anywhere] * 24,
         out_specs=pl.BlockSpec(memory_space=pltpu.VMEM),
         scratch_shapes=[
-            pltpu.VMEM((3, 4, 256, 384), jnp.bfloat16),
-            pltpu.VMEM((3, 576, 384), jnp.bfloat16),
+            pltpu.VMEM((4, 4, 256, 384), jnp.bfloat16),
+            pltpu.VMEM((4, 576, 384), jnp.bfloat16),
             pltpu.VMEM((8, 512, 256), jnp.float32),
-            pltpu.VMEM((4, 512, 256), jnp.float32),
+            pltpu.VMEM((8, 512, 256), jnp.float32),
             pltpu.VMEM((3, 512, 256), jnp.float32),
-            pltpu.SemaphoreType.DMA((3,)),
-            pltpu.SemaphoreType.DMA((3,)),
+            pltpu.SemaphoreType.DMA((4,)),
+            pltpu.SemaphoreType.DMA((4,)),
         ],
         out_shape=jax.ShapeDtypeStruct((3, NTAU, 256, 128), jnp.float32),
         compiler_params=pltpu.CompilerParams(vmem_limit_bytes=24 * 2**20),
@@ -142,7 +149,6 @@
 def on_device(occ_orbitals, virt_orbitals, occ_gap, virt_gap, partner):
     z, yh, c, x, yl = (lax.axis_index(a) for a in AXES)
     shift = (-partner[:, 0]) % 64
-    own = jnp.concatenate([occ_orbitals, virt_orbitals], axis=2)
     gaps = jnp.concatenate([occ_gap, virt_gap], axis=1)
     gaps = jnp.pad(gaps, ((0, 12), (0, 0)))
 
@@ -150,8 +156,10 @@
         cut = [lax.dynamic_slice_in_dim(a, core * 128, 128, 1) for a in (occ_orbitals, virt_orbitals)]
         return jnp.concatenate([jnp.concatenate(cut, axis=2).reshape(512, 384), gaps])
 
-    here = send(half(c), lambda z, yh, c, x, yl: (x, yl, c, x + z, yh))
-    there = send(half(1 - c), lambda z, yh, c, x, yl: (x, yl, 1 - c, x + z, yh))
+    halves = half(c), half(1 - c)
+    own = jnp.concatenate([after(occ_orbitals, *halves), virt_orbitals], axis=2)
+    here = send(halves[0], lambda z, yh, c, x, yl: (x, yl, c, x + z, yh))
+    there = send(halves[1], lambda z, yh, c, x, yl: (x, yl, 1 - c, x + z, yh))
     cols = jnp.stack([here, there])
     cols_same, rows_same = [cols], [own]
     cols_cross = [send(cols, lambda z, yh, c, x, yl: (z, yh, c, x, 1 - yl))]

time: 127 us -> 125 us (0.984)
  waiting for transfers between devices: 38.3 us -> 37 us
where the time goes in v5:
time: 125 us
  starting transfers between devices  60.6 us (48%)
  waiting for transfers between devices  37 us (30%)
  Pallas kernels  23.1 us (18%)
  local copies, waits for them, and re-layouts  3.44 us (3%)
    ppermute x24, starting transfers between devices, send(): return lax.ppermute(block, AXES, routes(target))  60.6 us
    ppermute x24, waiting for transfers between devices, send(): return lax.ppermute(block, AXES, routes(target))  37 us
    pallas_call x1, Pallas kernels, polarizability(): pl.pallas_call(kernel, in_specs=[scalars, scalars] + [anywhere] * 24, out...  23.1 us
  transfers between devices with their start and end apart: 24, of which 9 were waited for; matrix products, arithmetic and copies ran while one was open for 0% of the time, Pallas kernels for 0%

profile of v5, /device:TPU:1, one launch (start us, length us, event | category | flops | bytes accessed | tf_op | source)
XLA Modules:
  0.0 125.2 jit_solution(9014926981673342618)
XLA Ops:
  0.0 1.0 constant_dynamic-slice_fusion.1
  1.0 1.1 constant_dynamic-slice_fusion
  2.1 0.0 copy-start.3
  2.1 0.1 pad_maximum_fusion.3
  2.3 0.0 copy-start.1
  2.3 0.1 pad_maximum_fusion.1
  2.4 1.5 %collective-permute-start.8 = (bf16[528,384]{1,0:T(8,128)(2,1)S(1)}, bf16[528,384]{1,0:T(8,128)(2,1)S(1)}, u32[]{:S(2)}, u32[]{:S(2)}) collective-permute-start(bf16[528,384]{1,0:T(8,128)(2,1)S(1)} %get-tuple-element.17), channel_id=1, source_target_pairs={{0,8},{1,24},{2,42},{3,58},{4,76},{5,92},{6,110},{7,126},{8,0},{9,... | collective-permute-start | bytes 1216520 | tf_op jit(solution)/shard_map/ppermute | solution.py:30
  3.9 0.7 collective-permute-start.7
  4.6 0.6 collective-permute-done.8
  5.2 0.1 pad_maximum_fusion.refs_16_
  5.3 24.5 %collective-permute-start.18 = (bf16[2,528,384]{2,1,0:T(8,128)(2,1)S(1)}, bf16[2,528,384]{2,1,0:T(8,128)(2,1)S(1)}, u32[]{:S(2)}, u32[]{:S(2)}) collective-permute-start(bf16[2,528,384]{2,1,0:T(8,128)(2,1)S(1)} %pad_maximum_fusion.refs_16_), channel_id=1, source_target_pairs={{0,2},{1,3},{2,4},{3,5},{4,6},{5,7},{6,0},{7,1},{8,14},{9,15},{10,... | collective-permute-start | bytes 2433032 | tf_op jit(solution)/shard_map/ppermute | solution.py:30
  29.9 2.2 %collective-permute-start.9 = (bf16[2,528,384]{2,1,0:T(8,128)(2,1)S(1)}, bf16[2,528,384]{2,1,0:T(8,128)(2,1)S(1)}, u32[]{:S(2)}, u32[]{:S(2)}) collective-permute-start(bf16[2,528,384]{2,1,0:T(8,128)(2,1)S(1)} %pad_maximum_fusion.refs_16_), channel_id=1, source_target_pairs={{0,1},{1,0},{2,3},{3,2},{4,5},{5,4},{6,7},{7,6},{8,9},{9,8},{10,11... | collective-permute-start | bytes 2433032 | tf_op jit(solution)/shard_map/ppermute | solution.py:30
  32.1 1.7 %collective-permute-start.1 = (bf16[4,256,384]{2,1,0:T(8,128)(2,1)S(1)}, bf16[4,256,384]{2,1,0:T(8,128)(2,1)S(1)}, u32[]{:S(2)}, u32[]{:S(2)}) collective-permute-start(bf16[4,256,384]{2,1,0:T(8,128)(2,1)S(1)} %constant_dynamic-update-slice_fusion.refs_0_), channel_id=1, source_target_pairs={{0,32},{1,33},{2,34},{3,35},{4,36},{5,37},{6,38},{7,39},{8,104},{9... | collective-permute-start | bytes 2359304 | tf_op jit(solution)/shard_map/ppermute | solution.py:30
  33.9 9.5 %collective-permute-done.1.refs_2_ = bf16[4,256,384]{2,1,0:T(8,128)(2,1)S(1)} collective-permute-done((bf16[4,256,384]{2,1,0:T(8,128)(2,1)S(1)}, bf16[4,256,384]{2,1,0:T(8,128)(2,1)S(1)}, u32[]{:S(2)}, u32[]{:S(2)}) %collective-permute-start.1) | collective-permute-done | bytes 786464 | tf_op jit(solution)/shard_map/ppermute | solution.py:30
  43.3 2.6 %collective-permute-start.3 = (bf16[4,256,384]{2,1,0:T(8,128)(2,1)S(1)}, bf16[4,256,384]{2,1,0:T(8,128)(2,1)S(1)}, u32[]{:S(2)}, u32[]{:S(2)}) collective-permute-start(bf16[4,256,384]{2,1,0:T(8,128)(2,1)S(1)} %collective-permute-done.1.refs_2_), channel_id=1, source_target_pairs={{0,32},{1,33},{2,34},{3,35},{4,36},{5,37},{6,38},{7,39},{8,104},{9... | collective-permute-start | bytes 2359304 | tf_op jit(solution)/shard_map/ppermute | solution.py:30
  45.9 0.0 collective-permute-done.18.refs_17_
  45.9 0.1 collective-permute-start.19
  46.0 1.3 %collective-permute-start = (bf16[4,256,384]{2,1,0:T(8,128)(2,1)S(1)}, bf16[4,256,384]{2,1,0:T(8,128)(2,1)S(1)}, u32[]{:S(2)}, u32[]{:S(2)}) collective-permute-start(bf16[4,256,384]{2,1,0:T(8,128)(2,1)S(1)} %constant_dynamic-update-slice_fusion.refs_0_), channel_id=1, source_target_pairs={{0,8},{1,9},{2,10},{3,11},{4,12},{5,13},{6,14},{7,15},{8,0},{9,1},... | collective-permute-start | bytes 2359304 | tf_op jit(solution)/shard_map/ppermute | solution.py:30
  47.3 0.3 collective-permute-done.9.refs_20_
  47.6 3.7 %collective-permute-start.10 = (bf16[4,256,384]{2,1,0:T(8,128)(2,1)S(1)}, bf16[4,256,384]{2,1,0:T(8,128)(2,1)S(1)}, u32[]{:S(2)}, u32[]{:S(2)}) collective-permute-start(bf16[4,256,384]{2,1,0:T(8,128)(2,1)S(1)} %constant_dynamic-update-slice_fusion.refs_0_), channel_id=1, source_target_pairs={{0,16},{1,17},{2,18},{3,19},{4,20},{5,21},{6,22},{7,23},{8,24},{9,... | collective-permute-start | bytes 2359304 | tf_op jit(solution)/shard_map/ppermute | solution.py:30
  51.2 3.5 %collective-permute-start.21 = (bf16[2,528,384]{2,1,0:T(8,128)(2,1)S(1)}, bf16[2,528,384]{2,1,0:T(8,128)(2,1)S(1)}, u32[]{:S(2)}, u32[]{:S(2)}) collective-permute-start(bf16[2,528,384]{2,1,0:T(8,128)(2,1)S(1)} %collective-permute-done.9.refs_20_), channel_id=1, source_target_pairs={{0,2},{1,3},{2,4},{3,5},{4,6},{5,7},{6,0},{7,1},{8,14},{9,15},{10,... | collective-permute-start | bytes 2433032 | tf_op jit(solution)/shard_map/ppermute | solution.py:30
  54.7 0.1 collective-permute-done.3.refs_4_
  54.8 3.4 %collective-permute-start.5 = (bf16[4,256,384]{2,1,0:T(8,128)(2,1)S(1)}, bf16[4,256,384]{2,1,0:T(8,128)(2,1)}, u32[]{:S(2)}, u32[]{:S(2)}) collective-permute-start(bf16[4,256,384]{2,1,0:T(8,128)(2,1)S(1)} %collective-permute-done.3.refs_4_), channel_id=1, source_target_pairs={{0,32},{1,33},{2,34},{3,35},{4,36},{5,37},{6,38},{7,39},{8,104},{9... | collective-permute-start | bytes 2359304 | tf_op jit(solution)/shard_map/ppermute | solution.py:30
  58.3 0.0 collective-permute-done.refs_1_
  58.3 0.0 collective-permute-start.2
  58.3 10.3 %collective-permute-done.10.refs_8_ = bf16[4,256,384]{2,1,0:T(8,128)(2,1)S(1)} collective-permute-done((bf16[4,256,384]{2,1,0:T(8,128)(2,1)S(1)}, bf16[4,256,384]{2,1,0:T(8,128)(2,1)S(1)}, u32[]{:S(2)}, u32[]{:S(2)}) %collective-permute-start.10) | collective-permute-done | bytes 786464 | tf_op jit(solution)/shard_map/ppermute | solution.py:30
  68.6 0.3 collective-permute-start.4
  68.9 4.2 %collective-permute-start.12 = (bf16[4,256,384]{2,1,0:T(8,128)(2,1)S(1)}, bf16[4,256,384]{2,1,0:T(8,128)(2,1)}, u32[]{:S(2)}, u32[]{:S(2)}) collective-permute-start(bf16[4,256,384]{2,1,0:T(8,128)(2,1)S(1)} %collective-permute-done.10.refs_8_), channel_id=1, source_target_pairs={{0,32},{1,33},{2,34},{3,35},{4,36},{5,37},{6,38},{7,39},{8,104},{9... | collective-permute-start | bytes 2359304 | tf_op jit(solution)/shard_map/ppermute | solution.py:30
  73.1 0.2 collective-permute-start.22
  73.3 0.0 collective-permute-done.5.refs_6_
  73.3 2.2 %collective-permute-start.20 = (bf16[2,528,384]{2,1,0:T(8,128)(2,1)S(1)}, bf16[2,528,384]{2,1,0:T(8,128)(2,1)S(1)}, u32[]{:S(2)}, u32[]{:S(2)}) collective-permute-start(bf16[2,528,384]{2,1,0:T(8,128)(2,1)S(1)} %collective-permute-done.19.refs_18_), channel_id=1, source_target_pairs={{0,2},{1,3},{2,4},{3,5},{4,6},{5,7},{6,0},{7,1},{8,14},{9,15},{10,... | collective-permute-start | bytes 2433032 | tf_op jit(solution)/shard_map/ppermute | solution.py:30
  75.6 0.0 collective-permute-done.2.refs_3_
  75.6 2.9 %collective-permute-start.16 = (bf16[4,256,384]{2,1,0:T(8,128)(2,1)}, bf16[4,256,384]{2,1,0:T(8,128)(2,1)}, u32[]{:S(2)}, u32[]{:S(2)}) collective-permute-start(bf16[4,256,384]{2,1,0:T(8,128)(2,1)} %collective-permute-done.5.refs_6_), channel_id=1, source_target_pairs={{0,16},{1,17},{2,18},{3,19},{4,20},{5,21},{6,22},{7,23},{8,24},{9,... | collective-permute-start | bytes 2359304 | tf_op jit(solution)/shard_map/ppermute | solution.py:30
  78.5 3.5 %collective-permute-done.12.refs_10_ = bf16[4,256,384]{2,1,0:T(8,128)(2,1)} collective-permute-done((bf16[4,256,384]{2,1,0:T(8,128)(2,1)S(1)}, bf16[4,256,384]{2,1,0:T(8,128)(2,1)}, u32[]{:S(2)}, u32[]{:S(2)}) %collective-permute-start.12) | collective-permute-done | bytes 786464 | tf_op jit(solution)/shard_map/ppermute | solution.py:30
  82.0 3.5 %collective-permute-start.14 = (bf16[4,256,384]{2,1,0:T(8,128)(2,1)}, bf16[4,256,384]{2,1,0:T(8,128)(2,1)}, u32[]{:S(2)}, u32[]{:S(2)}) collective-permute-start(bf16[4,256,384]{2,1,0:T(8,128)(2,1)} %collective-permute-done.12.refs_10_), channel_id=1, source_target_pairs={{0,32},{1,33},{2,34},{3,35},{4,36},{5,37},{6,38},{7,39},{8,104},{9... | collective-permute-start | bytes 2359304 | tf_op jit(solution)/shard_map/ppermute | solution.py:30
  85.5 0.5 collective-permute-start.23
  86.1 7.5 %collective-permute-done.20.refs_19_ = bf16[2,528,384]{2,1,0:T(8,128)(2,1)S(1)} collective-permute-done((bf16[2,528,384]{2,1,0:T(8,128)(2,1)S(1)}, bf16[2,528,384]{2,1,0:T(8,128)(2,1)S(1)}, u32[]{:S(2)}, u32[]{:S(2)}) %collective-permute-start.20) | collective-permute-done | bytes 811040 | tf_op jit(solution)/shard_map/ppermute | solution.py:30
  93.6 0.9 copy-done.8
  94.4 1.7 %collective-permute-done.16.refs_14_ = bf16[4,256,384]{2,1,0:T(8,128)(2,1)} collective-permute-done((bf16[4,256,384]{2,1,0:T(8,128)(2,1)}, bf16[4,256,384]{2,1,0:T(8,128)(2,1)}, u32[]{:S(2)}, u32[]{:S(2)}) %collective-permute-start.16) | collective-permute-done | bytes 786464 | tf_op jit(solution)/shard_map/ppermute | solution.py:30
  96.2 1.2 collective-permute-start.17
  97.5 0.3 collective-permute-start.15
  98.0 0.1 stack.127
  98.1 0.1 stack.144
  98.2 0.1 select_reduce_fusion
  98.3 0.1 pad_add_fusion.source
  98.4 0.1 slice_reduce_fusion
  98.5 3.4 %collective-permute-done.23.refs_23_ = bf16[2,528,384]{2,1,0:T(8,128)(2,1)} collective-permute-done((bf16[2,528,384]{2,1,0:T(8,128)(2,1)}, bf16[2,528,384]{2,1,0:T(8,128)(2,1)}, u32[]{:S(2)}, u32[]{:S(2)}) %collective-permute-start.23) | collective-permute-done | bytes 811040 | tf_op jit(solution)/shard_map/ppermute | solution.py:30
  102.0 23.1 %shard_map.55 = f32[3,4,256,128]{3,2,1,0:T(8,128)} custom-call(s32[3]{0:T(128)S(1)} %and_select_fusion.shift, s32[32]{0:T(128)S(1)} %pad_add_fusion.source, bf16[4,256,384]{2,1,0:T(8,128)(2,1)} %copy-done.2, bf16[4,256,384]{2,1,0:T(8,128)(2,1)} %copy-done.11, bf16[4,256,384]{2,1,0:T(8,128)(2,1)} %copy-done.9, bf16[4,256,384]{2,1,0:T(8,128)(2,1)} %copy-done.13, ...), custom_call_target="tpu_custom_call" | custom-call | tf_op jit(solution)/shard_map/pallas_call | solution.py:111
  (53 shorter events, 0.2 us)
Async XLA Ops:
  0.0 2.1 %copy-start.16 = (bf16[4,256]{1,0:T(4,128)(2,1)S(1)}, bf16[4,256]{1,0:T(4,128)(2,1)}, u32[]{:S(2)}) copy-start(bf16[4,256]{1,0:T(4,128)(2,1)} %param.8) | copy-start | bytes 6148
  0.0 2.1 %copy-start.18 = (bf16[4,128]{1,0:T(4,128)(2,1)S(1)}, bf16[4,128]{1,0:T(4,128)(2,1)}, u32[]{:S(2)}) copy-start(bf16[4,128]{1,0:T(4,128)(2,1)} %param.7) | copy-start | bytes 3076
  2.1 2.4 %copy-start.3 = (bf16[4,256,128]{2,1,0:T(8,128)(2,1)S(1)}, bf16[4,256,128]{2,1,0:T(8,128)(2,1)}, u32[]{:S(2)}) copy-start(bf16[4,256,128]{2,1,0:T(8,128)(2,1)} %param.5) | copy-start | bytes 786436
  2.3 29.8 %copy-start.1 = (bf16[4,256,256]{2,1,0:T(8,128)(2,1)S(1)}, bf16[4,256,256]{2,1,0:T(8,128)(2,1)}, u32[]{:S(2)}) copy-start(bf16[4,256,256]{2,1,0:T(8,128)(2,1)} %param.6) | copy-start | bytes 1572868
  2.4 2.9 %collective-permute-start.8 = (bf16[528,384]{1,0:T(8,128)(2,1)S(1)}, bf16[528,384]{1,0:T(8,128)(2,1)S(1)}, u32[]{:S(2)}, u32[]{:S(2)}) collective-permute-start(bf16[528,384]{1,0:T(8,128)(2,1)S(1)} %get-tuple-element.17), channel_id=1, source_target_pairs={{0,8},{1,24},{2,42},{3,58},{4,76},{5,92},{6,110},{7,126},{8,0},{9,... | collective-permute-start | bytes 1216520 | tf_op jit(solution)/shard_map/ppermute | solution.py:30
  3.9 1.4 %collective-permute-start.7 = (bf16[528,384]{1,0:T(8,128)(2,1)S(1)}, bf16[528,384]{1,0:T(8,128)(2,1)S(1)}, u32[]{:S(2)}, u32[]{:S(2)}) collective-permute-start(bf16[528,384]{1,0:T(8,128)(2,1)S(1)} %get-tuple-element.18), channel_id=1, source_target_pairs={{0,0},{1,16},{2,34},{3,50},{4,68},{5,84},{6,102},{7,118},{8,8},{9,... | collective-permute-start | bytes 1216520 | tf_op jit(solution)/shard_map/ppermute | solution.py:30
  5.2 93.1 %copy-start.17 = (s32[3,64]{1,0:T(4,128)S(1)}, s32[3,64]{1,0:T(4,128)}, u32[]{:S(2)}) copy-start(s32[3,64]{1,0:T(4,128)} %param.9) | copy-start | bytes 2308
  5.3 96.6 %copy-start = (bf16[2,528,384]{2,1,0:T(8,128)(2,1)}, bf16[2,528,384]{2,1,0:T(8,128)(2,1)S(1)}, u32[]{:S(2)}) copy-start(bf16[2,528,384]{2,1,0:T(8,128)(2,1)S(1)} %pad_maximum_fusion.refs_16_) | copy-start | bytes 2433028
  5.3 40.6 %collective-permute-start.18 = (bf16[2,528,384]{2,1,0:T(8,128)(2,1)S(1)}, bf16[2,528,384]{2,1,0:T(8,128)(2,1)S(1)}, u32[]{:S(2)}, u32[]{:S(2)}) collective-permute-start(bf16[2,528,384]{2,1,0:T(8,128)(2,1)S(1)} %pad_maximum_fusion.refs_16_), channel_id=1, source_target_pairs={{0,2},{1,3},{2,4},{3,5},{4,6},{5,7},{6,0},{7,1},{8,14},{9,15},{10,... | collective-permute-start | bytes 2433032 | tf_op jit(solution)/shard_map/ppermute | solution.py:30
  29.9 17.7 %collective-permute-start.9 = (bf16[2,528,384]{2,1,0:T(8,128)(2,1)S(1)}, bf16[2,528,384]{2,1,0:T(8,128)(2,1)S(1)}, u32[]{:S(2)}, u32[]{:S(2)}) collective-permute-start(bf16[2,528,384]{2,1,0:T(8,128)(2,1)S(1)} %pad_maximum_fusion.refs_16_), channel_id=1, source_target_pairs={{0,1},{1,0},{2,3},{3,2},{4,5},{5,4},{6,7},{7,6},{8,9},{9,8},{10,11... | collective-permute-start | bytes 2433032 | tf_op jit(solution)/shard_map/ppermute | solution.py:30
  32.1 69.9 %copy-start.2 = (bf16[4,256,384]{2,1,0:T(8,128)(2,1)}, bf16[4,256,384]{2,1,0:T(8,128)(2,1)S(1)}, u32[]{:S(2)}) copy-start(bf16[4,256,384]{2,1,0:T(8,128)(2,1)S(1)} %constant_dynamic-update-slice_fusion.refs_0_) | copy-start | bytes 2359300
  32.1 11.2 %collective-permute-start.1 = (bf16[4,256,384]{2,1,0:T(8,128)(2,1)S(1)}, bf16[4,256,384]{2,1,0:T(8,128)(2,1)S(1)}, u32[]{:S(2)}, u32[]{:S(2)}) collective-permute-start(bf16[4,256,384]{2,1,0:T(8,128)(2,1)S(1)} %constant_dynamic-update-slice_fusion.refs_0_), channel_id=1, source_target_pairs={{0,32},{1,33},{2,34},{3,35},{4,36},{5,37},{6,38},{7,39},{8,104},{9... | collective-permute-start | bytes 2359304 | tf_op jit(solution)/shard_map/ppermute | solution.py:30
  43.3 52.9 %copy-start.9 = (bf16[4,256,384]{2,1,0:T(8,128)(2,1)}, bf16[4,256,384]{2,1,0:T(8,128)(2,1)S(1)}, u32[]{:S(2)}) copy-start(bf16[4,256,384]{2,1,0:T(8,128)(2,1)S(1)} %collective-permute-done.1.refs_2_) | copy-start | bytes 2359300
  43.3 11.5 %collective-permute-start.3 = (bf16[4,256,384]{2,1,0:T(8,128)(2,1)S(1)}, bf16[4,256,384]{2,1,0:T(8,128)(2,1)S(1)}, u32[]{:S(2)}, u32[]{:S(2)}) collective-permute-start(bf16[4,256,384]{2,1,0:T(8,128)(2,1)S(1)} %collective-permute-done.1.refs_2_), channel_id=1, source_target_pairs={{0,32},{1,33},{2,34},{3,35},{4,36},{5,37},{6,38},{7,39},{8,104},{9... | collective-permute-start | bytes 2359304 | tf_op jit(solution)/shard_map/ppermute | solution.py:30
  45.9 56.1 %copy-start.4 = (bf16[2,528,384]{2,1,0:T(8,128)(2,1)}, bf16[2,528,384]{2,1,0:T(8,128)(2,1)S(1)}, u32[]{:S(2)}) copy-start(bf16[2,528,384]{2,1,0:T(8,128)(2,1)S(1)} %collective-permute-done.18.refs_17_) | copy-start | bytes 2433028
  45.9 23.0 %collective-permute-start.19 = (bf16[2,528,384]{2,1,0:T(8,128)(2,1)S(1)}, bf16[2,528,384]{2,1,0:T(8,128)(2,1)S(1)}, u32[]{:S(2)}, u32[]{:S(2)}) collective-permute-start(bf16[2,528,384]{2,1,0:T(8,128)(2,1)S(1)} %collective-permute-done.18.refs_17_), channel_id=1, source_target_pairs={{0,2},{1,3},{2,4},{3,5},{4,6},{5,7},{6,0},{7,1},{8,14},{9,15},{10,... | collective-permute-start | bytes 2433032 | tf_op jit(solution)/shard_map/ppermute | solution.py:30
  46.0 12.3 %collective-permute-start = (bf16[4,256,384]{2,1,0:T(8,128)(2,1)S(1)}, bf16[4,256,384]{2,1,0:T(8,128)(2,1)S(1)}, u32[]{:S(2)}, u32[]{:S(2)}) collective-permute-start(bf16[4,256,384]{2,1,0:T(8,128)(2,1)S(1)} %constant_dynamic-update-slice_fusion.refs_0_), channel_id=1, source_target_pairs={{0,8},{1,9},{2,10},{3,11},{4,12},{5,13},{6,14},{7,15},{8,0},{9,1},... | collective-permute-start | bytes 2359304 | tf_op jit(solution)/shard_map/ppermute | solution.py:30
  47.6 54.4 %copy-start.5 = (bf16[2,528,384]{2,1,0:T(8,128)(2,1)}, bf16[2,528,384]{2,1,0:T(8,128)(2,1)S(1)}, u32[]{:S(2)}) copy-start(bf16[2,528,384]{2,1,0:T(8,128)(2,1)S(1)} %collective-permute-done.9.refs_20_) | copy-start | bytes 2433028
  47.6 21.0 %collective-permute-start.10 = (bf16[4,256,384]{2,1,0:T(8,128)(2,1)S(1)}, bf16[4,256,384]{2,1,0:T(8,128)(2,1)S(1)}, u32[]{:S(2)}, u32[]{:S(2)}) collective-permute-start(bf16[4,256,384]{2,1,0:T(8,128)(2,1)S(1)} %constant_dynamic-update-slice_fusion.refs_0_), channel_id=1, source_target_pairs={{0,16},{1,17},{2,18},{3,19},{4,20},{5,21},{6,22},{7,23},{8,24},{9,... | collective-permute-start | bytes 2359304 | tf_op jit(solution)/shard_map/ppermute | solution.py:30
  51.2 21.9 %collective-permute-start.21 = (bf16[2,528,384]{2,1,0:T(8,128)(2,1)S(1)}, bf16[2,528,384]{2,1,0:T(8,128)(2,1)S(1)}, u32[]{:S(2)}, u32[]{:S(2)}) collective-permute-start(bf16[2,528,384]{2,1,0:T(8,128)(2,1)S(1)} %collective-permute-done.9.refs_20_), channel_id=1, source_target_pairs={{0,2},{1,3},{2,4},{3,5},{4,6},{5,7},{6,0},{7,1},{8,14},{9,15},{10,... | collective-permute-start | bytes 2433032 | tf_op jit(solution)/shard_map/ppermute | solution.py:30
  54.8 42.6 %copy-start.10 = (bf16[4,256,384]{2,1,0:T(8,128)(2,1)}, bf16[4,256,384]{2,1,0:T(8,128)(2,1)S(1)}, u32[]{:S(2)}) copy-start(bf16[4,256,384]{2,1,0:T(8,128)(2,1)S(1)} %collective-permute-done.3.refs_4_) | copy-start | bytes 2359300
  54.8 18.5 %collective-permute-start.5 = (bf16[4,256,384]{2,1,0:T(8,128)(2,1)S(1)}, bf16[4,256,384]{2,1,0:T(8,128)(2,1)}, u32[]{:S(2)}, u32[]{:S(2)}) collective-permute-start(bf16[4,256,384]{2,1,0:T(8,128)(2,1)S(1)} %collective-permute-done.3.refs_4_), channel_id=1, source_target_pairs={{0,32},{1,33},{2,34},{3,35},{4,36},{5,37},{6,38},{7,39},{8,104},{9... | collective-permute-start | bytes 2359304 | tf_op jit(solution)/shard_map/ppermute | solution.py:30
  58.3 15.1 %copy-start.11 = (bf16[4,256,384]{2,1,0:T(8,128)(2,1)}, bf16[4,256,384]{2,1,0:T(8,128)(2,1)S(1)}, u32[]{:S(2)}) copy-start(bf16[4,256,384]{2,1,0:T(8,128)(2,1)S(1)} %collective-permute-done.refs_1_) | copy-start | bytes 2359300
  58.3 17.3 %collective-permute-start.2 = (bf16[4,256,384]{2,1,0:T(8,128)(2,1)S(1)}, bf16[4,256,384]{2,1,0:T(8,128)(2,1)S(1)}, u32[]{:S(2)}, u32[]{:S(2)}) collective-permute-start(bf16[4,256,384]{2,1,0:T(8,128)(2,1)S(1)} %collective-permute-done.1.refs_2_), channel_id=1, source_target_pairs={{0,8},{1,9},{2,10},{3,11},{4,12},{5,13},{6,14},{7,15},{8,0},{9,1},... | collective-permute-start | bytes 2359304 | tf_op jit(solution)/shard_map/ppermute | solution.py:30
  68.6 28.9 %copy-start.12 = (bf16[4,256,384]{2,1,0:T(8,128)(2,1)}, bf16[4,256,384]{2,1,0:T(8,128)(2,1)S(1)}, u32[]{:S(2)}) copy-start(bf16[4,256,384]{2,1,0:T(8,128)(2,1)S(1)} %collective-permute-done.10.refs_8_) | copy-start | bytes 2359300
  68.6 7.0 %collective-permute-start.4 = (bf16[4,256,384]{2,1,0:T(8,128)(2,1)S(1)}, bf16[4,256,384]{2,1,0:T(8,128)(2,1)S(1)}, u32[]{:S(2)}, u32[]{:S(2)}) collective-permute-start(bf16[4,256,384]{2,1,0:T(8,128)(2,1)S(1)} %collective-permute-done.3.refs_4_), channel_id=1, source_target_pairs={{0,8},{1,9},{2,10},{3,11},{4,12},{5,13},{6,14},{7,15},{8,0},{9,1},... | collective-permute-start | bytes 2359304 | tf_op jit(solution)/shard_map/ppermute | solution.py:30
  68.9 4.4 %copy-start.6 = (bf16[2,528,384]{2,1,0:T(8,128)(2,1)}, bf16[2,528,384]{2,1,0:T(8,128)(2,1)S(1)}, u32[]{:S(2)}) copy-start(bf16[2,528,384]{2,1,0:T(8,128)(2,1)S(1)} %collective-permute-done.19.refs_18_) | copy-start | bytes 2433028
  68.9 13.1 %collective-permute-start.12 = (bf16[4,256,384]{2,1,0:T(8,128)(2,1)S(1)}, bf16[4,256,384]{2,1,0:T(8,128)(2,1)}, u32[]{:S(2)}, u32[]{:S(2)}) collective-permute-start(bf16[4,256,384]{2,1,0:T(8,128)(2,1)S(1)} %collective-permute-done.10.refs_8_), channel_id=1, source_target_pairs={{0,32},{1,33},{2,34},{3,35},{4,36},{5,37},{6,38},{7,39},{8,104},{9... | collective-permute-start | bytes 2359304 | tf_op jit(solution)/shard_map/ppermute | solution.py:30
  73.1 20.5 %copy-start.7 = (bf16[2,528,384]{2,1,0:T(8,128)(2,1)}, bf16[2,528,384]{2,1,0:T(8,128)(2,1)S(1)}, u32[]{:S(2)}) copy-start(bf16[2,528,384]{2,1,0:T(8,128)(2,1)S(1)} %collective-permute-done.21.refs_21_) | copy-start | bytes 2433028
  73.1 12.4 %collective-permute-start.22 = (bf16[2,528,384]{2,1,0:T(8,128)(2,1)S(1)}, bf16[2,528,384]{2,1,0:T(8,128)(2,1)}, u32[]{:S(2)}, u32[]{:S(2)}) collective-permute-start(bf16[2,528,384]{2,1,0:T(8,128)(2,1)S(1)} %collective-permute-done.21.refs_21_), channel_id=1, source_target_pairs={{0,2},{1,3},{2,4},{3,5},{4,6},{5,7},{6,0},{7,1},{8,14},{9,15},{10,... | collective-permute-start | bytes 2433032 | tf_op jit(solution)/shard_map/ppermute | solution.py:30
  73.3 20.2 %collective-permute-start.20 = (bf16[2,528,384]{2,1,0:T(8,128)(2,1)S(1)}, bf16[2,528,384]{2,1,0:T(8,128)(2,1)S(1)}, u32[]{:S(2)}, u32[]{:S(2)}) collective-permute-start(bf16[2,528,384]{2,1,0:T(8,128)(2,1)S(1)} %collective-permute-done.19.refs_18_), channel_id=1, source_target_pairs={{0,2},{1,3},{2,4},{3,5},{4,6},{5,7},{6,0},{7,1},{8,14},{9,15},{10,... | collective-permute-start | bytes 2433032 | tf_op jit(solution)/shard_map/ppermute | solution.py:30
  75.6 21.9 %copy-start.13 = (bf16[4,256,384]{2,1,0:T(8,128)(2,1)}, bf16[4,256,384]{2,1,0:T(8,128)(2,1)S(1)}, u32[]{:S(2)}) copy-start(bf16[4,256,384]{2,1,0:T(8,128)(2,1)S(1)} %collective-permute-done.2.refs_3_) | copy-start | bytes 2359300
  75.6 10.5 %collective-permute-start.11 = (bf16[4,256,384]{2,1,0:T(8,128)(2,1)S(1)}, bf16[4,256,384]{2,1,0:T(8,128)(2,1)S(1)}, u32[]{:S(2)}, u32[]{:S(2)}) collective-permute-start(bf16[4,256,384]{2,1,0:T(8,128)(2,1)S(1)} %collective-permute-done.10.refs_8_), channel_id=1, source_target_pairs={{0,8},{1,9},{2,10},{3,11},{4,12},{5,13},{6,14},{7,15},{8,0},{9,1},... | collective-permute-start | bytes 2359304 | tf_op jit(solution)/shard_map/ppermute | solution.py:30
  75.6 21.9 %copy-start.14 = (bf16[4,256,384]{2,1,0:T(8,128)(2,1)}, bf16[4,256,384]{2,1,0:T(8,128)(2,1)S(1)}, u32[]{:S(2)}) copy-start(bf16[4,256,384]{2,1,0:T(8,128)(2,1)S(1)} %collective-permute-done.4.refs_5_) | copy-start | bytes 2359300
  75.6 20.6 %collective-permute-start.16 = (bf16[4,256,384]{2,1,0:T(8,128)(2,1)}, bf16[4,256,384]{2,1,0:T(8,128)(2,1)}, u32[]{:S(2)}, u32[]{:S(2)}) collective-permute-start(bf16[4,256,384]{2,1,0:T(8,128)(2,1)} %collective-permute-done.5.refs_6_), channel_id=1, source_target_pairs={{0,16},{1,17},{2,18},{3,19},{4,20},{5,21},{6,22},{7,23},{8,24},{9,... | collective-permute-start | bytes 2359304 | tf_op jit(solution)/shard_map/ppermute | solution.py:30
  82.0 15.4 %collective-permute-start.14 = (bf16[4,256,384]{2,1,0:T(8,128)(2,1)}, bf16[4,256,384]{2,1,0:T(8,128)(2,1)}, u32[]{:S(2)}, u32[]{:S(2)}) collective-permute-start(bf16[4,256,384]{2,1,0:T(8,128)(2,1)} %collective-permute-done.12.refs_10_), channel_id=1, source_target_pairs={{0,32},{1,33},{2,34},{3,35},{4,36},{5,37},{6,38},{7,39},{8,104},{9... | collective-permute-start | bytes 2359304 | tf_op jit(solution)/shard_map/ppermute | solution.py:30
  85.5 16.4 %collective-permute-start.23 = (bf16[2,528,384]{2,1,0:T(8,128)(2,1)}, bf16[2,528,384]{2,1,0:T(8,128)(2,1)}, u32[]{:S(2)}, u32[]{:S(2)}) collective-permute-start(bf16[2,528,384]{2,1,0:T(8,128)(2,1)} %collective-permute-done.22.refs_22_), channel_id=1, source_target_pairs={{0,2},{1,3},{2,4},{3,5},{4,6},{5,7},{6,0},{7,1},{8,14},{9,15},{10,... | collective-permute-start | bytes 2433032 | tf_op jit(solution)/shard_map/ppermute | solution.py:30
  86.1 11.4 %copy-start.15 = (bf16[4,256,384]{2,1,0:T(8,128)(2,1)}, bf16[4,256,384]{2,1,0:T(8,128)(2,1)S(1)}, u32[]{:S(2)}) copy-start(bf16[4,256,384]{2,1,0:T(8,128)(2,1)S(1)} %collective-permute-done.11.refs_9_) | copy-start | bytes 2359300
  86.1 12.4 %collective-permute-start.6 = (bf16[4,256,384]{2,1,0:T(8,128)(2,1)}, bf16[4,256,384]{2,1,0:T(8,128)(2,1)}, u32[]{:S(2)}, u32[]{:S(2)}) collective-permute-start(bf16[4,256,384]{2,1,0:T(8,128)(2,1)} %collective-permute-done.5.refs_6_), channel_id=1, source_target_pairs={{0,8},{1,9},{2,10},{3,11},{4,12},{5,13},{6,14},{7,15},{8,0},{9,1},... | collective-permute-start | bytes 2359304 | tf_op jit(solution)/shard_map/ppermute | solution.py:30
  93.6 0.9 copy-start.8
  93.6 4.9 %collective-permute-start.13 = (bf16[4,256,384]{2,1,0:T(8,128)(2,1)}, bf16[4,256,384]{2,1,0:T(8,128)(2,1)}, u32[]{:S(2)}, u32[]{:S(2)}) collective-permute-start(bf16[4,256,384]{2,1,0:T(8,128)(2,1)} %collective-permute-done.12.refs_10_), channel_id=1, source_target_pairs={{0,8},{1,9},{2,10},{3,11},{4,12},{5,13},{6,14},{7,15},{8,0},{9,1},... | collective-permute-start | bytes 2359304 | tf_op jit(solution)/shard_map/ppermute | solution.py:30
  96.2 5.8 %collective-permute-start.17 = (bf16[4,256,384]{2,1,0:T(8,128)(2,1)}, bf16[4,256,384]{2,1,0:T(8,128)(2,1)}, u32[]{:S(2)}, u32[]{:S(2)}) collective-permute-start(bf16[4,256,384]{2,1,0:T(8,128)(2,1)} %collective-permute-done.16.refs_14_), channel_id=1, source_target_pairs={{0,8},{1,9},{2,10},{3,11},{4,12},{5,13},{6,14},{7,15},{8,0},{9,1},... | collective-permute-start | bytes 2359304 | tf_op jit(solution)/shard_map/ppermute | solution.py:30
  97.5 4.5 %collective-permute-start.15 = (bf16[4,256,384]{2,1,0:T(8,128)(2,1)}, bf16[4,256,384]{2,1,0:T(8,128)(2,1)}, u32[]{:S(2)}, u32[]{:S(2)}) collective-permute-start(bf16[4,256,384]{2,1,0:T(8,128)(2,1)} %collective-permute-done.14.refs_12_), channel_id=1, source_target_pairs={{0,8},{1,9},{2,10},{3,11},{4,12},{5,13},{6,14},{7,15},{8,0},{9,1},... | collective-permute-start | bytes 2359304 | tf_op jit(solution)/shard_map/ppermute | solution.py:30

commit v6 on v5

--- a/solution.py
+++ b/solution.py
@@ -167,12 +167,12 @@
         rows_same.append(z_step(rows_same[-1], 1))
         cols_same.append(x_step(cols_same[-1], 1))
     rows_cross = [across_yh(after(own, cols_cross[0]))]
-    cols_cross.append(x_step(after(cols_cross[0], cols_same[1]), 1))
+    cols_cross.append(x_step(cols_cross[0], 1))
     rows_cross.append(z_step(rows_cross[0], 1))
     cols_cross += [x_step(cols_cross[1], 1)]
     cols_cross += [x_step(cols_cross[2], 1)]
     rows_cross += [z_step(rows_cross[1], 1)]
-    rows_cross += [across_yh(after(rows_same[3], rows_cross[0]))]
+    rows_cross += [across_yh(rows_same[3])]
 
     def slab(at, low, core):
         return at % 4 * 4 + low * 2 + core

time: 125 us -> 124 us (level)
  waiting for transfers between devices: 37 us -> 34.6 us
    ppermute x24, waiting for transfers between devices: 37 us -> 34.6 us  [send(): return lax.ppermute(block, AXES, routes(target))]
  transfers between devices with their start and end apart: 24 -> 24, of which waited for: 9 -> 8; matrix products, arithmetic and copies ran while one was open for 0% -> 0% of each run, Pallas kernels for 0% -> 0%
where the time goes in v6:
time: 124 us
  starting transfers between devices  60.7 us (49%)
  waiting for transfers between devices  34.6 us (28%)
  Pallas kernels  23.1 us (19%)
  local copies, waits for them, and re-layouts  4.27 us (3%)
    ppermute x24, starting transfers between devices, send(): return lax.ppermute(block, AXES, routes(target))  60.7 us
    ppermute x24, waiting for transfers between devices, send(): return lax.ppermute(block, AXES, routes(target))  34.6 us
    pallas_call x1, Pallas kernels, polarizability(): pl.pallas_call(kernel, in_specs=[scalars, scalars] + [anywhere] * 24, out...  23.1 us
  transfers between devices with their start and end apart: 24, of which 8 were waited for; matrix products, arithmetic and copies ran while one was open for 0% of the time, Pallas kernels for 0%

profile of v6, /device:TPU:1, one launch (start us, length us, event | category | flops | bytes accessed | tf_op | source)
XLA Modules:
  0.0 123.6 jit_solution(5627093287009545012)
XLA Ops:
  0.0 1.0 constant_dynamic-slice_fusion.1
  1.0 1.1 constant_dynamic-slice_fusion
  2.1 0.0 copy-start.3
  2.1 0.1 pad_maximum_fusion.3
  2.3 0.0 copy-start.1
  2.3 0.1 pad_maximum_fusion.1
  2.4 1.5 %collective-permute-start.8 = (bf16[528,384]{1,0:T(8,128)(2,1)S(1)}, bf16[528,384]{1,0:T(8,128)(2,1)S(1)}, u32[]{:S(2)}, u32[]{:S(2)}) collective-permute-start(bf16[528,384]{1,0:T(8,128)(2,1)S(1)} %get-tuple-element.13), channel_id=1, source_target_pairs={{0,8},{1,24},{2,42},{3,58},{4,76},{5,92},{6,110},{7,126},{8,0},{9,... | collective-permute-start | bytes 1216520 | tf_op jit(solution)/shard_map/ppermute | solution.py:30
  3.9 0.7 collective-permute-start.7
  4.6 0.6 collective-permute-done.8
  5.2 0.1 pad_maximum_fusion.refs_16_
  5.3 19.9 %collective-permute-start.9 = (bf16[2,528,384]{2,1,0:T(8,128)(2,1)S(1)}, bf16[2,528,384]{2,1,0:T(8,128)(2,1)S(1)}, u32[]{:S(2)}, u32[]{:S(2)}) collective-permute-start(bf16[2,528,384]{2,1,0:T(8,128)(2,1)S(1)} %pad_maximum_fusion.refs_16_), channel_id=1, source_target_pairs={{0,1},{1,0},{2,3},{3,2},{4,5},{5,4},{6,7},{7,6},{8,9},{9,8},{10,11... | collective-permute-start | bytes 2433032 | tf_op jit(solution)/shard_map/ppermute | solution.py:30
  25.3 8.5 %collective-permute-start.1 = (bf16[4,256,384]{2,1,0:T(8,128)(2,1)S(1)}, bf16[4,256,384]{2,1,0:T(8,128)(2,1)S(1)}, u32[]{:S(2)}, u32[]{:S(2)}) collective-permute-start(bf16[4,256,384]{2,1,0:T(8,128)(2,1)S(1)} %constant_dynamic-update-slice_fusion.refs_0_), channel_id=1, source_target_pairs={{0,32},{1,33},{2,34},{3,35},{4,36},{5,37},{6,38},{7,39},{8,104},{9... | collective-permute-start | bytes 2359304 | tf_op jit(solution)/shard_map/ppermute | solution.py:30
  33.8 0.1 collective-permute-start.18
  33.9 8.9 %collective-permute-done.1.refs_2_ = bf16[4,256,384]{2,1,0:T(8,128)(2,1)S(1)} collective-permute-done((bf16[4,256,384]{2,1,0:T(8,128)(2,1)S(1)}, bf16[4,256,384]{2,1,0:T(8,128)(2,1)S(1)}, u32[]{:S(2)}, u32[]{:S(2)}) %collective-permute-start.1) | collective-permute-done | bytes 786464 | tf_op jit(solution)/shard_map/ppermute | solution.py:30
  42.7 3.4 %collective-permute-start.3 = (bf16[4,256,384]{2,1,0:T(8,128)(2,1)S(1)}, bf16[4,256,384]{2,1,0:T(8,128)(2,1)S(1)}, u32[]{:S(2)}, u32[]{:S(2)}) collective-permute-start(bf16[4,256,384]{2,1,0:T(8,128)(2,1)S(1)} %collective-permute-done.1.refs_2_), channel_id=1, source_target_pairs={{0,32},{1,33},{2,34},{3,35},{4,36},{5,37},{6,38},{7,39},{8,104},{9... | collective-permute-start | bytes 2359304 | tf_op jit(solution)/shard_map/ppermute | solution.py:30
  46.1 0.0 collective-permute-start.2
  46.1 0.0 collective-permute-done.9.refs_20_
  46.1 1.8 %collective-permute-start.10 = (bf16[4,256,384]{2,1,0:T(8,128)(2,1)S(1)}, bf16[4,256,384]{2,1,0:T(8,128)(2,1)S(1)}, u32[]{:S(2)}, u32[]{:S(2)}) collective-permute-start(bf16[4,256,384]{2,1,0:T(8,128)(2,1)S(1)} %constant_dynamic-update-slice_fusion.refs_0_), channel_id=1, source_target_pairs={{0,16},{1,17},{2,18},{3,19},{4,20},{5,21},{6,22},{7,23},{8,24},{9,... | collective-permute-start | bytes 2359304 | tf_op jit(solution)/shard_map/ppermute | solution.py:30
  47.9 5.0 %collective-permute-start.21 = (bf16[2,528,384]{2,1,0:T(8,128)(2,1)S(1)}, bf16[2,528,384]{2,1,0:T(8,128)(2,1)S(1)}, u32[]{:S(2)}, u32[]{:S(2)}) collective-permute-start(bf16[2,528,384]{2,1,0:T(8,128)(2,1)S(1)} %collective-permute-done.9.refs_20_), channel_id=1, source_target_pairs={{0,2},{1,3},{2,4},{3,5},{4,6},{5,7},{6,0},{7,1},{8,14},{9,15},{10,... | collective-permute-start | bytes 2433032 | tf_op jit(solution)/shard_map/ppermute | solution.py:30
  52.9 0.0 collective-permute-done.18.refs_17_
  52.9 1.1 collective-permute-start.19
  54.1 1.0 collective-permute-done.3.refs_4_
  55.1 3.4 %collective-permute-start.5 = (bf16[4,256,384]{2,1,0:T(8,128)(2,1)S(1)}, bf16[4,256,384]{2,1,0:T(8,128)(2,1)}, u32[]{:S(2)}, u32[]{:S(2)}) collective-permute-start(bf16[4,256,384]{2,1,0:T(8,128)(2,1)S(1)} %collective-permute-done.3.refs_4_), channel_id=1, source_target_pairs={{0,32},{1,33},{2,34},{3,35},{4,36},{5,37},{6,38},{7,39},{8,104},{9... | collective-permute-start | bytes 2359304 | tf_op jit(solution)/shard_map/ppermute | solution.py:30
  58.5 0.0 collective-permute-done.2.refs_3_
  58.5 0.0 collective-permute-start.4
  58.5 7.9 %collective-permute-done.10.refs_8_ = bf16[4,256,384]{2,1,0:T(8,128)(2,1)S(1)} collective-permute-done((bf16[4,256,384]{2,1,0:T(8,128)(2,1)S(1)}, bf16[4,256,384]{2,1,0:T(8,128)(2,1)S(1)}, u32[]{:S(2)}, u32[]{:S(2)}) %collective-permute-start.10) | collective-permute-done | bytes 786464 | tf_op jit(solution)/shard_map/ppermute | solution.py:30
  66.4 5.0 %collective-permute-start.12 = (bf16[4,256,384]{2,1,0:T(8,128)(2,1)S(1)}, bf16[4,256,384]{2,1,0:T(8,128)(2,1)}, u32[]{:S(2)}, u32[]{:S(2)}) collective-permute-start(bf16[4,256,384]{2,1,0:T(8,128)(2,1)S(1)} %collective-permute-done.10.refs_8_), channel_id=1, source_target_pairs={{0,32},{1,33},{2,34},{3,35},{4,36},{5,37},{6,38},{7,39},{8,104},{9... | collective-permute-start | bytes 2359304 | tf_op jit(solution)/shard_map/ppermute | solution.py:30
  71.4 0.1 collective-permute-start.22
  71.5 0.8 copy-done.6
  72.3 1.7 %collective-permute-start.20 = (bf16[2,528,384]{2,1,0:T(8,128)(2,1)S(1)}, bf16[2,528,384]{2,1,0:T(8,128)(2,1)S(1)}, u32[]{:S(2)}, u32[]{:S(2)}) collective-permute-start(bf16[2,528,384]{2,1,0:T(8,128)(2,1)S(1)} %collective-permute-done.19.refs_18_), channel_id=1, source_target_pairs={{0,2},{1,3},{2,4},{3,5},{4,6},{5,7},{6,0},{7,1},{8,14},{9,15},{10,... | collective-permute-start | bytes 2433032 | tf_op jit(solution)/shard_map/ppermute | solution.py:30
  74.0 0.1 collective-permute-start.11
  74.0 1.7 %collective-permute-start.16 = (bf16[4,256,384]{2,1,0:T(8,128)(2,1)}, bf16[4,256,384]{2,1,0:T(8,128)(2,1)}, u32[]{:S(2)}, u32[]{:S(2)}) collective-permute-start(bf16[4,256,384]{2,1,0:T(8,128)(2,1)} %collective-permute-done.5.refs_6_), channel_id=1, source_target_pairs={{0,16},{1,17},{2,18},{3,19},{4,20},{5,21},{6,22},{7,23},{8,24},{9,... | collective-permute-start | bytes 2359304 | tf_op jit(solution)/shard_map/ppermute | solution.py:30
  75.7 4.6 %collective-permute-done.12.refs_10_ = bf16[4,256,384]{2,1,0:T(8,128)(2,1)} collective-permute-done((bf16[4,256,384]{2,1,0:T(8,128)(2,1)S(1)}, bf16[4,256,384]{2,1,0:T(8,128)(2,1)}, u32[]{:S(2)}, u32[]{:S(2)}) %collective-permute-start.12) | collective-permute-done | bytes 786464 | tf_op jit(solution)/shard_map/ppermute | solution.py:30
  80.3 3.5 %collective-permute-start.14 = (bf16[4,256,384]{2,1,0:T(8,128)(2,1)}, bf16[4,256,384]{2,1,0:T(8,128)(2,1)}, u32[]{:S(2)}, u32[]{:S(2)}) collective-permute-start(bf16[4,256,384]{2,1,0:T(8,128)(2,1)} %collective-permute-done.12.refs_10_), channel_id=1, source_target_pairs={{0,32},{1,33},{2,34},{3,35},{4,36},{5,37},{6,38},{7,39},{8,104},{9... | collective-permute-start | bytes 2359304 | tf_op jit(solution)/shard_map/ppermute | solution.py:30
  83.8 0.3 collective-permute-start.23
  84.2 7.4 %collective-permute-done.20.refs_19_ = bf16[2,528,384]{2,1,0:T(8,128)(2,1)S(1)} collective-permute-done((bf16[2,528,384]{2,1,0:T(8,128)(2,1)S(1)}, bf16[2,528,384]{2,1,0:T(8,128)(2,1)S(1)}, u32[]{:S(2)}, u32[]{:S(2)}) %collective-permute-start.20) | collective-permute-done | bytes 811040 | tf_op jit(solution)/shard_map/ppermute | solution.py:30
  91.6 0.9 copy-done.8
  92.5 0.5 collective-permute-start.13
  93.0 1.6 %collective-permute-done.16.refs_14_ = bf16[4,256,384]{2,1,0:T(8,128)(2,1)} collective-permute-done((bf16[4,256,384]{2,1,0:T(8,128)(2,1)}, bf16[4,256,384]{2,1,0:T(8,128)(2,1)}, u32[]{:S(2)}, u32[]{:S(2)}) %collective-permute-start.16) | collective-permute-done | bytes 786464 | tf_op jit(solution)/shard_map/ppermute | solution.py:30
  94.6 1.3 %collective-permute-start.17 = (bf16[4,256,384]{2,1,0:T(8,128)(2,1)}, bf16[4,256,384]{2,1,0:T(8,128)(2,1)}, u32[]{:S(2)}, u32[]{:S(2)}) collective-permute-start(bf16[4,256,384]{2,1,0:T(8,128)(2,1)} %collective-permute-done.16.refs_14_), channel_id=1, source_target_pairs={{0,8},{1,9},{2,10},{3,11},{4,12},{5,13},{6,14},{7,15},{8,0},{9,1},... | collective-permute-start | bytes 2359304 | tf_op jit(solution)/shard_map/ppermute | solution.py:30
  95.9 1.2 %collective-permute-start.15 = (bf16[4,256,384]{2,1,0:T(8,128)(2,1)}, bf16[4,256,384]{2,1,0:T(8,128)(2,1)}, u32[]{:S(2)}, u32[]{:S(2)}) collective-permute-start(bf16[4,256,384]{2,1,0:T(8,128)(2,1)} %collective-permute-done.14.refs_12_), channel_id=1, source_target_pairs={{0,8},{1,9},{2,10},{3,11},{4,12},{5,13},{6,14},{7,15},{8,0},{9,1},... | collective-permute-start | bytes 2359304 | tf_op jit(solution)/shard_map/ppermute | solution.py:30
  97.1 0.1 stack.127
  97.2 0.1 stack.144
  97.3 0.1 select_reduce_fusion
  97.4 0.1 pad_add_fusion.source
  97.5 0.1 slice_reduce_fusion
  97.6 2.7 %collective-permute-done.23.refs_23_ = bf16[2,528,384]{2,1,0:T(8,128)(2,1)} collective-permute-done((bf16[2,528,384]{2,1,0:T(8,128)(2,1)}, bf16[2,528,384]{2,1,0:T(8,128)(2,1)}, u32[]{:S(2)}, u32[]{:S(2)}) %collective-permute-start.23) | collective-permute-done | bytes 811040 | tf_op jit(solution)/shard_map/ppermute | solution.py:30
  100.3 23.1 %shard_map.55 = f32[3,4,256,128]{3,2,1,0:T(8,128)} custom-call(s32[3]{0:T(128)S(1)} %and_select_fusion.shift, s32[32]{0:T(128)S(1)} %pad_add_fusion.source, bf16[4,256,384]{2,1,0:T(8,128)(2,1)} %copy-done.2, bf16[4,256,384]{2,1,0:T(8,128)(2,1)} %collective-permute-done.refs_1_, bf16[4,256,384]{2,1,0:T(8,128)(2,1)} %copy-done.9, ...), custom_call_target="tpu_custom_call" | custom-call | tf_op jit(solution)/shard_map/pallas_call | solution.py:111
  (51 shorter events, 0.2 us)
Async XLA Ops:
  0.0 2.1 %copy-start.15 = (bf16[4,256]{1,0:T(4,128)(2,1)S(1)}, bf16[4,256]{1,0:T(4,128)(2,1)}, u32[]{:S(2)}) copy-start(bf16[4,256]{1,0:T(4,128)(2,1)} %param.8) | copy-start | bytes 6148
  0.0 2.1 %copy-start.17 = (bf16[4,128]{1,0:T(4,128)(2,1)S(1)}, bf16[4,128]{1,0:T(4,128)(2,1)}, u32[]{:S(2)}) copy-start(bf16[4,128]{1,0:T(4,128)(2,1)} %param.7) | copy-start | bytes 3076
  2.1 2.4 %copy-start.3 = (bf16[4,256,128]{2,1,0:T(8,128)(2,1)S(1)}, bf16[4,256,128]{2,1,0:T(8,128)(2,1)}, u32[]{:S(2)}) copy-start(bf16[4,256,128]{2,1,0:T(8,128)(2,1)} %param.5) | copy-start | bytes 786436
  2.3 23.0 %copy-start.1 = (bf16[4,256,256]{2,1,0:T(8,128)(2,1)S(1)}, bf16[4,256,256]{2,1,0:T(8,128)(2,1)}, u32[]{:S(2)}) copy-start(bf16[4,256,256]{2,1,0:T(8,128)(2,1)} %param.6) | copy-start | bytes 1572868
  2.4 2.9 %collective-permute-start.8 = (bf16[528,384]{1,0:T(8,128)(2,1)S(1)}, bf16[528,384]{1,0:T(8,128)(2,1)S(1)}, u32[]{:S(2)}, u32[]{:S(2)}) collective-permute-start(bf16[528,384]{1,0:T(8,128)(2,1)S(1)} %get-tuple-element.13), channel_id=1, source_target_pairs={{0,8},{1,24},{2,42},{3,58},{4,76},{5,92},{6,110},{7,126},{8,0},{9,... | collective-permute-start | bytes 1216520 | tf_op jit(solution)/shard_map/ppermute | solution.py:30
  3.9 1.4 %collective-permute-start.7 = (bf16[528,384]{1,0:T(8,128)(2,1)S(1)}, bf16[528,384]{1,0:T(8,128)(2,1)S(1)}, u32[]{:S(2)}, u32[]{:S(2)}) collective-permute-start(bf16[528,384]{1,0:T(8,128)(2,1)S(1)} %get-tuple-element.14), channel_id=1, source_target_pairs={{0,0},{1,16},{2,34},{3,50},{4,68},{5,84},{6,102},{7,118},{8,8},{9,... | collective-permute-start | bytes 1216520 | tf_op jit(solution)/shard_map/ppermute | solution.py:30
  5.2 92.2 %copy-start.16 = (s32[3,64]{1,0:T(4,128)S(1)}, s32[3,64]{1,0:T(4,128)}, u32[]{:S(2)}) copy-start(s32[3,64]{1,0:T(4,128)} %param.9) | copy-start | bytes 2308
  5.3 95.0 %copy-start = (bf16[2,528,384]{2,1,0:T(8,128)(2,1)}, bf16[2,528,384]{2,1,0:T(8,128)(2,1)S(1)}, u32[]{:S(2)}) copy-start(bf16[2,528,384]{2,1,0:T(8,128)(2,1)S(1)} %pad_maximum_fusion.refs_16_) | copy-start | bytes 2433028
  5.3 40.8 %collective-permute-start.9 = (bf16[2,528,384]{2,1,0:T(8,128)(2,1)S(1)}, bf16[2,528,384]{2,1,0:T(8,128)(2,1)S(1)}, u32[]{:S(2)}, u32[]{:S(2)}) collective-permute-start(bf16[2,528,384]{2,1,0:T(8,128)(2,1)S(1)} %pad_maximum_fusion.refs_16_), channel_id=1, source_target_pairs={{0,1},{1,0},{2,3},{3,2},{4,5},{5,4},{6,7},{7,6},{8,9},{9,8},{10,11... | collective-permute-start | bytes 2433032 | tf_op jit(solution)/shard_map/ppermute | solution.py:30
  25.3 75.0 %copy-start.2 = (bf16[4,256,384]{2,1,0:T(8,128)(2,1)}, bf16[4,256,384]{2,1,0:T(8,128)(2,1)S(1)}, u32[]{:S(2)}) copy-start(bf16[4,256,384]{2,1,0:T(8,128)(2,1)S(1)} %constant_dynamic-update-slice_fusion.refs_0_) | copy-start | bytes 2359300
  25.3 17.4 %collective-permute-start.1 = (bf16[4,256,384]{2,1,0:T(8,128)(2,1)S(1)}, bf16[4,256,384]{2,1,0:T(8,128)(2,1)S(1)}, u32[]{:S(2)}, u32[]{:S(2)}) collective-permute-start(bf16[4,256,384]{2,1,0:T(8,128)(2,1)S(1)} %constant_dynamic-update-slice_fusion.refs_0_), channel_id=1, source_target_pairs={{0,32},{1,33},{2,34},{3,35},{4,36},{5,37},{6,38},{7,39},{8,104},{9... | collective-permute-start | bytes 2359304 | tf_op jit(solution)/shard_map/ppermute | solution.py:30
  33.8 19.2 %collective-permute-start.18 = (bf16[2,528,384]{2,1,0:T(8,128)(2,1)S(1)}, bf16[2,528,384]{2,1,0:T(8,128)(2,1)S(1)}, u32[]{:S(2)}, u32[]{:S(2)}) collective-permute-start(bf16[2,528,384]{2,1,0:T(8,128)(2,1)S(1)} %pad_maximum_fusion.refs_16_), channel_id=1, source_target_pairs={{0,2},{1,3},{2,4},{3,5},{4,6},{5,7},{6,0},{7,1},{8,14},{9,15},{10,... | collective-permute-start | bytes 2433032 | tf_op jit(solution)/shard_map/ppermute | solution.py:30
  33.8 14.1 %collective-permute-start = (bf16[4,256,384]{2,1,0:T(8,128)(2,1)S(1)}, bf16[4,256,384]{2,1,0:T(8,128)(2,1)}, u32[]{:S(2)}, u32[]{:S(2)}) collective-permute-start(bf16[4,256,384]{2,1,0:T(8,128)(2,1)S(1)} %constant_dynamic-update-slice_fusion.refs_0_), channel_id=1, source_target_pairs={{0,8},{1,9},{2,10},{3,11},{4,12},{5,13},{6,14},{7,15},{8,0},{9,1},... | collective-permute-start | bytes 2359304 | tf_op jit(solution)/shard_map/ppermute | solution.py:30
  42.7 28.8 %copy-start.9 = (bf16[4,256,384]{2,1,0:T(8,128)(2,1)}, bf16[4,256,384]{2,1,0:T(8,128)(2,1)S(1)}, u32[]{:S(2)}) copy-start(bf16[4,256,384]{2,1,0:T(8,128)(2,1)S(1)} %collective-permute-done.1.refs_2_) | copy-start | bytes 2359300
  42.7 12.3 %collective-permute-start.3 = (bf16[4,256,384]{2,1,0:T(8,128)(2,1)S(1)}, bf16[4,256,384]{2,1,0:T(8,128)(2,1)S(1)}, u32[]{:S(2)}, u32[]{:S(2)}) collective-permute-start(bf16[4,256,384]{2,1,0:T(8,128)(2,1)S(1)} %collective-permute-done.1.refs_2_), channel_id=1, source_target_pairs={{0,32},{1,33},{2,34},{3,35},{4,36},{5,37},{6,38},{7,39},{8,104},{9... | collective-permute-start | bytes 2359304 | tf_op jit(solution)/shard_map/ppermute | solution.py:30
  46.1 12.4 %collective-permute-start.2 = (bf16[4,256,384]{2,1,0:T(8,128)(2,1)S(1)}, bf16[4,256,384]{2,1,0:T(8,128)(2,1)S(1)}, u32[]{:S(2)}, u32[]{:S(2)}) collective-permute-start(bf16[4,256,384]{2,1,0:T(8,128)(2,1)S(1)} %collective-permute-done.1.refs_2_), channel_id=1, source_target_pairs={{0,8},{1,9},{2,10},{3,11},{4,12},{5,13},{6,14},{7,15},{8,0},{9,1},... | collective-permute-start | bytes 2359304 | tf_op jit(solution)/shard_map/ppermute | solution.py:30
  46.1 54.2 %copy-start.4 = (bf16[2,528,384]{2,1,0:T(8,128)(2,1)}, bf16[2,528,384]{2,1,0:T(8,128)(2,1)S(1)}, u32[]{:S(2)}) copy-start(bf16[2,528,384]{2,1,0:T(8,128)(2,1)S(1)} %collective-permute-done.9.refs_20_) | copy-start | bytes 2433028
  46.1 20.3 %collective-permute-start.10 = (bf16[4,256,384]{2,1,0:T(8,128)(2,1)S(1)}, bf16[4,256,384]{2,1,0:T(8,128)(2,1)S(1)}, u32[]{:S(2)}, u32[]{:S(2)}) collective-permute-start(bf16[4,256,384]{2,1,0:T(8,128)(2,1)S(1)} %constant_dynamic-update-slice_fusion.refs_0_), channel_id=1, source_target_pairs={{0,16},{1,17},{2,18},{3,19},{4,20},{5,21},{6,22},{7,23},{8,24},{9,... | collective-permute-start | bytes 2359304 | tf_op jit(solution)/shard_map/ppermute | solution.py:30
  47.9 23.4 %collective-permute-start.21 = (bf16[2,528,384]{2,1,0:T(8,128)(2,1)S(1)}, bf16[2,528,384]{2,1,0:T(8,128)(2,1)S(1)}, u32[]{:S(2)}, u32[]{:S(2)}) collective-permute-start(bf16[2,528,384]{2,1,0:T(8,128)(2,1)S(1)} %collective-permute-done.9.refs_20_), channel_id=1, source_target_pairs={{0,2},{1,3},{2,4},{3,5},{4,6},{5,7},{6,0},{7,1},{8,14},{9,15},{10,... | collective-permute-start | bytes 2433032 | tf_op jit(solution)/shard_map/ppermute | solution.py:30
  52.9 47.4 %copy-start.5 = (bf16[2,528,384]{2,1,0:T(8,128)(2,1)}, bf16[2,528,384]{2,1,0:T(8,128)(2,1)S(1)}, u32[]{:S(2)}) copy-start(bf16[2,528,384]{2,1,0:T(8,128)(2,1)S(1)} %collective-permute-done.18.refs_17_) | copy-start | bytes 2433028
  52.9 18.5 %collective-permute-start.19 = (bf16[2,528,384]{2,1,0:T(8,128)(2,1)S(1)}, bf16[2,528,384]{2,1,0:T(8,128)(2,1)S(1)}, u32[]{:S(2)}, u32[]{:S(2)}) collective-permute-start(bf16[2,528,384]{2,1,0:T(8,128)(2,1)S(1)} %collective-permute-done.18.refs_17_), channel_id=1, source_target_pairs={{0,2},{1,3},{2,4},{3,5},{4,6},{5,7},{6,0},{7,1},{8,14},{9,15},{10,... | collective-permute-start | bytes 2433032 | tf_op jit(solution)/shard_map/ppermute | solution.py:30
  55.1 38.0 %copy-start.10 = (bf16[4,256,384]{2,1,0:T(8,128)(2,1)}, bf16[4,256,384]{2,1,0:T(8,128)(2,1)S(1)}, u32[]{:S(2)}) copy-start(bf16[4,256,384]{2,1,0:T(8,128)(2,1)S(1)} %collective-permute-done.3.refs_4_) | copy-start | bytes 2359300
  55.1 18.9 %collective-permute-start.5 = (bf16[4,256,384]{2,1,0:T(8,128)(2,1)S(1)}, bf16[4,256,384]{2,1,0:T(8,128)(2,1)}, u32[]{:S(2)}, u32[]{:S(2)}) collective-permute-start(bf16[4,256,384]{2,1,0:T(8,128)(2,1)S(1)} %collective-permute-done.3.refs_4_), channel_id=1, source_target_pairs={{0,32},{1,33},{2,34},{3,35},{4,36},{5,37},{6,38},{7,39},{8,104},{9... | collective-permute-start | bytes 2359304 | tf_op jit(solution)/shard_map/ppermute | solution.py:30
  58.5 36.1 %copy-start.11 = (bf16[4,256,384]{2,1,0:T(8,128)(2,1)}, bf16[4,256,384]{2,1,0:T(8,128)(2,1)S(1)}, u32[]{:S(2)}) copy-start(bf16[4,256,384]{2,1,0:T(8,128)(2,1)S(1)} %collective-permute-done.2.refs_3_) | copy-start | bytes 2359300
  58.5 15.6 %collective-permute-start.4 = (bf16[4,256,384]{2,1,0:T(8,128)(2,1)S(1)}, bf16[4,256,384]{2,1,0:T(8,128)(2,1)S(1)}, u32[]{:S(2)}, u32[]{:S(2)}) collective-permute-start(bf16[4,256,384]{2,1,0:T(8,128)(2,1)S(1)} %collective-permute-done.3.refs_4_), channel_id=1, source_target_pairs={{0,8},{1,9},{2,10},{3,11},{4,12},{5,13},{6,14},{7,15},{8,0},{9,1},... | collective-permute-start | bytes 2359304 | tf_op jit(solution)/shard_map/ppermute | solution.py:30
  66.4 29.4 %copy-start.12 = (bf16[4,256,384]{2,1,0:T(8,128)(2,1)}, bf16[4,256,384]{2,1,0:T(8,128)(2,1)S(1)}, u32[]{:S(2)}) copy-start(bf16[4,256,384]{2,1,0:T(8,128)(2,1)S(1)} %collective-permute-done.10.refs_8_) | copy-start | bytes 2359300
  66.4 13.9 %collective-permute-start.12 = (bf16[4,256,384]{2,1,0:T(8,128)(2,1)S(1)}, bf16[4,256,384]{2,1,0:T(8,128)(2,1)}, u32[]{:S(2)}, u32[]{:S(2)}) collective-permute-start(bf16[4,256,384]{2,1,0:T(8,128)(2,1)S(1)} %collective-permute-done.10.refs_8_), channel_id=1, source_target_pairs={{0,32},{1,33},{2,34},{3,35},{4,36},{5,37},{6,38},{7,39},{8,104},{9... | collective-permute-start | bytes 2359304 | tf_op jit(solution)/shard_map/ppermute | solution.py:30
  71.4 0.9 copy-start.6
  71.4 12.4 %collective-permute-start.22 = (bf16[2,528,384]{2,1,0:T(8,128)(2,1)S(1)}, bf16[2,528,384]{2,1,0:T(8,128)(2,1)}, u32[]{:S(2)}, u32[]{:S(2)}) collective-permute-start(bf16[2,528,384]{2,1,0:T(8,128)(2,1)S(1)} %collective-permute-done.21.refs_21_), channel_id=1, source_target_pairs={{0,2},{1,3},{2,4},{3,5},{4,6},{5,7},{6,0},{7,1},{8,14},{9,15},{10,... | collective-permute-start | bytes 2433032 | tf_op jit(solution)/shard_map/ppermute | solution.py:30
  72.3 11.5 %copy-start.7 = (bf16[2,528,384]{2,1,0:T(8,128)(2,1)}, bf16[2,528,384]{2,1,0:T(8,128)(2,1)S(1)}, u32[]{:S(2)}) copy-start(bf16[2,528,384]{2,1,0:T(8,128)(2,1)S(1)} %collective-permute-done.19.refs_18_) | copy-start | bytes 2433028
  72.3 19.3 %collective-permute-start.20 = (bf16[2,528,384]{2,1,0:T(8,128)(2,1)S(1)}, bf16[2,528,384]{2,1,0:T(8,128)(2,1)S(1)}, u32[]{:S(2)}, u32[]{:S(2)}) collective-permute-start(bf16[2,528,384]{2,1,0:T(8,128)(2,1)S(1)} %collective-permute-done.19.refs_18_), channel_id=1, source_target_pairs={{0,2},{1,3},{2,4},{3,5},{4,6},{5,7},{6,0},{7,1},{8,14},{9,15},{10,... | collective-permute-start | bytes 2433032 | tf_op jit(solution)/shard_map/ppermute | solution.py:30
  74.0 10.2 %collective-permute-start.11 = (bf16[4,256,384]{2,1,0:T(8,128)(2,1)S(1)}, bf16[4,256,384]{2,1,0:T(8,128)(2,1)S(1)}, u32[]{:S(2)}, u32[]{:S(2)}) collective-permute-start(bf16[4,256,384]{2,1,0:T(8,128)(2,1)S(1)} %collective-permute-done.10.refs_8_), channel_id=1, source_target_pairs={{0,8},{1,9},{2,10},{3,11},{4,12},{5,13},{6,14},{7,15},{8,0},{9,1},... | collective-permute-start | bytes 2359304 | tf_op jit(solution)/shard_map/ppermute | solution.py:30
  74.0 21.8 %copy-start.13 = (bf16[4,256,384]{2,1,0:T(8,128)(2,1)}, bf16[4,256,384]{2,1,0:T(8,128)(2,1)S(1)}, u32[]{:S(2)}) copy-start(bf16[4,256,384]{2,1,0:T(8,128)(2,1)S(1)} %collective-permute-done.4.refs_5_) | copy-start | bytes 2359300
  74.0 20.5 %collective-permute-start.16 = (bf16[4,256,384]{2,1,0:T(8,128)(2,1)}, bf16[4,256,384]{2,1,0:T(8,128)(2,1)}, u32[]{:S(2)}, u32[]{:S(2)}) collective-permute-start(bf16[4,256,384]{2,1,0:T(8,128)(2,1)} %collective-permute-done.5.refs_6_), channel_id=1, source_target_pairs={{0,16},{1,17},{2,18},{3,19},{4,20},{5,21},{6,22},{7,23},{8,24},{9,... | collective-permute-start | bytes 2359304 | tf_op jit(solution)/shard_map/ppermute | solution.py:30
  80.3 15.5 %collective-permute-start.14 = (bf16[4,256,384]{2,1,0:T(8,128)(2,1)}, bf16[4,256,384]{2,1,0:T(8,128)(2,1)}, u32[]{:S(2)}, u32[]{:S(2)}) collective-permute-start(bf16[4,256,384]{2,1,0:T(8,128)(2,1)} %collective-permute-done.12.refs_10_), channel_id=1, source_target_pairs={{0,32},{1,33},{2,34},{3,35},{4,36},{5,37},{6,38},{7,39},{8,104},{9... | collective-permute-start | bytes 2359304 | tf_op jit(solution)/shard_map/ppermute | solution.py:30
  83.8 16.4 %collective-permute-start.23 = (bf16[2,528,384]{2,1,0:T(8,128)(2,1)}, bf16[2,528,384]{2,1,0:T(8,128)(2,1)}, u32[]{:S(2)}, u32[]{:S(2)}) collective-permute-start(bf16[2,528,384]{2,1,0:T(8,128)(2,1)} %collective-permute-done.22.refs_22_), channel_id=1, source_target_pairs={{0,2},{1,3},{2,4},{3,5},{4,6},{5,7},{6,0},{7,1},{8,14},{9,15},{10,... | collective-permute-start | bytes 2433032 | tf_op jit(solution)/shard_map/ppermute | solution.py:30
  84.2 11.7 %copy-start.14 = (bf16[4,256,384]{2,1,0:T(8,128)(2,1)}, bf16[4,256,384]{2,1,0:T(8,128)(2,1)S(1)}, u32[]{:S(2)}) copy-start(bf16[4,256,384]{2,1,0:T(8,128)(2,1)S(1)} %collective-permute-done.11.refs_9_) | copy-start | bytes 2359300
  84.2 13.4 %collective-permute-start.6 = (bf16[4,256,384]{2,1,0:T(8,128)(2,1)}, bf16[4,256,384]{2,1,0:T(8,128)(2,1)}, u32[]{:S(2)}, u32[]{:S(2)}) collective-permute-start(bf16[4,256,384]{2,1,0:T(8,128)(2,1)} %collective-permute-done.5.refs_6_), channel_id=1, source_target_pairs={{0,8},{1,9},{2,10},{3,11},{4,12},{5,13},{6,14},{7,15},{8,0},{9,1},... | collective-permute-start | bytes 2359304 | tf_op jit(solution)/shard_map/ppermute | solution.py:30
  91.6 0.9 copy-start.8
  92.5 5.1 %collective-permute-start.13 = (bf16[4,256,384]{2,1,0:T(8,128)(2,1)}, bf16[4,256,384]{2,1,0:T(8,128)(2,1)}, u32[]{:S(2)}, u32[]{:S(2)}) collective-permute-start(bf16[4,256,384]{2,1,0:T(8,128)(2,1)} %collective-permute-done.12.refs_10_), channel_id=1, source_target_pairs={{0,8},{1,9},{2,10},{3,11},{4,12},{5,13},{6,14},{7,15},{8,0},{9,1},... | collective-permute-start | bytes 2359304 | tf_op jit(solution)/shard_map/ppermute | solution.py:30
  94.6 5.7 %collective-permute-start.17 = (bf16[4,256,384]{2,1,0:T(8,128)(2,1)}, bf16[4,256,384]{2,1,0:T(8,128)(2,1)}, u32[]{:S(2)}, u32[]{:S(2)}) collective-permute-start(bf16[4,256,384]{2,1,0:T(8,128)(2,1)} %collective-permute-done.16.refs_14_), channel_id=1, source_target_pairs={{0,8},{1,9},{2,10},{3,11},{4,12},{5,13},{6,14},{7,15},{8,0},{9,1},... | collective-permute-start | bytes 2359304 | tf_op jit(solution)/shard_map/ppermute | solution.py:30
  95.9 4.4 %collective-permute-start.15 = (bf16[4,256,384]{2,1,0:T(8,128)(2,1)}, bf16[4,256,384]{2,1,0:T(8,128)(2,1)}, u32[]{:S(2)}, u32[]{:S(2)}) collective-permute-start(bf16[4,256,384]{2,1,0:T(8,128)(2,1)} %collective-permute-done.14.refs_12_), channel_id=1, source_target_pairs={{0,8},{1,9},{2,10},{3,11},{4,12},{5,13},{6,14},{7,15},{8,0},{9,1},... | collective-permute-start | bytes 2359304 | tf_op jit(solution)/shard_map/ppermute | solution.py:30

commit v7 on v6

--- a/solution.py
+++ b/solution.py
@@ -43,15 +43,23 @@
     def fetch(step):
         slab, slot = lax.rem(step + 15, 16), lax.rem(step, 4)
         row_from, col_from = source[slab], source[16 + slab]
-        for n in range(16):
-
-            @pl.when(row_from == n)
+        for start in range(0, 16, 4):
+
+            @pl.when((row_from >= start) & (row_from < start + 4))
             def _():
-                row_copy(n, slot).start()
-
-            @pl.when(col_from == n)
+                for n in range(start, start + 4):
+
+                    @pl.when(row_from == n)
+                    def _():
+                        row_copy(n, slot).start()
+
+            @pl.when((col_from >= start) & (col_from < start + 4))
             def _():
-                col_copy(n, slot).start()
+                for n in range(start, start + 4):
+
+                    @pl.when(col_from == n)
+                    def _():
+                        col_copy(n, slot).start()
 
     def products(step, base, obase):
         slot = lax.rem(step, 4)

time: 124 us -> 124 us (level)
  no operation moved by 1% of the time
where the time goes in v7:
time: 124 us
  starting transfers between devices  60.7 us (49%)
  waiting for transfers between devices  34.6 us (28%)
  Pallas kernels  23.3 us (19%)
  local copies, waits for them, and re-layouts  4.27 us (3%)
    ppermute x24, starting transfers between devices, send(): return lax.ppermute(block, AXES, routes(target))  60.7 us
    ppermute x24, waiting for transfers between devices, send(): return lax.ppermute(block, AXES, routes(target))  34.6 us
    pallas_call x1, Pallas kernels, polarizability(): pl.pallas_call(kernel, in_specs=[scalars, scalars] + [anywhere] * 24, out...  23.3 us
  transfers between devices with their start and end apart: 24, of which 8 were waited for; matrix products, arithmetic and copies ran while one was open for 0% of the time, Pallas kernels for 0%

profile of v7, /device:TPU:1, one launch (start us, length us, event | category | flops | bytes accessed | tf_op | source)
XLA Modules:
  0.0 123.8 jit_solution(4300639848800652934)
XLA Ops:
  0.0 1.0 constant_dynamic-slice_fusion.1
  1.0 1.1 constant_dynamic-slice_fusion
  2.1 0.0 copy-start.3
  2.1 0.1 pad_maximum_fusion.3
  2.3 0.0 copy-start.1
  2.3 0.1 pad_maximum_fusion.1
  2.4 1.5 %collective-permute-start.8 = (bf16[528,384]{1,0:T(8,128)(2,1)S(1)}, bf16[528,384]{1,0:T(8,128)(2,1)S(1)}, u32[]{:S(2)}, u32[]{:S(2)}) collective-permute-start(bf16[528,384]{1,0:T(8,128)(2,1)S(1)} %get-tuple-element.13), channel_id=1, source_target_pairs={{0,8},{1,24},{2,42},{3,58},{4,76},{5,92},{6,110},{7,126},{8,0},{9,... | collective-permute-start | bytes 1216520 | tf_op jit(solution)/shard_map/ppermute | solution.py:30
  3.9 0.7 collective-permute-start.7
  4.6 0.6 collective-permute-done.8
  5.2 0.1 pad_maximum_fusion.refs_16_
  5.3 19.9 %collective-permute-start.9 = (bf16[2,528,384]{2,1,0:T(8,128)(2,1)S(1)}, bf16[2,528,384]{2,1,0:T(8,128)(2,1)S(1)}, u32[]{:S(2)}, u32[]{:S(2)}) collective-permute-start(bf16[2,528,384]{2,1,0:T(8,128)(2,1)S(1)} %pad_maximum_fusion.refs_16_), channel_id=1, source_target_pairs={{0,1},{1,0},{2,3},{3,2},{4,5},{5,4},{6,7},{7,6},{8,9},{9,8},{10,11... | collective-permute-start | bytes 2433032 | tf_op jit(solution)/shard_map/ppermute | solution.py:30
  25.3 8.5 %collective-permute-start.1 = (bf16[4,256,384]{2,1,0:T(8,128)(2,1)S(1)}, bf16[4,256,384]{2,1,0:T(8,128)(2,1)S(1)}, u32[]{:S(2)}, u32[]{:S(2)}) collective-permute-start(bf16[4,256,384]{2,1,0:T(8,128)(2,1)S(1)} %constant_dynamic-update-slice_fusion.refs_0_), channel_id=1, source_target_pairs={{0,32},{1,33},{2,34},{3,35},{4,36},{5,37},{6,38},{7,39},{8,104},{9... | collective-permute-start | bytes 2359304 | tf_op jit(solution)/shard_map/ppermute | solution.py:30
  33.8 0.1 collective-permute-start.18
  33.9 8.9 %collective-permute-done.1.refs_2_ = bf16[4,256,384]{2,1,0:T(8,128)(2,1)S(1)} collective-permute-done((bf16[4,256,384]{2,1,0:T(8,128)(2,1)S(1)}, bf16[4,256,384]{2,1,0:T(8,128)(2,1)S(1)}, u32[]{:S(2)}, u32[]{:S(2)}) %collective-permute-start.1) | collective-permute-done | bytes 786464 | tf_op jit(solution)/shard_map/ppermute | solution.py:30
  42.7 3.4 %collective-permute-start.3 = (bf16[4,256,384]{2,1,0:T(8,128)(2,1)S(1)}, bf16[4,256,384]{2,1,0:T(8,128)(2,1)S(1)}, u32[]{:S(2)}, u32[]{:S(2)}) collective-permute-start(bf16[4,256,384]{2,1,0:T(8,128)(2,1)S(1)} %collective-permute-done.1.refs_2_), channel_id=1, source_target_pairs={{0,32},{1,33},{2,34},{3,35},{4,36},{5,37},{6,38},{7,39},{8,104},{9... | collective-permute-start | bytes 2359304 | tf_op jit(solution)/shard_map/ppermute | solution.py:30
  46.1 0.0 collective-permute-start.2
  46.1 0.0 collective-permute-done.9.refs_20_
  46.1 1.8 %collective-permute-start.10 = (bf16[4,256,384]{2,1,0:T(8,128)(2,1)S(1)}, bf16[4,256,384]{2,1,0:T(8,128)(2,1)S(1)}, u32[]{:S(2)}, u32[]{:S(2)}) collective-permute-start(bf16[4,256,384]{2,1,0:T(8,128)(2,1)S(1)} %constant_dynamic-update-slice_fusion.refs_0_), channel_id=1, source_target_pairs={{0,16},{1,17},{2,18},{3,19},{4,20},{5,21},{6,22},{7,23},{8,24},{9,... | collective-permute-start | bytes 2359304 | tf_op jit(solution)/shard_map/ppermute | solution.py:30
  47.9 5.0 %collective-permute-start.21 = (bf16[2,528,384]{2,1,0:T(8,128)(2,1)S(1)}, bf16[2,528,384]{2,1,0:T(8,128)(2,1)S(1)}, u32[]{:S(2)}, u32[]{:S(2)}) collective-permute-start(bf16[2,528,384]{2,1,0:T(8,128)(2,1)S(1)} %collective-permute-done.9.refs_20_), channel_id=1, source_target_pairs={{0,2},{1,3},{2,4},{3,5},{4,6},{5,7},{6,0},{7,1},{8,14},{9,15},{10,... | collective-permute-start | bytes 2433032 | tf_op jit(solution)/shard_map/ppermute | solution.py:30
  52.9 0.0 collective-permute-done.18.refs_17_
  52.9 1.1 collective-permute-start.19
  54.1 1.0 collective-permute-done.3.refs_4_
  55.1 3.4 %collective-permute-start.5 = (bf16[4,256,384]{2,1,0:T(8,128)(2,1)S(1)}, bf16[4,256,384]{2,1,0:T(8,128)(2,1)}, u32[]{:S(2)}, u32[]{:S(2)}) collective-permute-start(bf16[4,256,384]{2,1,0:T(8,128)(2,1)S(1)} %collective-permute-done.3.refs_4_), channel_id=1, source_target_pairs={{0,32},{1,33},{2,34},{3,35},{4,36},{5,37},{6,38},{7,39},{8,104},{9... | collective-permute-start | bytes 2359304 | tf_op jit(solution)/shard_map/ppermute | solution.py:30
  58.5 0.0 collective-permute-done.2.refs_3_
  58.5 0.0 collective-permute-start.4
  58.5 7.9 %collective-permute-done.10.refs_8_ = bf16[4,256,384]{2,1,0:T(8,128)(2,1)S(1)} collective-permute-done((bf16[4,256,384]{2,1,0:T(8,128)(2,1)S(1)}, bf16[4,256,384]{2,1,0:T(8,128)(2,1)S(1)}, u32[]{:S(2)}, u32[]{:S(2)}) %collective-permute-start.10) | collective-permute-done | bytes 786464 | tf_op jit(solution)/shard_map/ppermute | solution.py:30
  66.4 5.0 %collective-permute-start.12 = (bf16[4,256,384]{2,1,0:T(8,128)(2,1)S(1)}, bf16[4,256,384]{2,1,0:T(8,128)(2,1)}, u32[]{:S(2)}, u32[]{:S(2)}) collective-permute-start(bf16[4,256,384]{2,1,0:T(8,128)(2,1)S(1)} %collective-permute-done.10.refs_8_), channel_id=1, source_target_pairs={{0,32},{1,33},{2,34},{3,35},{4,36},{5,37},{6,38},{7,39},{8,104},{9... | collective-permute-start | bytes 2359304 | tf_op jit(solution)/shard_map/ppermute | solution.py:30
  71.4 0.1 collective-permute-start.22
  71.5 0.8 copy-done.6
  72.3 1.7 %collective-permute-start.20 = (bf16[2,528,384]{2,1,0:T(8,128)(2,1)S(1)}, bf16[2,528,384]{2,1,0:T(8,128)(2,1)S(1)}, u32[]{:S(2)}, u32[]{:S(2)}) collective-permute-start(bf16[2,528,384]{2,1,0:T(8,128)(2,1)S(1)} %collective-permute-done.19.refs_18_), channel_id=1, source_target_pairs={{0,2},{1,3},{2,4},{3,5},{4,6},{5,7},{6,0},{7,1},{8,14},{9,15},{10,... | collective-permute-start | bytes 2433032 | tf_op jit(solution)/shard_map/ppermute | solution.py:30
  74.0 0.1 collective-permute-start.11
  74.0 1.7 %collective-permute-start.16 = (bf16[4,256,384]{2,1,0:T(8,128)(2,1)}, bf16[4,256,384]{2,1,0:T(8,128)(2,1)}, u32[]{:S(2)}, u32[]{:S(2)}) collective-permute-start(bf16[4,256,384]{2,1,0:T(8,128)(2,1)} %collective-permute-done.5.refs_6_), channel_id=1, source_target_pairs={{0,16},{1,17},{2,18},{3,19},{4,20},{5,21},{6,22},{7,23},{8,24},{9,... | collective-permute-start | bytes 2359304 | tf_op jit(solution)/shard_map/ppermute | solution.py:30
  75.7 4.6 %collective-permute-done.12.refs_10_ = bf16[4,256,384]{2,1,0:T(8,128)(2,1)} collective-permute-done((bf16[4,256,384]{2,1,0:T(8,128)(2,1)S(1)}, bf16[4,256,384]{2,1,0:T(8,128)(2,1)}, u32[]{:S(2)}, u32[]{:S(2)}) %collective-permute-start.12) | collective-permute-done | bytes 786464 | tf_op jit(solution)/shard_map/ppermute | solution.py:30
  80.3 3.5 %collective-permute-start.14 = (bf16[4,256,384]{2,1,0:T(8,128)(2,1)}, bf16[4,256,384]{2,1,0:T(8,128)(2,1)}, u32[]{:S(2)}, u32[]{:S(2)}) collective-permute-start(bf16[4,256,384]{2,1,0:T(8,128)(2,1)} %collective-permute-done.12.refs_10_), channel_id=1, source_target_pairs={{0,32},{1,33},{2,34},{3,35},{4,36},{5,37},{6,38},{7,39},{8,104},{9... | collective-permute-start | bytes 2359304 | tf_op jit(solution)/shard_map/ppermute | solution.py:30
  83.8 0.3 collective-permute-start.23
  84.2 7.4 %collective-permute-done.20.refs_19_ = bf16[2,528,384]{2,1,0:T(8,128)(2,1)S(1)} collective-permute-done((bf16[2,528,384]{2,1,0:T(8,128)(2,1)S(1)}, bf16[2,528,384]{2,1,0:T(8,128)(2,1)S(1)}, u32[]{:S(2)}, u32[]{:S(2)}) %collective-permute-start.20) | collective-permute-done | bytes 811040 | tf_op jit(solution)/shard_map/ppermute | solution.py:30
  91.6 0.9 copy-done.8
  92.5 0.5 collective-permute-start.13
  93.0 1.6 %collective-permute-done.16.refs_14_ = bf16[4,256,384]{2,1,0:T(8,128)(2,1)} collective-permute-done((bf16[4,256,384]{2,1,0:T(8,128)(2,1)}, bf16[4,256,384]{2,1,0:T(8,128)(2,1)}, u32[]{:S(2)}, u32[]{:S(2)}) %collective-permute-start.16) | collective-permute-done | bytes 786464 | tf_op jit(solution)/shard_map/ppermute | solution.py:30
  94.6 1.3 %collective-permute-start.17 = (bf16[4,256,384]{2,1,0:T(8,128)(2,1)}, bf16[4,256,384]{2,1,0:T(8,128)(2,1)}, u32[]{:S(2)}, u32[]{:S(2)}) collective-permute-start(bf16[4,256,384]{2,1,0:T(8,128)(2,1)} %collective-permute-done.16.refs_14_), channel_id=1, source_target_pairs={{0,8},{1,9},{2,10},{3,11},{4,12},{5,13},{6,14},{7,15},{8,0},{9,1},... | collective-permute-start | bytes 2359304 | tf_op jit(solution)/shard_map/ppermute | solution.py:30
  95.9 1.2 collective-permute-start.15
  97.1 0.1 stack.127
  97.2 0.1 stack.144
  97.3 0.1 select_reduce_fusion
  97.4 0.1 pad_add_fusion.source
  97.5 0.1 slice_reduce_fusion
  97.6 2.7 %collective-permute-done.23.refs_23_ = bf16[2,528,384]{2,1,0:T(8,128)(2,1)} collective-permute-done((bf16[2,528,384]{2,1,0:T(8,128)(2,1)}, bf16[2,528,384]{2,1,0:T(8,128)(2,1)}, u32[]{:S(2)}, u32[]{:S(2)}) %collective-permute-start.23) | collective-permute-done | bytes 811040 | tf_op jit(solution)/shard_map/ppermute | solution.py:30
  100.3 23.3 %shard_map.55 = f32[3,4,256,128]{3,2,1,0:T(8,128)} custom-call(s32[3]{0:T(128)S(1)} %and_select_fusion.shift, s32[32]{0:T(128)S(1)} %pad_add_fusion.source, bf16[4,256,384]{2,1,0:T(8,128)(2,1)} %copy-done.2, bf16[4,256,384]{2,1,0:T(8,128)(2,1)} %collective-permute-done.refs_1_, bf16[4,256,384]{2,1,0:T(8,128)(2,1)} %copy-done.9, ...), custom_call_target="tpu_custom_call" | custom-call | tf_op jit(solution)/shard_map/pallas_call | solution.py:119
  (51 shorter events, 0.2 us)
Async XLA Ops:
  0.0 2.1 %copy-start.15 = (bf16[4,256]{1,0:T(4,128)(2,1)S(1)}, bf16[4,256]{1,0:T(4,128)(2,1)}, u32[]{:S(2)}) copy-start(bf16[4,256]{1,0:T(4,128)(2,1)} %param.8) | copy-start | bytes 6148
  0.0 2.1 %copy-start.17 = (bf16[4,128]{1,0:T(4,128)(2,1)S(1)}, bf16[4,128]{1,0:T(4,128)(2,1)}, u32[]{:S(2)}) copy-start(bf16[4,128]{1,0:T(4,128)(2,1)} %param.7) | copy-start | bytes 3076
  2.1 2.4 %copy-start.3 = (bf16[4,256,128]{2,1,0:T(8,128)(2,1)S(1)}, bf16[4,256,128]{2,1,0:T(8,128)(2,1)}, u32[]{:S(2)}) copy-start(bf16[4,256,128]{2,1,0:T(8,128)(2,1)} %param.5) | copy-start | bytes 786436
  2.3 23.0 %copy-start.1 = (bf16[4,256,256]{2,1,0:T(8,128)(2,1)S(1)}, bf16[4,256,256]{2,1,0:T(8,128)(2,1)}, u32[]{:S(2)}) copy-start(bf16[4,256,256]{2,1,0:T(8,128)(2,1)} %param.6) | copy-start | bytes 1572868
  2.4 2.9 %collective-permute-start.8 = (bf16[528,384]{1,0:T(8,128)(2,1)S(1)}, bf16[528,384]{1,0:T(8,128)(2,1)S(1)}, u32[]{:S(2)}, u32[]{:S(2)}) collective-permute-start(bf16[528,384]{1,0:T(8,128)(2,1)S(1)} %get-tuple-element.13), channel_id=1, source_target_pairs={{0,8},{1,24},{2,42},{3,58},{4,76},{5,92},{6,110},{7,126},{8,0},{9,... | collective-permute-start | bytes 1216520 | tf_op jit(solution)/shard_map/ppermute | solution.py:30
  3.9 1.4 %collective-permute-start.7 = (bf16[528,384]{1,0:T(8,128)(2,1)S(1)}, bf16[528,384]{1,0:T(8,128)(2,1)S(1)}, u32[]{:S(2)}, u32[]{:S(2)}) collective-permute-start(bf16[528,384]{1,0:T(8,128)(2,1)S(1)} %get-tuple-element.14), channel_id=1, source_target_pairs={{0,0},{1,16},{2,34},{3,50},{4,68},{5,84},{6,102},{7,118},{8,8},{9,... | collective-permute-start | bytes 1216520 | tf_op jit(solution)/shard_map/ppermute | solution.py:30
  5.2 92.2 %copy-start.16 = (s32[3,64]{1,0:T(4,128)S(1)}, s32[3,64]{1,0:T(4,128)}, u32[]{:S(2)}) copy-start(s32[3,64]{1,0:T(4,128)} %param.9) | copy-start | bytes 2308
  5.3 95.0 %copy-start = (bf16[2,528,384]{2,1,0:T(8,128)(2,1)}, bf16[2,528,384]{2,1,0:T(8,128)(2,1)S(1)}, u32[]{:S(2)}) copy-start(bf16[2,528,384]{2,1,0:T(8,128)(2,1)S(1)} %pad_maximum_fusion.refs_16_) | copy-start | bytes 2433028
  5.3 40.8 %collective-permute-start.9 = (bf16[2,528,384]{2,1,0:T(8,128)(2,1)S(1)}, bf16[2,528,384]{2,1,0:T(8,128)(2,1)S(1)}, u32[]{:S(2)}, u32[]{:S(2)}) collective-permute-start(bf16[2,528,384]{2,1,0:T(8,128)(2,1)S(1)} %pad_maximum_fusion.refs_16_), channel_id=1, source_target_pairs={{0,1},{1,0},{2,3},{3,2},{4,5},{5,4},{6,7},{7,6},{8,9},{9,8},{10,11... | collective-permute-start | bytes 2433032 | tf_op jit(solution)/shard_map/ppermute | solution.py:30
  25.3 75.0 %copy-start.2 = (bf16[4,256,384]{2,1,0:T(8,128)(2,1)}, bf16[4,256,384]{2,1,0:T(8,128)(2,1)S(1)}, u32[]{:S(2)}) copy-start(bf16[4,256,384]{2,1,0:T(8,128)(2,1)S(1)} %constant_dynamic-update-slice_fusion.refs_0_) | copy-start | bytes 2359300
  25.3 17.4 %collective-permute-start.1 = (bf16[4,256,384]{2,1,0:T(8,128)(2,1)S(1)}, bf16[4,256,384]{2,1,0:T(8,128)(2,1)S(1)}, u32[]{:S(2)}, u32[]{:S(2)}) collective-permute-start(bf16[4,256,384]{2,1,0:T(8,128)(2,1)S(1)} %constant_dynamic-update-slice_fusion.refs_0_), channel_id=1, source_target_pairs={{0,32},{1,33},{2,34},{3,35},{4,36},{5,37},{6,38},{7,39},{8,104},{9... | collective-permute-start | bytes 2359304 | tf_op jit(solution)/shard_map/ppermute | solution.py:30
  33.8 19.2 %collective-permute-start.18 = (bf16[2,528,384]{2,1,0:T(8,128)(2,1)S(1)}, bf16[2,528,384]{2,1,0:T(8,128)(2,1)S(1)}, u32[]{:S(2)}, u32[]{:S(2)}) collective-permute-start(bf16[2,528,384]{2,1,0:T(8,128)(2,1)S(1)} %pad_maximum_fusion.refs_16_), channel_id=1, source_target_pairs={{0,2},{1,3},{2,4},{3,5},{4,6},{5,7},{6,0},{7,1},{8,14},{9,15},{10,... | collective-permute-start | bytes 2433032 | tf_op jit(solution)/shard_map/ppermute | solution.py:30
  33.8 14.1 %collective-permute-start = (bf16[4,256,384]{2,1,0:T(8,128)(2,1)S(1)}, bf16[4,256,384]{2,1,0:T(8,128)(2,1)}, u32[]{:S(2)}, u32[]{:S(2)}) collective-permute-start(bf16[4,256,384]{2,1,0:T(8,128)(2,1)S(1)} %constant_dynamic-update-slice_fusion.refs_0_), channel_id=1, source_target_pairs={{0,8},{1,9},{2,10},{3,11},{4,12},{5,13},{6,14},{7,15},{8,0},{9,1},... | collective-permute-start | bytes 2359304 | tf_op jit(solution)/shard_map/ppermute | solution.py:30
  42.7 28.8 %copy-start.9 = (bf16[4,256,384]{2,1,0:T(8,128)(2,1)}, bf16[4,256,384]{2,1,0:T(8,128)(2,1)S(1)}, u32[]{:S(2)}) copy-start(bf16[4,256,384]{2,1,0:T(8,128)(2,1)S(1)} %collective-permute-done.1.refs_2_) | copy-start | bytes 2359300
  42.7 12.3 %collective-permute-start.3 = (bf16[4,256,384]{2,1,0:T(8,128)(2,1)S(1)}, bf16[4,256,384]{2,1,0:T(8,128)(2,1)S(1)}, u32[]{:S(2)}, u32[]{:S(2)}) collective-permute-start(bf16[4,256,384]{2,1,0:T(8,128)(2,1)S(1)} %collective-permute-done.1.refs_2_), channel_id=1, source_target_pairs={{0,32},{1,33},{2,34},{3,35},{4,36},{5,37},{6,38},{7,39},{8,104},{9... | collective-permute-start | bytes 2359304 | tf_op jit(solution)/shard_map/ppermute | solution.py:30
  46.1 12.4 %collective-permute-start.2 = (bf16[4,256,384]{2,1,0:T(8,128)(2,1)S(1)}, bf16[4,256,384]{2,1,0:T(8,128)(2,1)S(1)}, u32[]{:S(2)}, u32[]{:S(2)}) collective-permute-start(bf16[4,256,384]{2,1,0:T(8,128)(2,1)S(1)} %collective-permute-done.1.refs_2_), channel_id=1, source_target_pairs={{0,8},{1,9},{2,10},{3,11},{4,12},{5,13},{6,14},{7,15},{8,0},{9,1},... | collective-permute-start | bytes 2359304 | tf_op jit(solution)/shard_map/ppermute | solution.py:30
  46.1 54.2 %copy-start.4 = (bf16[2,528,384]{2,1,0:T(8,128)(2,1)}, bf16[2,528,384]{2,1,0:T(8,128)(2,1)S(1)}, u32[]{:S(2)}) copy-start(bf16[2,528,384]{2,1,0:T(8,128)(2,1)S(1)} %collective-permute-done.9.refs_20_) | copy-start | bytes 2433028
  46.1 20.3 %collective-permute-start.10 = (bf16[4,256,384]{2,1,0:T(8,128)(2,1)S(1)}, bf16[4,256,384]{2,1,0:T(8,128)(2,1)S(1)}, u32[]{:S(2)}, u32[]{:S(2)}) collective-permute-start(bf16[4,256,384]{2,1,0:T(8,128)(2,1)S(1)} %constant_dynamic-update-slice_fusion.refs_0_), channel_id=1, source_target_pairs={{0,16},{1,17},{2,18},{3,19},{4,20},{5,21},{6,22},{7,23},{8,24},{9,... | collective-permute-start | bytes 2359304 | tf_op jit(solution)/shard_map/ppermute | solution.py:30
  47.9 23.4 %collective-permute-start.21 = (bf16[2,528,384]{2,1,0:T(8,128)(2,1)S(1)}, bf16[2,528,384]{2,1,0:T(8,128)(2,1)S(1)}, u32[]{:S(2)}, u32[]{:S(2)}) collective-permute-start(bf16[2,528,384]{2,1,0:T(8,128)(2,1)S(1)} %collective-permute-done.9.refs_20_), channel_id=1, source_target_pairs={{0,2},{1,3},{2,4},{3,5},{4,6},{5,7},{6,0},{7,1},{8,14},{9,15},{10,... | collective-permute-start | bytes 2433032 | tf_op jit(solution)/shard_map/ppermute | solution.py:30
  52.9 47.4 %copy-start.5 = (bf16[2,528,384]{2,1,0:T(8,128)(2,1)}, bf16[2,528,384]{2,1,0:T(8,128)(2,1)S(1)}, u32[]{:S(2)}) copy-start(bf16[2,528,384]{2,1,0:T(8,128)(2,1)S(1)} %collective-permute-done.18.refs_17_) | copy-start | bytes 2433028
  52.9 18.5 %collective-permute-start.19 = (bf16[2,528,384]{2,1,0:T(8,128)(2,1)S(1)}, bf16[2,528,384]{2,1,0:T(8,128)(2,1)S(1)}, u32[]{:S(2)}, u32[]{:S(2)}) collective-permute-start(bf16[2,528,384]{2,1,0:T(8,128)(2,1)S(1)} %collective-permute-done.18.refs_17_), channel_id=1, source_target_pairs={{0,2},{1,3},{2,4},{3,5},{4,6},{5,7},{6,0},{7,1},{8,14},{9,15},{10,... | collective-permute-start | bytes 2433032 | tf_op jit(solution)/shard_map/ppermute | solution.py:30
  55.1 38.0 %copy-start.10 = (bf16[4,256,384]{2,1,0:T(8,128)(2,1)}, bf16[4,256,384]{2,1,0:T(8,128)(2,1)S(1)}, u32[]{:S(2)}) copy-start(bf16[4,256,384]{2,1,0:T(8,128)(2,1)S(1)} %collective-permute-done.3.refs_4_) | copy-start | bytes 2359300
  55.1 18.9 %collective-permute-start.5 = (bf16[4,256,384]{2,1,0:T(8,128)(2,1)S(1)}, bf16[4,256,384]{2,1,0:T(8,128)(2,1)}, u32[]{:S(2)}, u32[]{:S(2)}) collective-permute-start(bf16[4,256,384]{2,1,0:T(8,128)(2,1)S(1)} %collective-permute-done.3.refs_4_), channel_id=1, source_target_pairs={{0,32},{1,33},{2,34},{3,35},{4,36},{5,37},{6,38},{7,39},{8,104},{9... | collective-permute-start | bytes 2359304 | tf_op jit(solution)/shard_map/ppermute | solution.py:30
  58.5 36.1 %copy-start.11 = (bf16[4,256,384]{2,1,0:T(8,128)(2,1)}, bf16[4,256,384]{2,1,0:T(8,128)(2,1)S(1)}, u32[]{:S(2)}) copy-start(bf16[4,256,384]{2,1,0:T(8,128)(2,1)S(1)} %collective-permute-done.2.refs_3_) | copy-start | bytes 2359300
  58.5 15.6 %collective-permute-start.4 = (bf16[4,256,384]{2,1,0:T(8,128)(2,1)S(1)}, bf16[4,256,384]{2,1,0:T(8,128)(2,1)S(1)}, u32[]{:S(2)}, u32[]{:S(2)}) collective-permute-start(bf16[4,256,384]{2,1,0:T(8,128)(2,1)S(1)} %collective-permute-done.3.refs_4_), channel_id=1, source_target_pairs={{0,8},{1,9},{2,10},{3,11},{4,12},{5,13},{6,14},{7,15},{8,0},{9,1},... | collective-permute-start | bytes 2359304 | tf_op jit(solution)/shard_map/ppermute | solution.py:30
  66.4 29.4 %copy-start.12 = (bf16[4,256,384]{2,1,0:T(8,128)(2,1)}, bf16[4,256,384]{2,1,0:T(8,128)(2,1)S(1)}, u32[]{:S(2)}) copy-start(bf16[4,256,384]{2,1,0:T(8,128)(2,1)S(1)} %collective-permute-done.10.refs_8_) | copy-start | bytes 2359300
  66.4 13.9 %collective-permute-start.12 = (bf16[4,256,384]{2,1,0:T(8,128)(2,1)S(1)}, bf16[4,256,384]{2,1,0:T(8,128)(2,1)}, u32[]{:S(2)}, u32[]{:S(2)}) collective-permute-start(bf16[4,256,384]{2,1,0:T(8,128)(2,1)S(1)} %collective-permute-done.10.refs_8_), channel_id=1, source_target_pairs={{0,32},{1,33},{2,34},{3,35},{4,36},{5,37},{6,38},{7,39},{8,104},{9... | collective-permute-start | bytes 2359304 | tf_op jit(solution)/shard_map/ppermute | solution.py:30
  71.4 0.9 copy-start.6
  71.4 12.4 %collective-permute-start.22 = (bf16[2,528,384]{2,1,0:T(8,128)(2,1)S(1)}, bf16[2,528,384]{2,1,0:T(8,128)(2,1)}, u32[]{:S(2)}, u32[]{:S(2)}) collective-permute-start(bf16[2,528,384]{2,1,0:T(8,128)(2,1)S(1)} %collective-permute-done.21.refs_21_), channel_id=1, source_target_pairs={{0,2},{1,3},{2,4},{3,5},{4,6},{5,7},{6,0},{7,1},{8,14},{9,15},{10,... | collective-permute-start | bytes 2433032 | tf_op jit(solution)/shard_map/ppermute | solution.py:30
  72.3 11.5 %copy-start.7 = (bf16[2,528,384]{2,1,0:T(8,128)(2,1)}, bf16[2,528,384]{2,1,0:T(8,128)(2,1)S(1)}, u32[]{:S(2)}) copy-start(bf16[2,528,384]{2,1,0:T(8,128)(2,1)S(1)} %collective-permute-done.19.refs_18_) | copy-start | bytes 2433028
  72.3 19.3 %collective-permute-start.20 = (bf16[2,528,384]{2,1,0:T(8,128)(2,1)S(1)}, bf16[2,528,384]{2,1,0:T(8,128)(2,1)S(1)}, u32[]{:S(2)}, u32[]{:S(2)}) collective-permute-start(bf16[2,528,384]{2,1,0:T(8,128)(2,1)S(1)} %collective-permute-done.19.refs_18_), channel_id=1, source_target_pairs={{0,2},{1,3},{2,4},{3,5},{4,6},{5,7},{6,0},{7,1},{8,14},{9,15},{10,... | collective-permute-start | bytes 2433032 | tf_op jit(solution)/shard_map/ppermute | solution.py:30
  74.0 10.2 %collective-permute-start.11 = (bf16[4,256,384]{2,1,0:T(8,128)(2,1)S(1)}, bf16[4,256,384]{2,1,0:T(8,128)(2,1)S(1)}, u32[]{:S(2)}, u32[]{:S(2)}) collective-permute-start(bf16[4,256,384]{2,1,0:T(8,128)(2,1)S(1)} %collective-permute-done.10.refs_8_), channel_id=1, source_target_pairs={{0,8},{1,9},{2,10},{3,11},{4,12},{5,13},{6,14},{7,15},{8,0},{9,1},... | collective-permute-start | bytes 2359304 | tf_op jit(solution)/shard_map/ppermute | solution.py:30
  74.0 21.8 %copy-start.13 = (bf16[4,256,384]{2,1,0:T(8,128)(2,1)}, bf16[4,256,384]{2,1,0:T(8,128)(2,1)S(1)}, u32[]{:S(2)}) copy-start(bf16[4,256,384]{2,1,0:T(8,128)(2,1)S(1)} %collective-permute-done.4.refs_5_) | copy-start | bytes 2359300
  74.0 20.5 %collective-permute-start.16 = (bf16[4,256,384]{2,1,0:T(8,128)(2,1)}, bf16[4,256,384]{2,1,0:T(8,128)(2,1)}, u32[]{:S(2)}, u32[]{:S(2)}) collective-permute-start(bf16[4,256,384]{2,1,0:T(8,128)(2,1)} %collective-permute-done.5.refs_6_), channel_id=1, source_target_pairs={{0,16},{1,17},{2,18},{3,19},{4,20},{5,21},{6,22},{7,23},{8,24},{9,... | collective-permute-start | bytes 2359304 | tf_op jit(solution)/shard_map/ppermute | solution.py:30
  80.3 15.5 %collective-permute-start.14 = (bf16[4,256,384]{2,1,0:T(8,128)(2,1)}, bf16[4,256,384]{2,1,0:T(8,128)(2,1)}, u32[]{:S(2)}, u32[]{:S(2)}) collective-permute-start(bf16[4,256,384]{2,1,0:T(8,128)(2,1)} %collective-permute-done.12.refs_10_), channel_id=1, source_target_pairs={{0,32},{1,33},{2,34},{3,35},{4,36},{5,37},{6,38},{7,39},{8,104},{9... | collective-permute-start | bytes 2359304 | tf_op jit(solution)/shard_map/ppermute | solution.py:30
  83.8 16.4 %collective-permute-start.23 = (bf16[2,528,384]{2,1,0:T(8,128)(2,1)}, bf16[2,528,384]{2,1,0:T(8,128)(2,1)}, u32[]{:S(2)}, u32[]{:S(2)}) collective-permute-start(bf16[2,528,384]{2,1,0:T(8,128)(2,1)} %collective-permute-done.22.refs_22_), channel_id=1, source_target_pairs={{0,2},{1,3},{2,4},{3,5},{4,6},{5,7},{6,0},{7,1},{8,14},{9,15},{10,... | collective-permute-start | bytes 2433032 | tf_op jit(solution)/shard_map/ppermute | solution.py:30
  84.2 11.7 %copy-start.14 = (bf16[4,256,384]{2,1,0:T(8,128)(2,1)}, bf16[4,256,384]{2,1,0:T(8,128)(2,1)S(1)}, u32[]{:S(2)}) copy-start(bf16[4,256,384]{2,1,0:T(8,128)(2,1)S(1)} %collective-permute-done.11.refs_9_) | copy-start | bytes 2359300
  84.2 13.4 %collective-permute-start.6 = (bf16[4,256,384]{2,1,0:T(8,128)(2,1)}, bf16[4,256,384]{2,1,0:T(8,128)(2,1)}, u32[]{:S(2)}, u32[]{:S(2)}) collective-permute-start(bf16[4,256,384]{2,1,0:T(8,128)(2,1)} %collective-permute-done.5.refs_6_), channel_id=1, source_target_pairs={{0,8},{1,9},{2,10},{3,11},{4,12},{5,13},{6,14},{7,15},{8,0},{9,1},... | collective-permute-start | bytes 2359304 | tf_op jit(solution)/shard_map/ppermute | solution.py:30
  91.6 0.9 copy-start.8
  92.5 5.1 %collective-permute-start.13 = (bf16[4,256,384]{2,1,0:T(8,128)(2,1)}, bf16[4,256,384]{2,1,0:T(8,128)(2,1)}, u32[]{:S(2)}, u32[]{:S(2)}) collective-permute-start(bf16[4,256,384]{2,1,0:T(8,128)(2,1)} %collective-permute-done.12.refs_10_), channel_id=1, source_target_pairs={{0,8},{1,9},{2,10},{3,11},{4,12},{5,13},{6,14},{7,15},{8,0},{9,1},... | collective-permute-start | bytes 2359304 | tf_op jit(solution)/shard_map/ppermute | solution.py:30
  94.6 5.7 %collective-permute-start.17 = (bf16[4,256,384]{2,1,0:T(8,128)(2,1)}, bf16[4,256,384]{2,1,0:T(8,128)(2,1)}, u32[]{:S(2)}, u32[]{:S(2)}) collective-permute-start(bf16[4,256,384]{2,1,0:T(8,128)(2,1)} %collective-permute-done.16.refs_14_), channel_id=1, source_target_pairs={{0,8},{1,9},{2,10},{3,11},{4,12},{5,13},{6,14},{7,15},{8,0},{9,1},... | collective-permute-start | bytes 2359304 | tf_op jit(solution)/shard_map/ppermute | solution.py:30
  95.9 4.4 %collective-permute-start.15 = (bf16[4,256,384]{2,1,0:T(8,128)(2,1)}, bf16[4,256,384]{2,1,0:T(8,128)(2,1)}, u32[]{:S(2)}, u32[]{:S(2)}) collective-permute-start(bf16[4,256,384]{2,1,0:T(8,128)(2,1)} %collective-permute-done.14.refs_12_), channel_id=1, source_target_pairs={{0,8},{1,9},{2,10},{3,11},{4,12},{5,13},{6,14},{7,15},{8,0},{9,1},... | collective-permute-start | bytes 2359304 | tf_op jit(solution)/shard_map/ppermute | solution.py:30
